TPU v7x, 256 devices: a whole 4x4x8 slice. The times are simulated.
256 devices in a mesh: dp: 32 (over z, x_lo, core), space: 8 (over y, x_hi).
Axes of the slice: x: 4 (x_hi: 2, x_lo: 2; x = x_hi * 2 + x_lo), y: 4, z: 8, core: 2. Of those that a mesh axis runs over, the one named last changes fastest.
Arguments:
- latents: bfloat16 [32, 8, 24, 8, 256], P('dp', None, 'space'), may hold values from -48 to 48
- cotangent: bfloat16 [32, 8, 24, 8, 256], P('dp', None, 'space'), may hold values from -17 to 17
- conv_weights: bfloat16 [2, 6912, 256], replicated, may hold values from -0.078125 to 0.078125
- gains: float32 [2, 256], replicated, may hold values from 0.25 to 1.75
- shifts: float32 [2, 256], replicated, may hold values from -3 to 3
- moment: float32 [2, 6912, 256], P(None, 'dp'), may hold values from -30 to 30
- second: float32 [2, 6912, 256], P(None, 'dp'), may hold values from 10 to 100
Outputs:
- decoded: bfloat16 [32, 8, 24, 8, 256], P('dp', None, 'space')
- grad_input: bfloat16 [32, 8, 24, 8, 256], P('dp', None, 'space')
- new_moment: float32 [2, 6912, 256], P(None, 'dp')
- new_second: float32 [2, 6912, 256], P(None, 'dp')
- direction: float32 [2, 6912, 256], P(None, 'dp')
- vector_grads: float32 [4, 256], replicated
All inputs are finite; a program needn't handle non-finite values.
Results may differ from a plain program's by a relative error of at most 0.0045.
Values may be sent and summed in bfloat16 or wider, within the bound.
No kernel may reach another device: no remote copies, remote signals or barrier semaphores. Data moves between devices by JAX's collectives and lax.ppermute only.
A program may use at most 128 MiB of HBM per device.

v0:
```python
import math

import jax
import jax.numpy as jnp
from jax import lax
from jax.experimental import pallas as pl
from jax.experimental.pallas import tpu as pltpu
from jax.sharding import PartitionSpec as P

GROUPS = 32
STEP = 4


bias_first = 1.0 - math.exp(100.0 * math.log(0.9))
bias_second = 1.0 - math.exp(100.0 * math.log(0.999))


def rolled(value, amount, axis):
    return pltpu.roll(value, amount % value.shape[axis], axis)


def all_cols(value):
    total = jnp.sum(value, 0)
    for step in (4, 2, 1):
        total = total + rolled(total, step, 0)
    return total


def group_all(sums):
    size = sums.shape[1] // GROUPS
    lane = lax.broadcasted_iota(jnp.int32, sums.shape, 1)
    step = 1
    while step < size:
        partner = jnp.where((lane & step) == 0, rolled(sums, -step, 1), rolled(sums, step, 1))
        sums = sums + partner
        step *= 2
    return sums


def norm_parts(values):
    count = values.shape[0] * values.shape[1] * (values.shape[2] // GROUPS)
    mean = group_all(all_cols(values)) / count
    var = group_all(all_cols(values * values)) / count - mean * mean
    return mean, lax.rsqrt(var + 1e-05)


def col_shifted(value, step):
    if step == 0:
        return value
    col = lax.broadcasted_iota(jnp.int32, value.shape, 1)
    edge = value.shape[1] - 1 if step > 0 else 0
    return jnp.where(col == edge, 0.0, rolled(value, -step, 1))


def row_shifted(value, step):
    if step == 0:
        return value
    zero = jnp.zeros_like(value[:1])
    if step > 0:
        return jnp.concatenate([value[1:], zero], 0)
    return jnp.concatenate([zero, value[:-1]], 0)


def store_nine(target, frame, value, sign):
    rows, cols, chans = value.shape
    size = rows * cols
    for w in range(3):
        moved = col_shifted(value, sign * (w - 1))
        for h in range(3):
            view = row_shifted(moved, sign * (h - 1)).reshape(size, chans)
            number = 3 * h + w
            target[pl.ds(pl.multiple_of(frame * size, 16), size), number * chans : (number + 1) * chans] = view.astype(jnp.bfloat16)


def load_frame(raw, frame):
    blocks, _, flat, chans = raw.shape
    parts = [raw[b, frame].astype(jnp.float32).reshape(flat // 8, 8, chans) for b in range(blocks)]
    return jnp.concatenate(parts, 0)


def frame_of(flat, frame, size):
    part = flat[pl.ds(pl.multiple_of(frame * size, 16), size), :]
    return part.astype(jnp.float32).reshape(size // 8, 8, part.shape[-1])


def put_frame(flat, frame, value):
    size = value.shape[0] * value.shape[1]
    flat[pl.ds(pl.multiple_of(frame * size, 16), size), :] = value.reshape(size, -1).astype(flat.dtype)


def ahead_kernel(raw, weight, gains, shifts, a_one, h_one, a_two, nine):
    frames, chans = raw.shape[1], raw.shape[3]
    size = raw.shape[0] * raw.shape[2]
    depth = 9 * chans

    @pl.loop(0, frames)
    def _(t):
        value = load_frame(raw, t)
        mean, factor = norm_parts(value)
        u = (value - mean) * factor * gains[0:1, :] + shifts[0:1, :]
        act = (u * jax.nn.sigmoid(u)).astype(jnp.bfloat16).astype(jnp.float32)
        put_frame(a_one, t, act)
        store_nine(nine, t + 2, act, 1)

    nine[0:size, :] = nine[2 * size : 3 * size, :]
    nine[size : 2 * size, :] = nine[2 * size : 3 * size, :]

    @pl.loop(0, frames // STEP)
    def _(b):
        total = None
        for t in range(3):
            left = nine[pl.ds(pl.multiple_of((b * STEP + t) * size, 16), STEP * size), :]
            part = jnp.dot(left, weight[t * depth : (t + 1) * depth, :], preferred_element_type=jnp.float32)
            total = part if total is None else total + part
        h_one[pl.ds(pl.multiple_of(b * STEP * size, 16), STEP * size), :] = total.astype(jnp.bfloat16)

    @pl.loop(0, frames)
    def _(t):
        value = frame_of(h_one, t, size)
        mean, factor = norm_parts(value)
        u = (value - mean) * factor * gains[1:2, :] + shifts[1:2, :]
        put_frame(a_two, t, u * jax.nn.sigmoid(u))


def back_kernel(raw, weight, h_one, gains, shifts, d_h1, vectors, nine, d_act):
    frames, chans = raw.shape[1], raw.shape[3]
    size = raw.shape[0] * raw.shape[2]
    depth = 9 * chans

    @pl.loop(0, frames)
    def _(t):
        store_nine(nine, t, load_frame(raw, t), -1)

    nine[frames * size :, :] = jnp.zeros((2 * size, depth), jnp.bfloat16)

    @pl.loop(0, frames // STEP)
    def _(b):
        total = None
        for t in range(3):
            left = nine[pl.ds(pl.multiple_of((b * STEP + 2 - t) * size, 16), STEP * size), :]
            part = jnp.dot(left, weight[t * depth : (t + 1) * depth, :], preferred_element_type=jnp.float32)
            total = part if total is None else total + part
        d_act[pl.ds(pl.multiple_of(b * STEP * size, 16), STEP * size), :] = total

    pair = jnp.dot(nine[0:size, :], weight[depth : 2 * depth, :], preferred_element_type=jnp.float32)
    both = jnp.dot(nine[0 : 2 * size, :], weight[0:depth, :], preferred_element_type=jnp.float32)
    d_act[0:size, :] = d_act[0:size, :] + (pair + (both[:size] + both[size:]))

    vectors[...] = jnp.zeros_like(vectors)
    count = size * (chans // GROUPS)

    @pl.loop(0, frames)
    def _(t):
        value = frame_of(h_one, t, size)
        mean, factor = norm_parts(value)
        normed = (value - mean) * factor
        u = normed * gains[1:2, :] + shifts[1:2, :]
        sig = jax.nn.sigmoid(u)
        d_out = frame_of(d_act, t, size) * (sig * (1.0 + u * (1.0 - sig)))
        d_shift = all_cols(d_out)
        d_gain = all_cols(d_out * normed)
        vectors[0] += d_gain
        vectors[1] += d_shift
        one = group_all(d_shift * gains[1:2, :]) / count
        two = group_all(d_gain * gains[1:2, :]) / count
        put_frame(d_h1, t, factor * (d_out * gains[1:2, :] - one - normed * two))


def grad_kernel(place, values, grads, extra, out, long, block, total):
    frames_size, chans = values.shape
    owners, tall, _ = out.shape
    size = long.shape[0] - frames_size
    size, outs = size // 2, total.shape[0] // 27
    frames = frames_size // size
    long[0:size, :] = values[0:size, :]
    long[size : 2 * size, :] = values[0:size, :]
    long[2 * size :, :] = values[...]
    lanes = block.shape[1]
    chan = lax.broadcasted_iota(jnp.int32, (chans, lanes), 0)
    lane = lax.broadcasted_iota(jnp.int32, (chans, lanes), 1)
    pick = (chan == place[0] * outs + lane % outs).astype(jnp.bfloat16)

    @pl.loop(0, frames)
    def _(t):
        rows = grads[pl.ds(pl.multiple_of(t * size, 16), size), :]
        spread_out = jnp.dot(rows, pick, preferred_element_type=jnp.float32).reshape(size // 8, 8, lanes)
        for piece in range(lanes // 128):
            value = spread_out[:, :, piece * 128 : (piece + 1) * 128]
            lane = lax.broadcasted_iota(jnp.int32, value.shape, 2)
            kept = jnp.zeros_like(value)
            for place_in in range(128 // outs):
                number = piece * (128 // outs) + place_in
                if number < 9:
                    h, w = divmod(number, 3)
                    moved = row_shifted(col_shifted(value, 1 - w), 1 - h)
                    kept = jnp.where(lane // outs == place_in, moved, kept)
            block[pl.ds(pl.multiple_of(t * size, 16), size), piece * 128 : (piece + 1) * 128] = kept.reshape(size, 128).astype(jnp.bfloat16)

    side = block[...].T
    for t in range(3):
        part = jnp.dot(side, long[t * size : (t + frames) * size, :], preferred_element_type=jnp.float32)
        total[t * 9 * outs : (t + 1) * 9 * outs, :] = part[: 9 * outs]

    owned = 27 * chans // owners
    for d in range(owners):
        tap, start = divmod(d * owned, chans)
        one = total[tap * outs : (tap + 1) * outs, :]
        if start + owned > chans:
            one = jnp.concatenate([one, total[(tap + 1) * outs : (tap + 2) * outs, :]], 1)
        out[d, 0:outs, :] = rolled(one, -start, 1)[:, :chans].astype(jnp.bfloat16)
        if tall > outs:
            out[d, outs:, :] = extra[...]


def adam_kernel(every, moment, second, new_moment, new_second, direction, vector):
    parts, tall, chans = every.shape
    owned = moment.shape[1]
    width = chans // parts
    for layer in range(2):
        start = width * (1 - layer)
        grad = every[:, start : start + width, :].reshape(chans, chans).T[:owned, :]
        new_m = 0.9 * moment[layer] + 0.1 * grad
        new_v = 0.999 * second[layer] + 0.001 * grad * grad
        new_moment[layer] = new_m
        new_second[layer] = new_v
        direction[layer] = new_m / bias_first / (jnp.sqrt(new_v / bias_second) + 1e-08)
    sums = every[0, 2 * width :, :]
    for p in range(1, parts):
        sums = sums + every[p, 2 * width :, :]
    vector[...] = sums[0:4] + sums[4:8]


def called(kernel, outs, scratch, args, scalars=0, flops=0, limit=56):
    whole = pl.BlockSpec(memory_space=pltpu.VMEM)
    small = pl.BlockSpec(memory_space=pltpu.SMEM)
    moved = sum(math.prod(a.shape) * a.dtype.itemsize for a in (*args, *outs))
    return pl.pallas_call(
        kernel,
        out_shape=outs,
        in_specs=[small] * scalars + [whole] * (len(args) - scalars),
        out_specs=[whole] * len(outs),
        scratch_shapes=scratch,
        compiler_params=pltpu.CompilerParams(vmem_limit_bytes=limit * 2**20),
        cost_estimate=pl.CostEstimate(flops=flops, bytes_accessed=moved, transcendentals=0),
    )(*args)


def ahead(raw, weight, gains, shifts):
    blocks, frames, flat, chans = raw.shape
    places = blocks * frames * flat
    shape = jax.ShapeDtypeStruct((places, chans), jnp.bfloat16)
    scratch = [pltpu.VMEM((places + 2 * blocks * flat, 9 * chans), jnp.bfloat16)]
    return called(ahead_kernel, [shape] * 3, scratch, (raw, weight, gains, shifts), 0, 2 * places * weight.size)


def back(raw, weight, h_one, gains, shifts):
    blocks, frames, flat, chans = raw.shape
    places = blocks * frames * flat
    outs = [jax.ShapeDtypeStruct((places, chans), jnp.bfloat16), jax.ShapeDtypeStruct((2, 8, chans), jnp.float32)]
    scratch = [
        pltpu.VMEM((places + 2 * blocks * flat, 9 * chans), jnp.bfloat16),
        pltpu.VMEM((places, chans), jnp.float32),
    ]
    return called(back_kernel, outs, scratch, (raw, weight, h_one, gains, shifts), 0, 2 * places * weight.size)


def kernel_grad(place, values, grads, extra, width, size, clips):
    places, chans = values.shape
    outs = [jax.ShapeDtypeStruct((clips, width + extra.shape[0], chans), jnp.bfloat16)]
    if extra.shape[0] == 0:
        body = lambda p, v, g, *rest: grad_kernel(p, v, g, None, *rest)
        args = (place, values, grads)
    else:
        body, args = grad_kernel, (place, values, grads, extra)
    scratch = [
        pltpu.VMEM((places + 2 * size, chans), jnp.bfloat16),
        pltpu.VMEM((places, -(-9 * width // 128) * 128), jnp.bfloat16),
        pltpu.VMEM((27 * width, chans), jnp.float32),
    ]
    return called(body, outs, scratch, args, 1, 2 * places * 27 * width * chans)[0]


def spread(value, axis):
    return lax.all_to_all(jnp.broadcast_to(value[None], (lax.axis_size(axis),) + value.shape), axis, 0, 0)


def silu_slope(values):
    sig = jax.nn.sigmoid(values)
    return sig * (1.0 + values * (1.0 - sig))


def group_sum(sums):
    frames, chans = sums.shape
    size = chans // GROUPS
    return jnp.repeat(jnp.sum(sums.reshape(frames, GROUPS, size), -1), size, axis=-1)


def frame_stats(values):
    count = values.shape[1] * values.shape[2] * (values.shape[3] // GROUPS)
    mean = group_sum(jnp.sum(values, (1, 2))) / count
    var = group_sum(jnp.sum(values * values, (1, 2))) / count - mean * mean
    return mean[:, None, None], lax.rsqrt(var + 1e-05)[:, None, None]


def norm_back(normed, factor, gain, d_out):
    count = normed.shape[1] * normed.shape[2] * (normed.shape[3] // GROUPS)
    d_shift = jnp.sum(d_out, (1, 2))
    d_gain = jnp.sum(d_out * normed, (1, 2))
    one = group_sum(d_shift * gain)[:, None, None] / count
    two = group_sum(d_gain * gain)[:, None, None] / count
    d_in = factor * (d_out * gain - one - normed * two)
    return d_in, jnp.sum(d_gain, 0), jnp.sum(d_shift, 0)


def conv(values, weight, row_pad):
    chans = values.shape[-1]
    return lax.conv_general_dilated(
        values[None],
        weight.reshape(3, 3, 3, chans, -1),
        (1, 1, 1),
        ((0, 0), (row_pad, row_pad), (1, 1)),
        dimension_numbers=("NDHWC", "DHWIO", "NDHWC"),
        preferred_element_type=jnp.float32,
    )[0]


def conv_back(grads, weight):
    chans = grads.shape[-1]
    return lax.conv_general_dilated(
        grads[None],
        weight.reshape(3, 3, 3, -1, chans)[::-1, ::-1, ::-1],
        (1, 1, 1),
        ((0, 0), (1, 1), (1, 1)),
        dimension_numbers=("NDHWC", "DHWOI", "NDHWC"),
        preferred_element_type=jnp.float32,
    )[0]


def per_device(latents, cotangent, conv_weights, gains, shifts, moment, second):
    frames, rows, cols, chans = latents.shape[1:]
    clips, parts = lax.axis_size("dp"), lax.axis_size("space")
    me = lax.axis_index("space")
    place = me.astype(jnp.int32).reshape(1)
    width, size = chans // parts, parts * rows * cols
    f32, bf16 = jnp.float32, jnp.bfloat16
    raw_lat = spread(latents[0].reshape(frames, rows * cols, chans), "space")
    raw_cot = spread(cotangent[0].reshape(frames, rows * cols, chans), "space")
    turned = conv_weights[1].reshape(27, chans, chans).transpose(0, 2, 1).reshape(27 * chans, chans)

    a_one, h_one, a_two = ahead(raw_lat, conv_weights[0], gains, shifts)
    cot = raw_cot.transpose(1, 0, 2, 3).reshape(frames * size, chans)
    none = jnp.zeros((0, chans), bf16)
    later = kernel_grad(place, a_two, cot, none, width, size, clips)
    later = lax.all_to_all(later, "dp", 0, 0)

    d_h1, sums_two = back(raw_cot, turned, h_one, gains, shifts)

    def frame(raw):
        value = lax.dynamic_slice_in_dim(raw, me, 1, 1)
        return value.reshape(1, parts * rows, cols, chans).astype(f32)

    xown = frame(raw_lat)
    mean_one, factor_one = frame_stats(xown)
    normed_one = (xown - mean_one) * factor_one
    u_one = normed_one * gains[0] + shifts[0]
    near = jnp.pad(d_h1.reshape(frames, size // cols, cols, chans), ((0, 2), (0, 0), (0, 0), (0, 0)))
    near = lax.dynamic_slice_in_dim(near, me, 3, 0).astype(f32)
    first = (me == 0).astype(f32)
    near = jnp.stack(
        [near[0], near[1] + first * near[0], near[2] + first * (near[0] + near[1])]
    ).astype(bf16)
    d_a1 = conv_back(near, conv_weights[0])
    d_x, gain_one, shift_one = norm_back(normed_one, factor_one, gains[0], d_a1 * silu_slope(u_one))
    grad_input = (frame(raw_cot) + d_x).astype(bf16)
    grad_input = grad_input[0].reshape(parts, rows, cols, chans)
    grad_input = lax.all_to_all(grad_input, "space", 0, 0)

    share = 1.0 / parts
    vectors = jnp.concatenate([gain_one[None], shift_one[None], sums_two[:, 0] * share])
    high = vectors.astype(bf16)
    low = (vectors - high.astype(f32)).astype(bf16)
    extra = jnp.concatenate([high, low, jnp.zeros((8, chans), bf16)], 0)
    earlier = kernel_grad(place, a_one, d_h1, extra, width, size, clips)
    earlier = lax.all_to_all(earlier, "dp", 0, 0)

    tall = a_two.reshape(frames, size // cols, cols, chans)
    tall = jnp.pad(jnp.concatenate([tall[:1], tall[:1], tall], 0), ((0, 0), (1, 1), (0, 0), (0, 0)))
    tall = lax.dynamic_slice_in_dim(tall, me * rows, rows + 2, 1)
    decoded = (latents[0].astype(f32) + conv(tall, conv_weights[1], 0)).astype(bf16)

    total = jnp.sum(jnp.concatenate([later, earlier], 1).astype(f32), 0) / clips
    every = spread(total, "space")
    shape = jax.ShapeDtypeStruct(moment.shape, f32)
    outs = [shape, shape, shape, jax.ShapeDtypeStruct((4, chans), f32)]
    new_moment, new_second, direction, vector = called(adam_kernel, outs, [], (every, moment, second))
    return (decoded[None], grad_input[None], new_moment, new_second, direction, vector)


def solution(mesh):
    placed = (
        P("dp", None, "space", None, None),
        P("dp", None, "space", None, None),
        P(),
        P(),
        P(),
        P(None, "dp", None),
        P(None, "dp", None),
    )
    return jax.shard_map(
        per_device,
        mesh=mesh,
        in_specs=placed,
        out_specs=(
            P("dp", None, "space", None, None),
            P("dp", None, "space", None, None),
            P(None, "dp", None),
            P(None, "dp", None),
            P(None, "dp", None),
            P(),
        ),
        check_vma=False,
    )
```

profile of v0, /device:TPU:2, one launch (start us, length us, event | category | flops | bytes accessed | tf_op | source)
XLA Modules:
  0.0 171.9 jit_solution(11694206254544157288)
XLA Ops:
  0.6 1.8 %broadcast_in_dim.48 = bf16[8,8,24,256]{3,2,1,0:T(8,128)(2,1)} broadcast(bf16[8,24,256]{2,1,0:T(8,128)(2,1)} %bitcast.57), dimensions={1,2,3} | broadcast | bytes 884736 | tf_op jit(solution)/shard_map/broadcast_in_dim | solution.py:284
  2.4 6.0 %all-to-all-start = ((bf16[8,8,24,256]{3,2,1,0:T(8,128)(2,1)}), bf16[8,8,24,256]{3,2,1,0:T(8,128)(2,1)}, u32[]{:S(2)}, u32[]{:S(2)}) async-start(bf16[8,8,24,256]{3,2,1,0:T(8,128)(2,1)} %broadcast_in_dim.48), calls=%async_computation | async-start | bytes 1572864 | tf_op jit(solution)/shard_map/all_to_all | solution.py:284
  8.5 5.3 %fusion.29 = (bf16[1,6912,256]{2,1,0:T(8,128)(2,1)}, bf16[6912,256]{1,0:T(8,128)(2,1)}, bf16[1,6912,256]{2,1,0:T(8,128)(2,1)S(1)}) fusion(bf16[2,6912,256]{2,1,0:T(8,128)(2,1)} %param.9), kind=kLoop, calls=%fused_computation.62 | loop fusion | bytes 17694720 | tf_op jit(solution)/shard_map/slice | solution.py:350
  14.8 3.6 %copy.41 = bf16[27,256,256]{1,2,0:T(8,128)(2,1)} copy(bf16[27,256,256]{2,1,0:T(8,128)(2,1)S(1)} %bitcast.47) | data formatting | bytes 7077888 | tf_op jit(solution)/shard_map/reshape;squeeze | solution.py:348
  18.4 0.7 pad.14.clone
  19.1 3.9 %all-to-all-done.raw = bf16[8,8,24,256]{3,2,1,0:T(8,128)(2,1)} async-done(((bf16[8,8,24,256]{3,2,1,0:T(8,128)(2,1)}), bf16[8,8,24,256]{3,2,1,0:T(8,128)(2,1)}, u32[]{:S(2)}, u32[]{:S(2)}) %all-to-all-start) | async-done | bytes 786464 | tf_op jit(solution)/shard_map/all_to_all | solution.py:284
  23.0 1.8 %broadcast_in_dim.51 = bf16[8,8,24,256]{3,2,1,0:T(8,128)(2,1)} broadcast(bf16[8,24,256]{2,1,0:T(8,128)(2,1)} %bitcast.56), dimensions={1,2,3} | broadcast | bytes 884736 | tf_op jit(solution)/shard_map/broadcast_in_dim | solution.py:284
  24.8 4.2 %all-to-all-start.1 = ((bf16[8,8,24,256]{3,2,1,0:T(8,128)(2,1)}), bf16[8,8,24,256]{3,2,1,0:T(8,128)(2,1)}, u32[]{:S(2)}, u32[]{:S(2)}) async-start(bf16[8,8,24,256]{3,2,1,0:T(8,128)(2,1)} %broadcast_in_dim.51), calls=%async_computation.1 | async-start | bytes 1572864 | tf_op jit(solution)/shard_map/all_to_all | solution.py:284
  29.0 1.5 convert_reduce_fusion.1
  30.6 0.8 reshape.306
  32.0 0.7 broadcast_multiply_fusion.4
  32.7 0.7 div.46
  33.3 0.8 reshape.307
  34.7 0.7 broadcast_multiply_fusion.3
  35.5 0.7 div.48
  36.1 14.8 %shard_map.118 = (bf16[1536,256]{1,0:T(8,128)(2,1)}, bf16[1536,256]{1,0:T(8,128)(2,1)}, bf16[1536,256]{1,0:T(8,128)(2,1)}) custom-call(bf16[8,8,24,256]{3,2,1,0:T(8,128)(2,1)} %all-to-all-done.raw, bf16[6912,256]{1,0:T(8,128)(2,1)} %get-tuple-element.55.weight, f32[2,256]{1,0:T(2,128)} %gains.3, f32[2,256]{1,0:T(2,128)} %shifts.3), custom_call_target="tpu_custom_call" | custom-call | flops 5435817984 | bytes 6688768 | tf_op jit(solution)/shard_map/pallas_call | solution.py:237
  50.9 15.7 %shard_map.119 = (bf16[1536,256]{1,0:T(8,128)(2,1)}, f32[2,8,256]{2,1,0:T(8,128)}) custom-call(bf16[8,8,24,256]{3,2,1,0:T(8,128)(2,1)} %all-to-all-done.1.raw, bf16[6912,256]{1,0:T(8,128)(2,1)} %bitcast.49, bf16[1536,256]{1,0:T(8,128)(2,1)} %get-tuple-element.16.h_one, f32[2,256]{1,0:T(2,128)} %gains.3, f32[2,256]{1,0:T(2,128)} %shifts.3), custom_call_target="tpu_custom_call" | custom-call | flops 5435817984 | bytes 5918720 | tf_op jit(solution)/shard_map/pallas_call | solution.py:237
  66.6 1.0 fusion.11
  67.7 0.8 copy.44
  68.5 0.8 copy.43
  69.4 0.8 copy.42
  70.2 2.1 %copy.46 = bf16[8,8,24,256]{3,2,1,0:T(8,128)(2,1)} copy(bf16[8,8,24,256]{3,2,0,1:T(8,128)(2,1)} %bitcast.25) | data formatting | bytes 1572864 | tf_op jit(solution)/shard_map/transpose | solution.py:351
  72.3 5.3 %shard_map.120 = bf16[32,32,256]{2,1,0:T(8,128)(2,1)} custom-call(s32[1]{0:T(128)} %bitcast.24.p.place, bf16[1536,256]{1,0:T(8,128)(2,1)} %get-tuple-element.15.v, bf16[1536,256]{1,0:T(8,128)(2,1)} %bitcast.53), custom_call_target="tpu_custom_call" | custom-call | flops 679477248 | bytes 2097156 | tf_op jit(solution)/shard_map/pallas_call | solution.py:237
  77.6 10.1 %all-to-all-start.3 = ((bf16[32,32,256]{2,1,0:T(8,128)(2,1)}), bf16[32,32,256]{2,1,0:T(8,128)(2,1)}, u32[]{:S(2)}, u32[]{:S(2)}) async-start(bf16[32,32,256]{2,1,0:T(8,128)(2,1)} %shard_map.120), calls=%async_computation.3 | async-start | bytes 1048576 | tf_op jit(solution)/shard_map/all_to_all | solution.py:354
  87.8 0.9 dynamic-slice_convert_fusion
  88.8 7.9 %fusion.28 = (f32[256]{0:T(256)S(1)}, f32[256]{0:T(256)S(1)}, f32[1,1,24,8,256]{4,0,3,2,1:T(1,128)}) fusion(f32[256]{0:T(256)S(1)} %add_rsqrt_fusion, f32[256]{0:T(256)S(1)} %copy-done.1, f32[1,24,8,256]{3,2,1,0:T(8,128)S(1)} %bitcast.55, f32[256]{0:T(256)S(1)} %bitcast.65, f32[256]{0:T(256)} %bitcast.66, bf16[3,3,3,256,256]{4,3,2,1,0:T(8,128)(2,1)} %bitcast.50, ...), kind=kOutput, calls=%fused_computation.61 | convolution fusion | flops 607174144 | bytes 4233216 | tf_op jit(solution)/shard_map/conv_general_dilated | solution.py:329
  96.8 0.7 maximum_maximum_fusion.extra
  97.5 5.4 %shard_map.121 = bf16[32,48,256]{2,1,0:T(8,128)(2,1)} custom-call(s32[1]{0:T(128)} %bitcast.24.p.place, bf16[1536,256]{1,0:T(8,128)(2,1)} %get-tuple-element.18.values, bf16[1536,256]{1,0:T(8,128)(2,1)} %get-tuple-element.17.grads, bf16[16,256]{1,0:T(8,128)(2,1)} %maximum_maximum_fusion.extra), custom_call_target="tpu_custom_call" | custom-call | flops 679477248 | bytes 2367492 | tf_op jit(solution)/shard_map/pallas_call | solution.py:237
  102.9 2.6 %all-to-all-done.3 = bf16[32,32,256]{2,1,0:T(8,128)(2,1)} async-done(((bf16[32,32,256]{2,1,0:T(8,128)(2,1)}), bf16[32,32,256]{2,1,0:T(8,128)(2,1)}, u32[]{:S(2)}, u32[]{:S(2)}) %all-to-all-start.3) | async-done | bytes 524320 | tf_op jit(solution)/shard_map/all_to_all | solution.py:354
  105.5 5.7 %all-to-all-start.4 = ((bf16[32,48,256]{2,1,0:T(8,128)(2,1)}), bf16[32,48,256]{2,1,0:T(8,128)(2,1)}, u32[]{:S(2)}, u32[]{:S(2)}) async-start(bf16[32,48,256]{2,1,0:T(8,128)(2,1)} %shard_map.121), calls=%async_computation.4 | async-start | bytes 1572864 | tf_op jit(solution)/shard_map/all_to_all | solution.py:384
  111.2 1.6 copy.49
  113.4 0.8 reshape.311
  114.8 0.7 broadcast_multiply_fusion.1
  116.2 0.8 reshape.310
  117.6 0.7 broadcast_multiply_fusion.2
  119.0 0.9 slice_bitcast_fusion
  119.9 1.7 fusion.17
  121.5 1.9 %fusion.19 = bf16[8,3,8,256]{3,2,1,0:T(8,128)(2,1)} fusion(f32[8,3,8,256]{3,2,1,0:T(8,128)} %bitcast.54, f32[256]{0:T(256)} %div.54, f32[256]{0:T(256)} %div.52, f32[256]{0:T(256)} %bitcast.64, f32[256]{0:T(256)} %bitcast.67, f32[256]{0:T(256)} %div.48, f32[256]{0:T(256)} %copy-done.2, bf16[8,8,24,256]{3,2,1,0:T(8,128)(2,1)} %all-to-all-done.1.raw, ...), kind=kLoop, calls=%fused_computation.28 | loop fusion | flops 1032192 | bytes 497668 | tf_op jit(solution)/shard_map/convert_element_type | solution.py:374
  123.4 11.2 %all-to-all-done.4 = bf16[32,48,256]{2,1,0:T(8,128)(2,1)} async-done(((bf16[32,48,256]{2,1,0:T(8,128)(2,1)}), bf16[32,48,256]{2,1,0:T(8,128)(2,1)}, u32[]{:S(2)}, u32[]{:S(2)}) %all-to-all-start.4) | async-done | bytes 786464 | tf_op jit(solution)/shard_map/all_to_all | solution.py:384
  134.6 7.1 %all-to-all-start.2 = ((bf16[8,3,8,256]{3,2,1,0:T(8,128)(2,1)}), bf16[8,3,8,256]{3,2,1,0:T(8,128)(2,1)}, u32[]{:S(2)}, u32[]{:S(2)}) async-start(bf16[8,3,8,256]{3,2,1,0:T(8,128)(2,1)} %fusion.19), calls=%async_computation.2 | async-start | bytes 196608 | tf_op jit(solution)/shard_map/all_to_all | solution.py:376
  141.7 1.5 convert_reduce_fusion
  143.8 6.0 %all-to-all-done.2 = bf16[8,3,8,256]{3,2,1,0:T(8,128)(2,1)} async-done(((bf16[8,3,8,256]{3,2,1,0:T(8,128)(2,1)}), bf16[8,3,8,256]{3,2,1,0:T(8,128)(2,1)}, u32[]{:S(2)}, u32[]{:S(2)}) %all-to-all-start.2) | async-done | bytes 98336 | tf_op jit(solution)/shard_map/all_to_all | solution.py:376
  149.8 1.8 %broadcast_in_dim.58 = f32[8,80,256]{2,1,0:T(8,128)} broadcast(f32[80,256]{1,0:T(8,128)} %broadcast_multiply_fusion), dimensions={1,2} | broadcast | bytes 737280 | tf_op jit(solution)/shard_map/broadcast_in_dim | solution.py:284
  151.6 4.4 %all-to-all-start.5 = ((f32[8,80,256]{2,1,0:T(8,128)}), f32[8,80,256]{2,1,0:T(8,128)}, u32[]{:S(2)}, u32[]{:S(2)}) async-start(f32[8,80,256]{2,1,0:T(8,128)} %broadcast_in_dim.58), calls=%async_computation.5 | async-start | bytes 1310720 | tf_op jit(solution)/shard_map/all_to_all | solution.py:284
  156.1 5.5 %fusion = bf16[1,8,3,8,256]{4,0,3,2,1:T(2,128)(2,1)S(1)} fusion(bf16[3,3,3,256,256]{4,3,2,1,0:T(8,128)(2,1)S(1)} %bitcast.48, bf16[1,10,5,8,256]{4,3,2,1,0:T(8,128)(2,1)} %fusion.17, bf16[1,8,3,8,256]{4,3,2,1,0:T(8,128)(2,1)} %param.7), kind=kOutput, calls=%fused_computation.2 | convolution fusion | flops 623001600 | bytes 3940352 | tf_op jit(solution)/shard_map/conv_general_dilated | solution.py:317
  162.2 5.4 %all-to-all-done.5.every = f32[8,80,256]{2,1,0:T(8,128)} async-done(((f32[8,80,256]{2,1,0:T(8,128)}), f32[8,80,256]{2,1,0:T(8,128)}, u32[]{:S(2)}, u32[]{:S(2)}) %all-to-all-start.5) | async-done | bytes 655392 | tf_op jit(solution)/shard_map/all_to_all | solution.py:284
  167.6 2.7 %shard_map.122 = (f32[2,216,256]{2,1,0:T(8,128)}, f32[2,216,256]{2,1,0:T(8,128)}, f32[2,216,256]{2,1,0:T(8,128)}, f32[4,256]{1,0:T(4,128)}) custom-call(f32[8,80,256]{2,1,0:T(8,128)} %all-to-all-done.5.every, f32[2,216,256]{2,1,0:T(8,128)} %moment.1, f32[2,216,256]{2,1,0:T(8,128)} %second.1), custom_call_target="tpu_custom_call" | custom-call | bytes 2871296 | tf_op jit(solution)/shard_map/pallas_call | solution.py:237
  170.4 1.5 copy.63
  (42 shorter events, 7.3 us)
Async XLA Ops:
  2.4 20.5 %all-to-all-start = ((bf16[8,8,24,256]{3,2,1,0:T(8,128)(2,1)}), bf16[8,8,24,256]{3,2,1,0:T(8,128)(2,1)}, u32[]{:S(2)}, u32[]{:S(2)}) async-start(bf16[8,8,24,256]{3,2,1,0:T(8,128)(2,1)} %broadcast_in_dim.48), calls=%async_computation | async-start | bytes 1572864 | tf_op jit(solution)/shard_map/all_to_all | solution.py:284
  8.5 5.3 %copy-start.8 = (f32[2,256]{1,0:T(2,128)S(1)}, f32[2,256]{1,0:T(2,128)}, u32[]{:S(2)}) copy-start(f32[2,256]{1,0:T(2,128)} %shifts.3) | copy-start | bytes 6148
  8.5 5.8 %copy-start.5 = (f32[2,256]{1,0:T(2,128)S(1)}, f32[2,256]{1,0:T(2,128)}, u32[]{:S(2)}) copy-start(f32[2,256]{1,0:T(2,128)} %gains.3) | copy-start | bytes 6148
  24.8 26.1 %all-to-all-start.1 = ((bf16[8,8,24,256]{3,2,1,0:T(8,128)(2,1)}), bf16[8,8,24,256]{3,2,1,0:T(8,128)(2,1)}, u32[]{:S(2)}, u32[]{:S(2)}) async-start(bf16[8,8,24,256]{3,2,1,0:T(8,128)(2,1)} %broadcast_in_dim.51), calls=%async_computation.1 | async-start | bytes 1572864 | tf_op jit(solution)/shard_map/all_to_all | solution.py:284
  67.6 20.2 %copy-start.1 = (f32[256]{0:T(256)S(1)}, f32[256]{0:T(256)}, u32[]{:S(2)}) copy-start(f32[256]{0:T(256)} %div.48) | copy-start | bytes 3076
  67.6 20.2 %copy-start.4 = (f32[256]{0:T(256)S(1)}, f32[256]{0:T(256)}, u32[]{:S(2)}) copy-start(f32[256]{0:T(256)} %div.46) | copy-start | bytes 3076
  67.6 21.1 %copy-start.3 = (f32[1,256]{1,0:T(1,128)S(1)}, f32[1,256]{1,0:T(1,128)}, u32[]{:S(2)}) copy-start(f32[1,256]{1,0:T(1,128)} %slice.45) | copy-start | bytes 3076
  77.6 27.9 %all-to-all-start.3 = ((bf16[32,32,256]{2,1,0:T(8,128)(2,1)}), bf16[32,32,256]{2,1,0:T(8,128)(2,1)}, u32[]{:S(2)}, u32[]{:S(2)}) async-start(bf16[32,32,256]{2,1,0:T(8,128)(2,1)} %shard_map.120), calls=%async_computation.3 | async-start | bytes 1048576 | tf_op jit(solution)/shard_map/all_to_all | solution.py:354
  87.8 8.9 %copy-start.2 = (f32[256]{0:T(256)}, f32[256]{0:T(256)S(1)}, u32[]{:S(2)}) copy-start(f32[256]{0:T(256)S(1)} %add_rsqrt_fusion) | copy-start | bytes 3076
  88.7 8.0 %copy-start = (f32[2,8,256]{2,1,0:T(8,128)S(1)}, f32[2,8,256]{2,1,0:T(8,128)}, u32[]{:S(2)}) copy-start(f32[2,8,256]{2,1,0:T(8,128)} %get-tuple-element.19) | copy-start | bytes 49156
  88.7 8.0 %copy-start.7 = (bf16[16]{0:T(256)(128)(2,1)S(1)}, bf16[16]{0:T(256)(128)(2,1)}, u32[]{:S(2)}) copy-start(bf16[16]{0:T(256)(128)(2,1)} %pad.14.clone) | copy-start | bytes 100
  96.7 16.1 %copy-start.6 = (f32[2,256]{1,0:T(2,128)S(1)}, f32[2,256]{1,0:T(2,128)}, u32[]{:S(2)}) copy-start(f32[2,256]{1,0:T(2,128)} %gains.3) | copy-start | bytes 6148
  105.5 29.1 %all-to-all-start.4 = ((bf16[32,48,256]{2,1,0:T(8,128)(2,1)}), bf16[32,48,256]{2,1,0:T(8,128)(2,1)}, u32[]{:S(2)}, u32[]{:S(2)}) async-start(bf16[32,48,256]{2,1,0:T(8,128)(2,1)} %shard_map.121), calls=%async_computation.4 | async-start | bytes 1572864 | tf_op jit(solution)/shard_map/all_to_all | solution.py:384
  134.6 15.2 %all-to-all-start.2 = ((bf16[8,3,8,256]{3,2,1,0:T(8,128)(2,1)}), bf16[8,3,8,256]{3,2,1,0:T(8,128)(2,1)}, u32[]{:S(2)}, u32[]{:S(2)}) async-start(bf16[8,3,8,256]{3,2,1,0:T(8,128)(2,1)} %fusion.19), calls=%async_computation.2 | async-start | bytes 196608 | tf_op jit(solution)/shard_map/all_to_all | solution.py:376
  151.6 16.0 %all-to-all-start.5 = ((f32[8,80,256]{2,1,0:T(8,128)}), f32[8,80,256]{2,1,0:T(8,128)}, u32[]{:S(2)}, u32[]{:S(2)}) async-start(f32[8,80,256]{2,1,0:T(8,128)} %broadcast_in_dim.58), calls=%async_computation.5 | async-start | bytes 1310720 | tf_op jit(solution)/shard_map/all_to_all | solution.py:284
where the time goes:
time: 173 us; the launch traced here: 172 us
  Pallas kernels  44 us (25%)
  starting transfers between devices  37.6 us (22%)
  local copies, waits for them, and re-layouts  31.3 us (18%)
  waiting for transfers between devices  29.1 us (17%)
  other arithmetic  15.6 us (9%)
  matrix products  13.4 us (8%)
    pallas_call x5, Pallas kernels, called(): pl.pallas_call(kernel, out_shape=outs, in_specs=[small] * scalars + [whol...  44 us
    all_to_all x3, starting transfers between devices, spread(): lax.all_to_all(jnp.broadcast_to(value[None], (lax.axis_size(axis),) + val...  14.7 us
    all_to_all x1, waiting for transfers between devices, per_device(): earlier = lax.all_to_all(earlier, 'dp', 0, 0)  11.2 us
    all_to_all x1, starting transfers between devices, per_device(): later = lax.all_to_all(later, 'dp', 0, 0)  10.1 us
    all_to_all x3, waiting for transfers between devices, spread(): lax.all_to_all(jnp.broadcast_to(value[None], (lax.axis_size(axis),) + val...  9.31 us
    conv_general_dilated x1, matrix products, conv_back(): lax.conv_general_dilated(grads[None], weight.reshape(3, 3, 3, -1, chans)[...  7.94 us
    all_to_all x1, starting transfers between devices, per_device(): grad_input = lax.all_to_all(grad_input, 'space', 0, 0)  7.1 us
    all_to_all x1, waiting for transfers between devices, per_device(): grad_input = lax.all_to_all(grad_input, 'space', 0, 0)  6.03 us
  transfers between devices with their start and end apart: 6, of which 5 were waited for; matrix products, arithmetic and copies ran while one was open for 28% of the time, Pallas kernels for 12%

commit v1 on v0

--- a/solution.py
+++ b/solution.py
@@ -1,3 +1,4 @@
+import functools
 import math
 
 import jax
@@ -169,8 +170,7 @@
 def grad_kernel(place, values, grads, extra, out, long, block, total):
     frames_size, chans = values.shape
     owners, tall, _ = out.shape
-    size = long.shape[0] - frames_size
-    size, outs = size // 2, total.shape[0] // 27
+    size, outs = (long.shape[0] - frames_size) // 2, total.shape[0] // 27
     frames = frames_size // size
     long[0:size, :] = values[0:size, :]
     long[size : 2 * size, :] = values[0:size, :]
@@ -202,17 +202,110 @@
         total[t * 9 * outs : (t + 1) * 9 * outs, :] = part[: 9 * outs]
 
     owned = 27 * chans // owners
+    lane = lax.broadcasted_iota(jnp.int32, (outs, chans), 1)
     for d in range(owners):
         tap, start = divmod(d * owned, chans)
         one = total[tap * outs : (tap + 1) * outs, :]
         if start + owned > chans:
             one = jnp.concatenate([one, total[(tap + 1) * outs : (tap + 2) * outs, :]], 1)
-        out[d, 0:outs, :] = rolled(one, -start, 1)[:, :chans].astype(jnp.bfloat16)
-        if tall > outs:
-            out[d, outs:, :] = extra[...]
-
-
-def adam_kernel(every, moment, second, new_moment, new_second, direction, vector):
+        one = rolled(one, -start, 1)[:, :chans]
+        if extra is not None:
+            one = jnp.where(lane < owned, one, extra[...])
+        out[d] = one.astype(jnp.bfloat16)
+
+
+def halves(value):
+    high = value.astype(jnp.bfloat16).astype(jnp.float32)
+    return high, value - high
+
+
+def to_spare(value, start, width):
+    chans = value.shape[1]
+    row = lax.broadcasted_iota(jnp.int32, value.shape, 0)
+    lane = lax.broadcasted_iota(jnp.int32, value.shape, 1)
+    held = (lane >= start) & (lane < start + width)
+    tiles = []
+    for tile in range(chans // width // 8):
+        kept = jnp.zeros_like(value)
+        for r in range(8):
+            moved = rolled(value, start - width * (8 * tile + r), 1)
+            kept = jnp.where((row == r) & held, moved, kept)
+        tiles.append(kept)
+    return jnp.concatenate(tiles, 0)
+
+
+def from_spare(value, start, width):
+    rows, chans = value.shape
+    row = lax.broadcasted_iota(jnp.int32, (8, chans), 0)
+    lane = lax.broadcasted_iota(jnp.int32, (8, chans), 1)
+    kept = jnp.zeros((8, chans), jnp.float32)
+    for r in range(rows):
+        tile = value[8 * (r // 8) : 8 * (r // 8) + 8, :]
+        moved = rolled(tile, width * r - start, 1)
+        kept = kept + jnp.where((row == r % 8) & (lane // width == r), moved, 0.0)
+    for step in (4, 2, 1):
+        kept = kept + rolled(kept, step, 0)
+    return kept
+
+
+def own_kernel(place, d_h1, weight, raw_lat, raw_cot, gains, shifts, sums_two, grad, extra, nine, d_act):
+    blocks, frames, flat, chans = raw_lat.shape
+    size = blocks * flat
+    depth = 9 * chans
+    me = place[0]
+    for ahead_by in range(3):
+        value = frame_of(d_h1, jnp.minimum(me + ahead_by, frames - 1), size)
+        if ahead_by:
+            value = jnp.where(me + ahead_by < frames, value, 0.0)
+        store_nine(nine, ahead_by, value, -1)
+
+    def term(frame, tap):
+        left = nine[frame * size : (frame + 1) * size, :]
+        return jnp.dot(left, weight[tap * depth : (tap + 1) * depth, :], preferred_element_type=jnp.float32)
+
+    d_act[...] = term(2, 0) + term(1, 1) + term(0, 2)
+
+    @pl.when(me == 0)
+    def _():
+        d_act[...] = d_act[...] + (term(0, 1) + (term(0, 0) + term(1, 0)))
+
+    count = size * (chans // GROUPS)
+    value = load_frame(raw_lat, me)
+    mean, factor = norm_parts(value)
+    normed = (value - mean) * factor
+    u = normed * gains[0:1, :] + shifts[0:1, :]
+    sig = jax.nn.sigmoid(u)
+    d_out = d_act[...].reshape(size // 8, 8, chans) * (sig * (1.0 + u * (1.0 - sig)))
+    d_shift = all_cols(d_out)
+    d_gain = all_cols(d_out * normed)
+    one = group_all(d_shift * gains[0:1, :]) / count
+    two = group_all(d_gain * gains[0:1, :]) / count
+    d_in = factor * (d_out * gains[0:1, :] - one - normed * two)
+    result = (load_frame(raw_cot, me) + d_in).astype(jnp.bfloat16).astype(jnp.float32)
+    grad[...] = result.reshape(blocks, flat, chans)
+
+    owned = chans - 40
+    pieces = [to_spare(part, owned, 32) for part in (*halves(d_gain), *halves(d_shift))]
+    gain_high, gain_low = halves(sums_two[0])
+    shift_high, shift_low = halves(sums_two[1])
+    turn = me % 4
+    mine = jnp.where(turn < 2, jnp.where(turn == 0, gain_high, gain_low), jnp.where(turn == 2, shift_high, shift_low))
+    extra[...] = jnp.concatenate(pieces, 0) + to_spare(0.5 * mine, owned + 32, 8)
+
+
+def sum_kernel(later, earlier, grad, out, *, clips):
+    total = earlier[0].astype(jnp.float32)
+    for d in range(1, clips):
+        total = total + earlier[d].astype(jnp.float32)
+    total = total / clips
+    rows = total.shape[0]
+    for p in range(out.shape[0]):
+        out[p, 0:rows, :] = later[...]
+        out[p, rows : 2 * rows, :] = total
+        out[p, 2 * rows :, :] = grad[p]
+
+
+def adam_kernel(every, moment, second, new_moment, new_second, direction, vector, grad_input):
     parts, tall, chans = every.shape
     owned = moment.shape[1]
     width = chans // parts
@@ -224,10 +317,18 @@
         new_moment[layer] = new_m
         new_second[layer] = new_v
         direction[layer] = new_m / bias_first / (jnp.sqrt(new_v / bias_second) + 1e-08)
-    sums = every[0, 2 * width :, :]
+    for p in range(parts):
+        grad_input[p] = every[p, 2 * width :, :].astype(jnp.bfloat16)
+    held = [every[p, width : 2 * width, :] for p in range(parts)]
+    summed = held[0]
     for p in range(1, parts):
-        sums = sums + every[p, 2 * width :, :]
-    vector[...] = sums[0:4] + sums[4:8]
+        summed = summed + held[p]
+    for row in range(2):
+        high = from_spare(summed[16 * row : 16 * row + 8], owned, 32)
+        low = from_spare(summed[16 * row + 8 : 16 * row + 16], owned, 32)
+        vector[row : row + 1, :] = (high + low)[0:1]
+        mine = sum(held[p] for p in range(parts) if p % 4 in (2 * row, 2 * row + 1))
+        vector[2 + row : 3 + row, :] = from_spare(mine, owned + 32, 8)[0:1]
 
 
 def called(kernel, outs, scratch, args, scalars=0, flops=0, limit=56):
@@ -266,8 +367,8 @@
 
 def kernel_grad(place, values, grads, extra, width, size, clips):
     places, chans = values.shape
-    outs = [jax.ShapeDtypeStruct((clips, width + extra.shape[0], chans), jnp.bfloat16)]
-    if extra.shape[0] == 0:
+    outs = [jax.ShapeDtypeStruct((clips, width, chans), jnp.bfloat16)]
+    if extra is None:
         body = lambda p, v, g, *rest: grad_kernel(p, v, g, None, *rest)
         args = (place, values, grads)
     else:
@@ -280,36 +381,26 @@
     return called(body, outs, scratch, args, 1, 2 * places * 27 * width * chans)[0]
 
 
+def own(place, d_h1, weight, raw_lat, raw_cot, gains, shifts, sums_two):
+    blocks, frames, flat, chans = raw_lat.shape
+    size = blocks * flat
+    outs = [
+        jax.ShapeDtypeStruct((blocks, flat, chans), jnp.float32),
+        jax.ShapeDtypeStruct((32, chans), jnp.float32),
+    ]
+    scratch = [pltpu.VMEM((3 * size, 9 * chans), jnp.bfloat16), pltpu.VMEM((size, chans), jnp.float32)]
+    args = (place, d_h1, weight, raw_lat, raw_cot, gains, shifts, sums_two)
+    return called(own_kernel, outs, scratch, args, 1, 2 * size * weight.size)
+
+
+def gathered(later, earlier, grads, clips):
+    parts, flat, chans = grads.shape
+    outs = [jax.ShapeDtypeStruct((parts, 2 * later.shape[0] + flat, chans), jnp.float32)]
+    return called(functools.partial(sum_kernel, clips=clips), outs, [], (later, earlier, grads))[0]
+
+
 def spread(value, axis):
     return lax.all_to_all(jnp.broadcast_to(value[None], (lax.axis_size(axis),) + value.shape), axis, 0, 0)
-
-
-def silu_slope(values):
-    sig = jax.nn.sigmoid(values)
-    return sig * (1.0 + values * (1.0 - sig))
-
-
-def group_sum(sums):
-    frames, chans = sums.shape
-    size = chans // GROUPS
-    return jnp.repeat(jnp.sum(sums.reshape(frames, GROUPS, size), -1), size, axis=-1)
-
-
-def frame_stats(values):
-    count = values.shape[1] * values.shape[2] * (values.shape[3] // GROUPS)
-    mean = group_sum(jnp.sum(values, (1, 2))) / count
-    var = group_sum(jnp.sum(values * values, (1, 2))) / count - mean * mean
-    return mean[:, None, None], lax.rsqrt(var + 1e-05)[:, None, None]
-
-
-def norm_back(normed, factor, gain, d_out):
-    count = normed.shape[1] * normed.shape[2] * (normed.shape[3] // GROUPS)
-    d_shift = jnp.sum(d_out, (1, 2))
-    d_gain = jnp.sum(d_out * normed, (1, 2))
-    one = group_sum(d_shift * gain)[:, None, None] / count
-    two = group_sum(d_gain * gain)[:, None, None] / count
-    d_in = factor * (d_out * gain - one - normed * two)
-    return d_in, jnp.sum(d_gain, 0), jnp.sum(d_shift, 0)
 
 
 def conv(values, weight, row_pad):
@@ -324,18 +415,6 @@
     )[0]
 
 
-def conv_back(grads, weight):
-    chans = grads.shape[-1]
-    return lax.conv_general_dilated(
-        grads[None],
-        weight.reshape(3, 3, 3, -1, chans)[::-1, ::-1, ::-1],
-        (1, 1, 1),
-        ((0, 0), (1, 1), (1, 1)),
-        dimension_numbers=("NDHWC", "DHWOI", "NDHWC"),
-        preferred_element_type=jnp.float32,
-    )[0]
-
-
 def per_device(latents, cotangent, conv_weights, gains, shifts, moment, second):
     frames, rows, cols, chans = latents.shape[1:]
     clips, parts = lax.axis_size("dp"), lax.axis_size("space")
@@ -345,41 +424,16 @@
     f32, bf16 = jnp.float32, jnp.bfloat16
     raw_lat = spread(latents[0].reshape(frames, rows * cols, chans), "space")
     raw_cot = spread(cotangent[0].reshape(frames, rows * cols, chans), "space")
-    turned = conv_weights[1].reshape(27, chans, chans).transpose(0, 2, 1).reshape(27 * chans, chans)
+    turned = conv_weights.reshape(2, 27, chans, chans).transpose(0, 1, 3, 2).reshape(2, 27 * chans, chans)
 
     a_one, h_one, a_two = ahead(raw_lat, conv_weights[0], gains, shifts)
     cot = raw_cot.transpose(1, 0, 2, 3).reshape(frames * size, chans)
-    none = jnp.zeros((0, chans), bf16)
-    later = kernel_grad(place, a_two, cot, none, width, size, clips)
+    later = kernel_grad(place, a_two, cot, None, width, size, clips)
+    later, raw_cot = lax.optimization_barrier((later, raw_cot))
     later = lax.all_to_all(later, "dp", 0, 0)
 
-    d_h1, sums_two = back(raw_cot, turned, h_one, gains, shifts)
-
-    def frame(raw):
-        value = lax.dynamic_slice_in_dim(raw, me, 1, 1)
-        return value.reshape(1, parts * rows, cols, chans).astype(f32)
-
-    xown = frame(raw_lat)
-    mean_one, factor_one = frame_stats(xown)
-    normed_one = (xown - mean_one) * factor_one
-    u_one = normed_one * gains[0] + shifts[0]
-    near = jnp.pad(d_h1.reshape(frames, size // cols, cols, chans), ((0, 2), (0, 0), (0, 0), (0, 0)))
-    near = lax.dynamic_slice_in_dim(near, me, 3, 0).astype(f32)
-    first = (me == 0).astype(f32)
-    near = jnp.stack(
-        [near[0], near[1] + first * near[0], near[2] + first * (near[0] + near[1])]
-    ).astype(bf16)
-    d_a1 = conv_back(near, conv_weights[0])
-    d_x, gain_one, shift_one = norm_back(normed_one, factor_one, gains[0], d_a1 * silu_slope(u_one))
-    grad_input = (frame(raw_cot) + d_x).astype(bf16)
-    grad_input = grad_input[0].reshape(parts, rows, cols, chans)
-    grad_input = lax.all_to_all(grad_input, "space", 0, 0)
-
-    share = 1.0 / parts
-    vectors = jnp.concatenate([gain_one[None], shift_one[None], sums_two[:, 0] * share])
-    high = vectors.astype(bf16)
-    low = (vectors - high.astype(f32)).astype(bf16)
-    extra = jnp.concatenate([high, low, jnp.zeros((8, chans), bf16)], 0)
+    d_h1, sums_two = back(raw_cot, turned[1], h_one, gains, shifts)
+    grads, extra = own(place, d_h1, turned[0], raw_lat, raw_cot, gains, shifts, sums_two)
     earlier = kernel_grad(place, a_one, d_h1, extra, width, size, clips)
     earlier = lax.all_to_all(earlier, "dp", 0, 0)
 
@@ -388,12 +442,16 @@
     tall = lax.dynamic_slice_in_dim(tall, me * rows, rows + 2, 1)
     decoded = (latents[0].astype(f32) + conv(tall, conv_weights[1], 0)).astype(bf16)
 
-    total = jnp.sum(jnp.concatenate([later, earlier], 1).astype(f32), 0) / clips
-    every = spread(total, "space")
+    later = jnp.sum(later.astype(f32), 0) / clips
+    every = gathered(later, earlier, grads, clips)
+    every = lax.all_to_all(every, "space", 0, 0)
     shape = jax.ShapeDtypeStruct(moment.shape, f32)
     outs = [shape, shape, shape, jax.ShapeDtypeStruct((4, chans), f32)]
-    new_moment, new_second, direction, vector = called(adam_kernel, outs, [], (every, moment, second))
-    return (decoded[None], grad_input[None], new_moment, new_second, direction, vector)
+    outs.append(jax.ShapeDtypeStruct((frames, rows * cols, chans), bf16))
+    outs = called(adam_kernel, outs, [], (every, moment, second))
+    new_moment, new_second, direction, vector, grad_input = outs
+    grad_input = grad_input.reshape(latents.shape)
+    return (decoded[None], grad_input, new_moment, new_second, direction, vector)
 
 
 def solution(mesh):

time: 173 us -> 161 us (0.931)
  blocking collectives: 0 us -> 20.3 us
  other arithmetic: 15.6 us -> 2.73 us
  starting transfers between devices: 37.6 us -> 28.5 us
  waiting for transfers between devices: 29.1 us -> 20.7 us
  matrix products: 13.4 us -> 5.37 us
  Pallas kernels: 44 us -> 51.8 us
    all_to_all x0 -> x1, blocking collectives: none -> 20.3 us  [spread(): lax.all_to_all(jnp.broadcast_to(value[None], (lax.axis_size(axis),) + val...]
    all_to_all x3 -> x1, starting transfers between devices: 14.7 us -> 3.55 us  [spread(): lax.all_to_all(jnp.broadcast_to(value[None], (lax.axis_size(axis),) + val...]
    all_to_all x3 -> x1, waiting for transfers between devices: 9.31 us -> 0.01 us  [spread(): lax.all_to_all(jnp.broadcast_to(value[None], (lax.axis_size(axis),) + val...]
    conv_general_dilated x1 -> x0, matrix products: 7.94 us -> none  [conv_back(): lax.conv_general_dilated(grads[None], weight.reshape(3, 3, 3, -1, chans)[...]
    pallas_call x5 -> x7, Pallas kernels: 44 us -> 51.8 us  [called(): pl.pallas_call(kernel, out_shape=outs, in_specs=[small] * scalars + [whol...]
    reshape x4 -> x1, local copies, waits for them, and re-layouts: 3.03 us -> 10.3 us  [per_device(): conv_weights.reshape(2, 27, chans, chans).transpose(0, 1, 3, 2)]
    squeeze x0 -> x1, local copies, waits for them, and re-layouts: none -> 6.45 us  [per_device(): a_one, h_one, a_two = ahead(raw_lat, conv_weights[0], gains, shifts)]
    another operation x5 -> x0, local copies, waits for them, and re-layouts: 6.1 us -> none  [the longest x1 3.6 us: per_device(): conv_weights[1].reshape(27, chans, chans).transpose(0, 2, 1)]
  transfers between devices with their start and end apart: 6 -> 4, of which waited for: 5 -> 2; matrix products, arithmetic and copies ran while one was open for 28% -> 22% of each run, Pallas kernels for 12% -> 17%
where the time goes in v1:
time: 161 us
  Pallas kernels  51.8 us (32%)
  local copies, waits for them, and re-layouts  30.5 us (19%)
  starting transfers between devices  28.5 us (18%)
  waiting for transfers between devices  20.7 us (13%)
  blocking collectives  20.3 us (13%)
  matrix products  5.37 us (3%)
  other arithmetic  2.73 us (2%)
    pallas_call x7, Pallas kernels, called(): pl.pallas_call(kernel, out_shape=outs, in_specs=[small] * scalars + [whol...  51.8 us
    all_to_all x1, blocking collectives, spread(): lax.all_to_all(jnp.broadcast_to(value[None], (lax.axis_size(axis),) + val...  20.3 us
    all_to_all x1, waiting for transfers between devices, per_device(): earlier = lax.all_to_all(earlier, 'dp', 0, 0)  14.5 us
    reshape x1, local copies, waits for them, and re-layouts, per_device(): conv_weights.reshape(2, 27, chans, chans).transpose(0, 1, 3, 2)  10.3 us
    all_to_all x1, starting transfers between devices, per_device(): later = lax.all_to_all(later, 'dp', 0, 0)  10.1 us
    all_to_all x1, starting transfers between devices, per_device(): earlier = lax.all_to_all(earlier, 'dp', 0, 0)  8.59 us
    slice x1, local copies, waits for them, and re-layouts, per_device(): turned[0]  6.78 us
    squeeze x1, local copies, waits for them, and re-layouts, per_device(): a_one, h_one, a_two = ahead(raw_lat, conv_weights[0], gains, shifts)  6.45 us
  transfers between devices with their start and end apart: 4, of which 2 were waited for; matrix products, arithmetic and copies ran while one was open for 22% of the time, Pallas kernels for 17%

profile of v1, /device:TPU:2, one launch (start us, length us, event | category | flops | bytes accessed | tf_op | source)
XLA Modules:
  0.0 160.5 jit_solution(12102773448125391286)
XLA Ops:
  0.6 0.9 broadcast_in_dim.22
  1.6 20.3 %all_to_all.25.raw.raw_cot = bf16[8,8,24,256]{3,2,1,0:T(8,128)(2,1)S(1)} all-to-all(bf16[8,8,24,256]{3,2,1,0:T(8,128)(2,1)S(1)} %broadcast_in_dim.22), channel_id=1, replica_groups=mesh['dp'=32,'space'=8] {'space'}, dimensions={0} | all-to-all | bytes 1572864 | tf_op jit(solution)/shard_map/all_to_all | solution.py:403
  21.8 0.0 copy-start
  21.9 1.9 %broadcast_in_dim.19 = bf16[8,8,24,256]{3,2,1,0:T(8,128)(2,1)} broadcast(bf16[8,24,256]{2,1,0:T(8,128)(2,1)} %bitcast.28), dimensions={1,2,3} | broadcast | bytes 884736 | tf_op jit(solution)/shard_map/broadcast_in_dim | solution.py:403
  23.8 3.5 %all-to-all-start = ((bf16[8,8,24,256]{3,2,1,0:T(8,128)(2,1)}), bf16[8,8,24,256]{3,2,1,0:T(8,128)(2,1)S(1)}, u32[]{:S(2)}, u32[]{:S(2)}) async-start(bf16[8,8,24,256]{3,2,1,0:T(8,128)(2,1)} %broadcast_in_dim.19), calls=%async_computation | async-start | bytes 1572864 | tf_op jit(solution)/shard_map/all_to_all | solution.py:403
  27.3 6.4 %slice_bitcast_fusion = (bf16[6912,256]{1,0:T(8,128)(2,1)}, bf16[1,6912,256]{2,1,0:T(8,128)(2,1)}) fusion(bf16[2,6912,256]{2,1,0:T(8,128)(2,1)} %param.9), kind=kLoop, calls=%fused_computation | loop fusion | bytes 14155776 | tf_op jit(solution)/shard_map/squeeze | solution.py:429
  33.8 10.3 %copy.19 = bf16[2,27,256,256]{2,3,1,0:T(8,128)(2,1)} copy(bf16[2,27,256,256]{3,2,1,0:T(8,128)(2,1)} %bitcast.19) | data formatting | bytes 14155776 | tf_op jit(solution)/shard_map/reshape | solution.py:427
  44.1 0.0 copy-done
  44.1 1.0 copy.18
  45.0 0.0 all-to-all-done.raw.raw_lat
  45.0 0.0 copy-start.2
  45.0 0.9 copy-done.2
  45.9 14.8 %shard_map.118 = (bf16[1536,256]{1,0:T(8,128)(2,1)}, bf16[1536,256]{1,0:T(8,128)(2,1)}, bf16[1536,256]{1,0:T(8,128)(2,1)}) custom-call(bf16[8,8,24,256]{3,2,1,0:T(8,128)(2,1)} %copy-done.2, bf16[6912,256]{1,0:T(8,128)(2,1)} %get-tuple-element.48.weight, f32[2,256]{1,0:T(2,128)} %gains.5, f32[2,256]{1,0:T(2,128)} %shifts.5), custom_call_target="tpu_custom_call" | custom-call | flops 5435817984 | bytes 6688768 | tf_op jit(solution)/shard_map/pallas_call | solution.py:338
  60.7 5.4 %shard_map.119 = bf16[32,32,256]{2,1,0:T(8,128)(2,1)} custom-call(s32[1]{0:T(128)} %bitcast.6.p.place, bf16[1536,256]{1,0:T(8,128)(2,1)} %get-tuple-element.20.v, bf16[1536,256]{1,0:T(8,128)(2,1)} %bitcast.26), custom_call_target="tpu_custom_call" | custom-call | flops 679477248 | bytes 2097156 | tf_op jit(solution)/shard_map/pallas_call | solution.py:338
  66.0 10.1 %all-to-all-start.2 = ((bf16[32,32,256]{2,1,0:T(8,128)(2,1)}), bf16[32,32,256]{2,1,0:T(8,128)(2,1)}, u32[]{:S(2)}, u32[]{:S(2)}) async-start(bf16[32,32,256]{2,1,0:T(8,128)(2,1)} %shard_map.119), calls=%async_computation.2 | async-start | bytes 1048576 | tf_op jit(solution)/shard_map/all_to_all | solution.py:433
  76.2 6.8 %fusion.11 = (bf16[1,27,256,256]{3,2,1,0:T(8,128)(2,1)}, bf16[1,27,256,256]{3,2,1,0:T(8,128)(2,1)}) fusion(bf16[2,27,256,256]{3,2,1,0:T(8,128)(2,1)} %bitcast.20), kind=kLoop, calls=%fused_computation.21 | loop fusion | bytes 14155776 | tf_op jit(solution)/shard_map/slice | solution.py:436
  83.0 15.7 %shard_map.120 = (bf16[1536,256]{1,0:T(8,128)(2,1)}, f32[2,8,256]{2,1,0:T(8,128)}) custom-call(bf16[8,8,24,256]{3,2,1,0:T(8,128)(2,1)} %copy-done, bf16[6912,256]{1,0:T(8,128)(2,1)} %bitcast.24, bf16[1536,256]{1,0:T(8,128)(2,1)} %get-tuple-element.24.h_one, f32[2,256]{1,0:T(2,128)} %gains.5, f32[2,256]{1,0:T(2,128)} %shifts.5), custom_call_target="tpu_custom_call" | custom-call | flops 5435817984 | bytes 5918720 | tf_op jit(solution)/shard_map/pallas_call | solution.py:338
  98.7 5.8 %shard_map.121 = (f32[8,24,256]{2,1,0:T(8,128)}, f32[32,256]{1,0:T(8,128)}) custom-call(s32[1]{0:T(128)} %bitcast.6.p.place, bf16[1536,256]{1,0:T(8,128)(2,1)} %get-tuple-element.25.d_h1.grads, bf16[6912,256]{1,0:T(8,128)(2,1)} %bitcast.21, bf16[8,8,24,256]{3,2,1,0:T(8,128)(2,1)} %copy-done.2, bf16[8,8,24,256]{3,2,1,0:T(8,128)(2,1)} %copy-done, ...), custom_call_target="tpu_custom_call" | custom-call | flops 679477248 | bytes 6148100 | tf_op jit(solution)/shard_map/pallas_call | solution.py:338
  104.4 5.4 %shard_map.122 = bf16[32,32,256]{2,1,0:T(8,128)(2,1)} custom-call(s32[1]{0:T(128)} %bitcast.6.p.place, bf16[1536,256]{1,0:T(8,128)(2,1)} %get-tuple-element.22.values, bf16[1536,256]{1,0:T(8,128)(2,1)} %get-tuple-element.25.d_h1.grads, f32[32,256]{1,0:T(8,128)} %get-tuple-element.27.extra), custom_call_target="tpu_custom_call" | custom-call | flops 679477248 | bytes 2129924 | tf_op jit(solution)/shard_map/pallas_call | solution.py:338
  109.8 0.0 copy-start.1
  109.8 0.0 all-to-all-done.2
  109.8 8.6 %all-to-all-start.3 = ((bf16[32,32,256]{2,1,0:T(8,128)(2,1)}), bf16[32,32,256]{2,1,0:T(8,128)(2,1)}, u32[]{:S(2)}, u32[]{:S(2)}) async-start(bf16[32,32,256]{2,1,0:T(8,128)(2,1)} %shard_map.122), calls=%async_computation.3 | async-start | bytes 1048576 | tf_op jit(solution)/shard_map/all_to_all | solution.py:438
  118.4 1.5 slice_bitcast_fusion.1
  119.9 1.1 convert_reduce_fusion
  121.1 0.6 broadcast_multiply_fusion.later
  121.7 14.5 %all-to-all-done.3.earlier = bf16[32,32,256]{2,1,0:T(8,128)(2,1)} async-done(((bf16[32,32,256]{2,1,0:T(8,128)(2,1)}), bf16[32,32,256]{2,1,0:T(8,128)(2,1)}, u32[]{:S(2)}, u32[]{:S(2)}) %all-to-all-start.3) | async-done | bytes 524320 | tf_op jit(solution)/shard_map/all_to_all | solution.py:438
  136.1 2.1 %shard_map.123 = f32[8,88,256]{2,1,0:T(8,128)} custom-call(f32[32,256]{1,0:T(8,128)} %broadcast_multiply_fusion.later, bf16[32,32,256]{2,1,0:T(8,128)(2,1)} %all-to-all-done.3.earlier, f32[8,24,256]{2,1,0:T(8,128)} %get-tuple-element.28.grad), custom_call_target="tpu_custom_call" | custom-call | bytes 1474560 | tf_op jit(solution)/shard_map/pallas_call | solution.py:338
  138.2 6.3 %all-to-all-start.4 = ((f32[8,88,256]{2,1,0:T(8,128)}), f32[8,88,256]{2,1,0:T(8,128)}, u32[]{:S(2)}, u32[]{:S(2)}) async-start(f32[8,88,256]{2,1,0:T(8,128)} %shard_map.123), calls=%async_computation.4 | async-start | bytes 1441792 | tf_op jit(solution)/shard_map/all_to_all | solution.py:447
  144.5 1.0 fusion.10
  145.5 0.0 copy-done.1
  145.5 5.4 %fusion = bf16[1,8,3,8,256]{4,0,3,2,1:T(2,128)(2,1)S(1)} fusion(bf16[3,3,3,256,256]{4,3,2,1,0:T(8,128)(2,1)S(1)} %bitcast.23, bf16[1,10,5,8,256]{4,3,2,1,0:T(8,128)(2,1)S(1)} %fusion.10, bf16[1,8,3,8,256]{4,3,2,1,0:T(8,128)(2,1)} %param.7), kind=kOutput, calls=%fused_computation.2 | convolution fusion | flops 623001600 | bytes 3940352 | tf_op jit(solution)/shard_map/conv_general_dilated | solution.py:408
  150.8 0.7 copy.20
  151.5 6.3 %all-to-all-done.4.every = f32[8,88,256]{2,1,0:T(8,128)} async-done(((f32[8,88,256]{2,1,0:T(8,128)}), f32[8,88,256]{2,1,0:T(8,128)}, u32[]{:S(2)}, u32[]{:S(2)}) %all-to-all-start.4) | async-done | bytes 720928 | tf_op jit(solution)/shard_map/all_to_all | solution.py:447
  157.8 2.8 %shard_map.124 = (f32[2,216,256]{2,1,0:T(8,128)}, f32[2,216,256]{2,1,0:T(8,128)}, f32[2,216,256]{2,1,0:T(8,128)}, f32[4,256]{1,0:T(4,128)}, bf16[8,24,256]{2,1,0:T(8,128)(2,1)}) custom-call(f32[8,88,256]{2,1,0:T(8,128)} %all-to-all-done.4.every, f32[2,216,256]{2,1,0:T(8,128)} %moment.1, f32[2,216,256]{2,1,0:T(8,128)} %second.1), custom_call_target="tpu_custom_call" | custom-call | bytes 3035136 | tf_op jit(solution)/shard_map/pallas_call | solution.py:338
Async XLA Ops:
  21.8 22.2 %copy-start = (bf16[8,8,24,256]{3,2,1,0:T(8,128)(2,1)}, bf16[8,8,24,256]{3,2,1,0:T(8,128)(2,1)S(1)}, u32[]{:S(2)}) copy-start(bf16[8,8,24,256]{3,2,1,0:T(8,128)(2,1)S(1)} %all_to_all.25.raw.raw_cot) | copy-start | bytes 2359300
  23.8 21.3 %all-to-all-start = ((bf16[8,8,24,256]{3,2,1,0:T(8,128)(2,1)}), bf16[8,8,24,256]{3,2,1,0:T(8,128)(2,1)S(1)}, u32[]{:S(2)}, u32[]{:S(2)}) async-start(bf16[8,8,24,256]{3,2,1,0:T(8,128)(2,1)} %broadcast_in_dim.19), calls=%async_computation | async-start | bytes 1572864 | tf_op jit(solution)/shard_map/all_to_all | solution.py:403
  45.0 0.9 copy-start.2
  66.0 43.7 %all-to-all-start.2 = ((bf16[32,32,256]{2,1,0:T(8,128)(2,1)}), bf16[32,32,256]{2,1,0:T(8,128)(2,1)}, u32[]{:S(2)}, u32[]{:S(2)}) async-start(bf16[32,32,256]{2,1,0:T(8,128)(2,1)} %shard_map.119), calls=%async_computation.2 | async-start | bytes 1048576 | tf_op jit(solution)/shard_map/all_to_all | solution.py:433
  109.8 35.7 %copy-start.1 = (bf16[1,6912,256]{2,1,0:T(8,128)(2,1)S(1)}, bf16[1,6912,256]{2,1,0:T(8,128)(2,1)}, u32[]{:S(2)}) copy-start(bf16[1,6912,256]{2,1,0:T(8,128)(2,1)} %get-tuple-element.49) | copy-start | bytes 10616836
  109.8 26.4 %all-to-all-start.3 = ((bf16[32,32,256]{2,1,0:T(8,128)(2,1)}), bf16[32,32,256]{2,1,0:T(8,128)(2,1)}, u32[]{:S(2)}, u32[]{:S(2)}) async-start(bf16[32,32,256]{2,1,0:T(8,128)(2,1)} %shard_map.122), calls=%async_computation.3 | async-start | bytes 1048576 | tf_op jit(solution)/shard_map/all_to_all | solution.py:438
  138.2 19.5 %all-to-all-start.4 = ((f32[8,88,256]{2,1,0:T(8,128)}), f32[8,88,256]{2,1,0:T(8,128)}, u32[]{:S(2)}, u32[]{:S(2)}) async-start(f32[8,88,256]{2,1,0:T(8,128)} %shard_map.123), calls=%async_computation.4 | async-start | bytes 1441792 | tf_op jit(solution)/shard_map/all_to_all | solution.py:447

commit v2 on v1

--- a/solution.py
+++ b/solution.py
@@ -89,12 +89,14 @@
     flat[pl.ds(pl.multiple_of(frame * size, 16), size), :] = value.reshape(size, -1).astype(flat.dtype)
 
 
-def ahead_kernel(raw, weight, gains, shifts, a_one, h_one, a_two, nine):
+def ahead_kernel(raw, weights, gains, shifts, a_one, h_one, a_two, nine, weight, sem):
+    copy = pltpu.make_async_copy(weights.at[0], weight, sem)
+    copy.start()
     frames, chans = raw.shape[1], raw.shape[3]
     size = raw.shape[0] * raw.shape[2]
     depth = 9 * chans
 
-    @pl.loop(0, frames)
+    @pl.loop(0, frames, unroll=frames)
     def _(t):
         value = load_frame(raw, t)
         mean, factor = norm_parts(value)
@@ -105,6 +107,7 @@
 
     nine[0:size, :] = nine[2 * size : 3 * size, :]
     nine[size : 2 * size, :] = nine[2 * size : 3 * size, :]
+    copy.wait()
 
     @pl.loop(0, frames // STEP)
     def _(b):
@@ -115,7 +118,7 @@
             total = part if total is None else total + part
         h_one[pl.ds(pl.multiple_of(b * STEP * size, 16), STEP * size), :] = total.astype(jnp.bfloat16)
 
-    @pl.loop(0, frames)
+    @pl.loop(0, frames, unroll=frames)
     def _(t):
         value = frame_of(h_one, t, size)
         mean, factor = norm_parts(value)
@@ -123,16 +126,19 @@
         put_frame(a_two, t, u * jax.nn.sigmoid(u))
 
 
-def back_kernel(raw, weight, h_one, gains, shifts, d_h1, vectors, nine, d_act):
+def back_kernel(raw, weights, h_one, gains, shifts, d_h1, vectors, nine, d_act, weight, sem):
+    copy = pltpu.make_async_copy(weights.at[1], weight, sem)
+    copy.start()
     frames, chans = raw.shape[1], raw.shape[3]
     size = raw.shape[0] * raw.shape[2]
     depth = 9 * chans
 
-    @pl.loop(0, frames)
+    @pl.loop(0, frames, unroll=frames)
     def _(t):
         store_nine(nine, t, load_frame(raw, t), -1)
 
     nine[frames * size :, :] = jnp.zeros((2 * size, depth), jnp.bfloat16)
+    copy.wait()
 
     @pl.loop(0, frames // STEP)
     def _(b):
@@ -150,7 +156,7 @@
     vectors[...] = jnp.zeros_like(vectors)
     count = size * (chans // GROUPS)
 
-    @pl.loop(0, frames)
+    @pl.loop(0, frames, unroll=frames)
     def _(t):
         value = frame_of(h_one, t, size)
         mean, factor = norm_parts(value)
@@ -180,9 +186,12 @@
     lane = lax.broadcasted_iota(jnp.int32, (chans, lanes), 1)
     pick = (chan == place[0] * outs + lane % outs).astype(jnp.bfloat16)
 
-    @pl.loop(0, frames)
+    @pl.loop(0, frames, unroll=frames)
     def _(t):
-        rows = grads[pl.ds(pl.multiple_of(t * size, 16), size), :]
+        if len(grads.shape) == 4:
+            rows = load_frame(grads, t).reshape(size, chans).astype(jnp.bfloat16)
+        else:
+            rows = grads[pl.ds(pl.multiple_of(t * size, 16), size), :]
         spread_out = jnp.dot(rows, pick, preferred_element_type=jnp.float32).reshape(size // 8, 8, lanes)
         for piece in range(lanes // 128):
             value = spread_out[:, :, piece * 128 : (piece + 1) * 128]
@@ -248,7 +257,9 @@
     return kept
 
 
-def own_kernel(place, d_h1, weight, raw_lat, raw_cot, gains, shifts, sums_two, grad, extra, nine, d_act):
+def own_kernel(place, d_h1, weights, raw_lat, raw_cot, gains, shifts, sums_two, grad, extra, nine, d_act, weight, sem):
+    copy = pltpu.make_async_copy(weights.at[0], weight, sem)
+    copy.start()
     blocks, frames, flat, chans = raw_lat.shape
     size = blocks * flat
     depth = 9 * chans
@@ -258,6 +269,7 @@
         if ahead_by:
             value = jnp.where(me + ahead_by < frames, value, 0.0)
         store_nine(nine, ahead_by, value, -1)
+    copy.wait()
 
     def term(frame, tap):
         left = nine[frame * size : (frame + 1) * size, :]
@@ -331,14 +343,55 @@
         vector[2 + row : 3 + row, :] = from_spare(mine, owned + 32, 8)[0:1]
 
 
-def called(kernel, outs, scratch, args, scalars=0, flops=0, limit=56):
+def turn_kernel(weights, turned):
+    chans = weights.shape[2]
+    for tap in range(weights.shape[1] // chans):
+        rows = slice(tap * chans, (tap + 1) * chans)
+        turned[0, rows, :] = weights[0, rows, :].T
+
+
+def decode_kernel(place, a_two, weights, latent, decoded, tall, nine, weight, sem):
+    copy = pltpu.make_async_copy(weights.at[1], weight, sem)
+    copy.start()
+    frames, flat, chans = latent.shape
+    size = a_two.shape[0] // frames
+    rows, every = flat // 8, size // 8
+    pitch = nine.shape[0] // (frames + 2)
+    depth = 9 * chans
+    tall[0] = jnp.zeros(tall.shape[1:], jnp.float32)
+    tall[every + 1] = jnp.zeros(tall.shape[1:], jnp.float32)
+    rest = jnp.zeros((pitch // 8 - rows, 8, chans), jnp.float32)
+    for t in range(frames):
+        tall[1 : every + 1] = frame_of(a_two, t, size)
+        part = tall[pl.ds(place[0] * rows, rows + 2)]
+        for w in range(3):
+            moved = col_shifted(part, w - 1)
+            for h in range(3):
+                view = jnp.concatenate([moved[h : h + rows], rest], 0).reshape(pitch, chans)
+                number = 3 * h + w
+                nine[(t + 2) * pitch : (t + 3) * pitch, number * chans : (number + 1) * chans] = view.astype(jnp.bfloat16)
+    nine[0:pitch, :] = nine[2 * pitch : 3 * pitch, :]
+    nine[pitch : 2 * pitch, :] = nine[2 * pitch : 3 * pitch, :]
+    copy.wait()
+    total = None
+    for t in range(3):
+        left = nine[t * pitch : (t + frames) * pitch, :]
+        part = jnp.dot(left, weight[t * depth : (t + 1) * depth, :], preferred_element_type=jnp.float32)
+        total = part if total is None else total + part
+    for t in range(frames):
+        value = latent[t].astype(jnp.float32) + total[t * pitch : t * pitch + flat, :]
+        decoded[t] = value.astype(jnp.bfloat16)
+
+
+def called(kernel, outs, scratch, args, scalars=0, flops=0, apart=None, limit=16):
     whole = pl.BlockSpec(memory_space=pltpu.VMEM)
     small = pl.BlockSpec(memory_space=pltpu.SMEM)
+    away = pl.BlockSpec(memory_space=pl.ANY)
     moved = sum(math.prod(a.shape) * a.dtype.itemsize for a in (*args, *outs))
     return pl.pallas_call(
         kernel,
         out_shape=outs,
-        in_specs=[small] * scalars + [whole] * (len(args) - scalars),
+        in_specs=[small if n < scalars else away if n == apart else whole for n in range(len(args))],
         out_specs=[whole] * len(outs),
         scratch_shapes=scratch,
         compiler_params=pltpu.CompilerParams(vmem_limit_bytes=limit * 2**20),
@@ -346,23 +399,27 @@
     )(*args)
 
 
-def ahead(raw, weight, gains, shifts):
+def held(weights):
+    return [pltpu.VMEM(weights.shape[1:], weights.dtype), pltpu.SemaphoreType.DMA]
+
+
+def ahead(raw, weights, gains, shifts):
     blocks, frames, flat, chans = raw.shape
     places = blocks * frames * flat
     shape = jax.ShapeDtypeStruct((places, chans), jnp.bfloat16)
-    scratch = [pltpu.VMEM((places + 2 * blocks * flat, 9 * chans), jnp.bfloat16)]
-    return called(ahead_kernel, [shape] * 3, scratch, (raw, weight, gains, shifts), 0, 2 * places * weight.size)
-
-
-def back(raw, weight, h_one, gains, shifts):
+    scratch = [pltpu.VMEM((places + 2 * blocks * flat, 9 * chans), jnp.bfloat16)] + held(weights)
+    return called(ahead_kernel, [shape] * 3, scratch, (raw, weights, gains, shifts), 0, places * weights.size, 1, 58)
+
+
+def back(raw, weights, h_one, gains, shifts):
     blocks, frames, flat, chans = raw.shape
     places = blocks * frames * flat
     outs = [jax.ShapeDtypeStruct((places, chans), jnp.bfloat16), jax.ShapeDtypeStruct((2, 8, chans), jnp.float32)]
     scratch = [
         pltpu.VMEM((places + 2 * blocks * flat, 9 * chans), jnp.bfloat16),
         pltpu.VMEM((places, chans), jnp.float32),
-    ]
-    return called(back_kernel, outs, scratch, (raw, weight, h_one, gains, shifts), 0, 2 * places * weight.size)
+    ] + held(weights)
+    return called(back_kernel, outs, scratch, (raw, weights, h_one, gains, shifts), 0, places * weights.size, 1, 58)
 
 
 def kernel_grad(place, values, grads, extra, width, size, clips):
@@ -381,16 +438,16 @@
     return called(body, outs, scratch, args, 1, 2 * places * 27 * width * chans)[0]
 
 
-def own(place, d_h1, weight, raw_lat, raw_cot, gains, shifts, sums_two):
+def own(place, d_h1, weights, raw_lat, raw_cot, gains, shifts, sums_two):
     blocks, frames, flat, chans = raw_lat.shape
     size = blocks * flat
     outs = [
         jax.ShapeDtypeStruct((blocks, flat, chans), jnp.float32),
         jax.ShapeDtypeStruct((32, chans), jnp.float32),
     ]
-    scratch = [pltpu.VMEM((3 * size, 9 * chans), jnp.bfloat16), pltpu.VMEM((size, chans), jnp.float32)]
-    args = (place, d_h1, weight, raw_lat, raw_cot, gains, shifts, sums_two)
-    return called(own_kernel, outs, scratch, args, 1, 2 * size * weight.size)
+    scratch = [pltpu.VMEM((3 * size, 9 * chans), jnp.bfloat16), pltpu.VMEM((size, chans), jnp.float32)] + held(weights)
+    args = (place, d_h1, weights, raw_lat, raw_cot, gains, shifts, sums_two)
+    return called(own_kernel, outs, scratch, args, 1, size * weights.size, 2, 58)
 
 
 def gathered(later, earlier, grads, clips):
@@ -399,20 +456,33 @@
     return called(functools.partial(sum_kernel, clips=clips), outs, [], (later, earlier, grads))[0]
 
 
+def turn(weights):
+    layers, depth, chans = weights.shape
+    block = pl.BlockSpec((1, depth // 9, chans), lambda k, n: (k, n, 0))
+    return pl.pallas_call(
+        turn_kernel,
+        grid=(layers, 9),
+        out_shape=jax.ShapeDtypeStruct(weights.shape, weights.dtype),
+        in_specs=[block],
+        out_specs=block,
+        cost_estimate=pl.CostEstimate(flops=0, bytes_accessed=4 * weights.size, transcendentals=0),
+    )(weights)
+
+
+def decode(place, a_two, weights, latent):
+    frames, flat, chans = latent.shape
+    size = a_two.shape[0] // frames
+    pitch = -(-flat // 16) * 16
+    outs = [jax.ShapeDtypeStruct(latent.shape, jnp.bfloat16)]
+    scratch = [
+        pltpu.VMEM((size // 8 + 2, 8, chans), jnp.float32),
+        pltpu.VMEM(((frames + 2) * pitch, 9 * chans), jnp.bfloat16),
+    ] + held(weights)
+    return called(decode_kernel, outs, scratch, (place, a_two, weights, latent), 1, frames * pitch * weights.size, 2, 58)[0]
+
+
 def spread(value, axis):
     return lax.all_to_all(jnp.broadcast_to(value[None], (lax.axis_size(axis),) + value.shape), axis, 0, 0)
-
-
-def conv(values, weight, row_pad):
-    chans = values.shape[-1]
-    return lax.conv_general_dilated(
-        values[None],
-        weight.reshape(3, 3, 3, chans, -1),
-        (1, 1, 1),
-        ((0, 0), (row_pad, row_pad), (1, 1)),
-        dimension_numbers=("NDHWC", "DHWIO", "NDHWC"),
-        preferred_element_type=jnp.float32,
-    )[0]
 
 
 def per_device(latents, cotangent, conv_weights, gains, shifts, moment, second):
@@ -422,25 +492,22 @@
     place = me.astype(jnp.int32).reshape(1)
     width, size = chans // parts, parts * rows * cols
     f32, bf16 = jnp.float32, jnp.bfloat16
-    raw_lat = spread(latents[0].reshape(frames, rows * cols, chans), "space")
-    raw_cot = spread(cotangent[0].reshape(frames, rows * cols, chans), "space")
-    turned = conv_weights.reshape(2, 27, chans, chans).transpose(0, 1, 3, 2).reshape(2, 27 * chans, chans)
-
-    a_one, h_one, a_two = ahead(raw_lat, conv_weights[0], gains, shifts)
-    cot = raw_cot.transpose(1, 0, 2, 3).reshape(frames * size, chans)
-    later = kernel_grad(place, a_two, cot, None, width, size, clips)
+    latent = latents[0].reshape(frames, rows * cols, chans)
+    raw_lat = spread(latent, "space")
+    turned = turn(conv_weights)
+    upstream, raw_lat, turned = lax.optimization_barrier((cotangent[0], raw_lat, turned))
+    raw_cot = spread(upstream.reshape(frames, rows * cols, chans), "space")
+
+    a_one, h_one, a_two = ahead(raw_lat, conv_weights, gains, shifts)
+    later = kernel_grad(place, a_two, raw_cot, None, width, size, clips)
     later, raw_cot = lax.optimization_barrier((later, raw_cot))
     later = lax.all_to_all(later, "dp", 0, 0)
 
-    d_h1, sums_two = back(raw_cot, turned[1], h_one, gains, shifts)
-    grads, extra = own(place, d_h1, turned[0], raw_lat, raw_cot, gains, shifts, sums_two)
+    d_h1, sums_two = back(raw_cot, turned, h_one, gains, shifts)
+    grads, extra = own(place, d_h1, turned, raw_lat, raw_cot, gains, shifts, sums_two)
     earlier = kernel_grad(place, a_one, d_h1, extra, width, size, clips)
     earlier = lax.all_to_all(earlier, "dp", 0, 0)
-
-    tall = a_two.reshape(frames, size // cols, cols, chans)
-    tall = jnp.pad(jnp.concatenate([tall[:1], tall[:1], tall], 0), ((0, 0), (1, 1), (0, 0), (0, 0)))
-    tall = lax.dynamic_slice_in_dim(tall, me * rows, rows + 2, 1)
-    decoded = (latents[0].astype(f32) + conv(tall, conv_weights[1], 0)).astype(bf16)
+    decoded = decode(place, a_two, conv_weights, latent)
 
     later = jnp.sum(later.astype(f32), 0) / clips
     every = gathered(later, earlier, grads, clips)
@@ -451,7 +518,7 @@
     outs = called(adam_kernel, outs, [], (every, moment, second))
     new_moment, new_second, direction, vector, grad_input = outs
     grad_input = grad_input.reshape(latents.shape)
-    return (decoded[None], grad_input, new_moment, new_second, direction, vector)
+    return (decoded.reshape(latents.shape), grad_input, new_moment, new_second, direction, vector)
 
 
 def solution(mesh):

time: 161 us -> 129 us (0.80)
  local copies, waits for them, and re-layouts: 30.5 us -> 6 us
  blocking collectives: 20.3 us -> 0 us
  waiting for transfers between devices: 20.7 us -> 30.2 us
  starting transfers between devices: 28.5 us -> 34.1 us
  matrix products: 5.37 us -> 0 us
  Pallas kernels: 51.8 us -> 56.6 us
  other arithmetic: 2.73 us -> 0.09 us
    all_to_all x1 -> x0, blocking collectives: 20.3 us -> none  [spread(): lax.all_to_all(jnp.broadcast_to(value[None], (lax.axis_size(axis),) + val...]
    reshape x1 -> x0, local copies, waits for them, and re-layouts: 10.3 us -> none  [per_device(): conv_weights.reshape(2, 27, chans, chans).transpose(0, 1, 3, 2)]
    all_to_all x1 -> x2, starting transfers between devices: 3.55 us -> 12.2 us  [spread(): lax.all_to_all(jnp.broadcast_to(value[None], (lax.axis_size(axis),) + val...]
    slice x2 -> x0, local copies, waits for them, and re-layouts: 8.32 us -> none  [the longest x1 6.78 us: per_device(): turned[0]]
    squeeze x1 -> x0, local copies, waits for them, and re-layouts: 6.45 us -> none  [per_device(): a_one, h_one, a_two = ahead(raw_lat, conv_weights[0], gains, shifts)]
    conv_general_dilated x1 -> x0, matrix products: 5.37 us -> none  [conv(): lax.conv_general_dilated(values[None], weight.reshape(3, 3, 3, chans, -1)...]
    pallas_call x7 -> x9, Pallas kernels: 51.8 us -> 56.6 us  [the longest x8 43.2 us: called(): pl.pallas_call(kernel, out_shape=outs, in_specs=[small if n < scalars els...]
    all_to_all x1 -> x2, waiting for transfers between devices: 0.01 us -> 4.19 us  [spread(): lax.all_to_all(jnp.broadcast_to(value[None], (lax.axis_size(axis),) + val...]
  transfers between devices with their start and end apart: 4 -> 5, of which waited for: 2 -> 4; matrix products, arithmetic and copies ran while one was open for 22% -> 0% of each run, Pallas kernels for 17% -> 40%
where the time goes in v2:
time: 129 us; the launch traced here: 128 us
  Pallas kernels  56.6 us (44%)
  starting transfers between devices  34.1 us (26%)
  waiting for transfers between devices  30.2 us (23%)
  local copies, waits for them, and re-layouts  6 us (5%)
    pallas_call x8, Pallas kernels, called(): pl.pallas_call(kernel, out_shape=outs, in_specs=[small if n < scalars els...  43.2 us
    all_to_all x1, waiting for transfers between devices, per_device(): earlier = lax.all_to_all(earlier, 'dp', 0, 0)  17.6 us
    pallas_call x1, Pallas kernels, turn(): pl.pallas_call(turn_kernel, grid=(layers, 9), out_shape=jax.ShapeDtypeStr...  13.4 us
    all_to_all x2, starting transfers between devices, spread(): lax.all_to_all(jnp.broadcast_to(value[None], (lax.axis_size(axis),) + val...  12.2 us
    all_to_all x1, starting transfers between devices, per_device(): later = lax.all_to_all(later, 'dp', 0, 0)  10.1 us
    all_to_all x1, waiting for transfers between devices, per_device(): every = lax.all_to_all(every, 'space', 0, 0)  8.45 us
    all_to_all x1, starting transfers between devices, per_device(): earlier = lax.all_to_all(earlier, 'dp', 0, 0)  8.28 us
    all_to_all x2, waiting for transfers between devices, spread(): lax.all_to_all(jnp.broadcast_to(value[None], (lax.axis_size(axis),) + val...  4.19 us
  transfers between devices with their start and end apart: 5, of which 4 were waited for; matrix products, arithmetic and copies ran while one was open for 0% of the time, Pallas kernels for 40%

profile of v2, /device:TPU:2, one launch (start us, length us, event | category | flops | bytes accessed | tf_op | source)
XLA Modules:
  0.0 127.8 jit_solution(13182346643659894754)
XLA Ops:
  0.6 1.8 %broadcast_in_dim.15 = bf16[8,8,24,256]{3,2,1,0:T(8,128)(2,1)} broadcast(bf16[8,24,256]{2,1,0:T(8,128)(2,1)} %bitcast.6), dimensions={1,2,3} | broadcast | bytes 884736 | tf_op jit(solution)/shard_map/broadcast_in_dim | solution.py:485
  2.5 6.0 %all-to-all-start = ((bf16[8,8,24,256]{3,2,1,0:T(8,128)(2,1)}), bf16[8,8,24,256]{3,2,1,0:T(8,128)(2,1)S(1)}, u32[]{:S(2)}, u32[]{:S(2)}) async-start(bf16[8,8,24,256]{3,2,1,0:T(8,128)(2,1)} %broadcast_in_dim.15), calls=%async_computation | async-start | bytes 1572864 | tf_op jit(solution)/shard_map/all_to_all | solution.py:485
  8.5 0.0 copy-start.9
  8.5 13.4 %shard_map.118.weights = bf16[2,6912,256]{2,1,0:T(8,128)(2,1)} custom-call(bf16[2,6912,256]{2,1,0:T(8,128)(2,1)} %weights.5), custom_call_target="tpu_custom_call" | custom-call | bytes 14155776 | tf_op jit(solution)/shard_map/pallas_call | solution.py:462
  21.9 1.0 all-to-all-done.raw.raw_lat
  22.9 0.0 copy-start.8
  22.9 0.0 copy-done.9
  22.9 1.0 broadcast_in_dim.17
  23.9 6.2 %all-to-all-start.1 = ((bf16[8,8,24,256]{3,2,1,0:T(8,128)(2,1)}), bf16[8,8,24,256]{3,2,1,0:T(8,128)(2,1)S(1)}, u32[]{:S(2)}, u32[]{:S(2)}) async-start(bf16[8,8,24,256]{3,2,1,0:T(8,128)(2,1)} %broadcast_in_dim.17), calls=%async_computation.1 | async-start | bytes 1572864 | tf_op jit(solution)/shard_map/all_to_all | solution.py:485
  30.1 0.0 copy-done.8
  30.1 10.7 %shard_map.119 = (bf16[1536,256]{1,0:T(8,128)(2,1)}, bf16[1536,256]{1,0:T(8,128)(2,1)}, bf16[1536,256]{1,0:T(8,128)(2,1)}) custom-call(bf16[8,8,24,256]{3,2,1,0:T(8,128)(2,1)} %copy-done.8, bf16[2,6912,256]{2,1,0:T(8,128)(2,1)} %weights.5, f32[2,256]{1,0:T(2,128)} %gains.5, f32[2,256]{1,0:T(2,128)} %shifts.5), custom_call_target="tpu_custom_call" | custom-call | flops 5435817984 | bytes 10227712 | tf_op jit(solution)/shard_map/pallas_call | solution.py:391
  40.8 3.2 %all-to-all-done.1.g.raw.raw_cot = bf16[8,8,24,256]{3,2,1,0:T(8,128)(2,1)S(1)} async-done(((bf16[8,8,24,256]{3,2,1,0:T(8,128)(2,1)}), bf16[8,8,24,256]{3,2,1,0:T(8,128)(2,1)S(1)}, u32[]{:S(2)}, u32[]{:S(2)}) %all-to-all-start.1) | async-done | bytes 786464 | tf_op jit(solution)/shard_map/all_to_all | solution.py:485
  44.0 0.0 copy-start
  44.0 0.0 copy-start.2
  44.0 1.4 %copy-done.2 = bf16[1536,256]{1,0:T(8,128)(2,1)S(1)} copy-done((bf16[1536,256]{1,0:T(8,128)(2,1)S(1)}, bf16[1536,256]{1,0:T(8,128)(2,1)}, u32[]{:S(2)}) %copy-start.2) | copy-done | bytes 786456
  45.4 3.0 %shard_map.121 = bf16[32,32,256]{2,1,0:T(8,128)(2,1)} custom-call(s32[1]{0:T(128)} %bitcast.place.p, bf16[1536,256]{1,0:T(8,128)(2,1)S(1)} %copy-done.2, bf16[8,8,24,256]{3,2,1,0:T(8,128)(2,1)S(1)} %all-to-all-done.1.g.raw.raw_cot), custom_call_target="tpu_custom_call" | custom-call | flops 679477248 | bytes 2097156 | tf_op jit(solution)/shard_map/pallas_call | solution.py:391
  48.4 10.1 %all-to-all-start.2 = ((bf16[32,32,256]{2,1,0:T(8,128)(2,1)}), bf16[32,32,256]{2,1,0:T(8,128)(2,1)S(1)}, u32[]{:S(2)}, u32[]{:S(2)}) async-start(bf16[32,32,256]{2,1,0:T(8,128)(2,1)} %shard_map.121), calls=%async_computation.2 | async-start | bytes 1048576 | tf_op jit(solution)/shard_map/all_to_all | solution.py:504
  58.5 0.0 copy-done
  58.5 12.2 %shard_map.122 = (bf16[1536,256]{1,0:T(8,128)(2,1)}, f32[2,8,256]{2,1,0:T(8,128)}) custom-call(bf16[8,8,24,256]{3,2,1,0:T(8,128)(2,1)} %copy-done, bf16[2,6912,256]{2,1,0:T(8,128)(2,1)} %shard_map.118.weights, bf16[1536,256]{1,0:T(8,128)(2,1)} %get-tuple-element.30.h_one, f32[2,256]{1,0:T(2,128)} %gains.5, f32[2,256]{1,0:T(2,128)} %shifts.5), custom_call_target="tpu_custom_call" | custom-call | flops 5435817984 | bytes 9457664 | tf_op jit(solution)/shard_map/pallas_call | solution.py:391
  70.7 0.0 copy-start.1
  70.7 0.0 copy-start.7
  70.8 6.8 %shard_map.123 = (f32[8,24,256]{2,1,0:T(8,128)}, f32[32,256]{1,0:T(8,128)}) custom-call(s32[1]{0:T(128)} %bitcast.place.p, bf16[1536,256]{1,0:T(8,128)(2,1)} %get-tuple-element.31.d_h1.grads, bf16[2,6912,256]{2,1,0:T(8,128)(2,1)} %shard_map.118.weights, bf16[8,8,24,256]{3,2,1,0:T(8,128)(2,1)} %copy-done.8, bf16[8,8,24,256]{3,2,1,0:T(8,128)(2,1)} %copy-done, ...), custom_call_target="tpu_custom_call" | custom-call | flops 679477248 | bytes 9687044 | tf_op jit(solution)/shard_map/pallas_call | solution.py:391
  77.6 0.0 copy-done.1
  77.6 0.0 copy-done.7
  77.6 0.0 copy-start.6
  77.6 0.7 copy-done.6
  78.4 0.0 copy-start.3
  78.4 0.0 copy-start.4
  78.4 3.1 %shard_map.124 = bf16[32,32,256]{2,1,0:T(8,128)(2,1)} custom-call(s32[1]{0:T(128)} %bitcast.place.p, bf16[1536,256]{1,0:T(8,128)(2,1)S(1)} %copy-done.7, bf16[1536,256]{1,0:T(8,128)(2,1)S(1)} %copy-done.1, f32[32,256]{1,0:T(8,128)S(1)} %copy-done.6), custom_call_target="tpu_custom_call" | custom-call | flops 679477248 | bytes 2129924 | tf_op jit(solution)/shard_map/pallas_call | solution.py:391
  81.4 0.0 all-to-all-done.2
  81.4 8.3 %all-to-all-start.3 = ((bf16[32,32,256]{2,1,0:T(8,128)(2,1)}), bf16[32,32,256]{2,1,0:T(8,128)(2,1)S(1)}, u32[]{:S(2)}, u32[]{:S(2)}) async-start(bf16[32,32,256]{2,1,0:T(8,128)(2,1)} %shard_map.124), calls=%async_computation.3 | async-start | bytes 1048576 | tf_op jit(solution)/shard_map/all_to_all | solution.py:509
  89.7 0.1 convert_reduce_fusion
  89.8 17.6 %all-to-all-done.3.earlier = bf16[32,32,256]{2,1,0:T(8,128)(2,1)S(1)} async-done(((bf16[32,32,256]{2,1,0:T(8,128)(2,1)}), bf16[32,32,256]{2,1,0:T(8,128)(2,1)S(1)}, u32[]{:S(2)}, u32[]{:S(2)}) %all-to-all-start.3) | async-done | bytes 524320 | tf_op jit(solution)/shard_map/all_to_all | solution.py:509
  107.4 0.0 copy-start.5
  107.4 0.9 copy-done.5
  108.3 1.0 shard_map.125
  109.3 3.5 %all-to-all-start.4 = ((f32[8,88,256]{2,1,0:T(8,128)}), f32[8,88,256]{2,1,0:T(8,128)S(1)}, u32[]{:S(2)}, u32[]{:S(2)}) async-start(f32[8,88,256]{2,1,0:T(8,128)} %shard_map.125), calls=%async_computation.4 | async-start | bytes 1441792 | tf_op jit(solution)/shard_map/all_to_all | solution.py:514
  112.9 4.9 %shard_map.120 = bf16[8,24,256]{2,1,0:T(8,128)(2,1)} custom-call(s32[1]{0:T(128)} %bitcast.place.p, bf16[1536,256]{1,0:T(8,128)(2,1)} %get-tuple-element.24.a_two.v, bf16[2,6912,256]{2,1,0:T(8,128)(2,1)} %weights.5, bf16[8,24,256]{2,1,0:T(8,128)(2,1)} %bitcast.7), custom_call_target="tpu_custom_call" | custom-call | flops 905969664 | bytes 8060932 | tf_op jit(solution)/shard_map/pallas_call | solution.py:391
  117.8 8.4 %all-to-all-done.4.every = f32[8,88,256]{2,1,0:T(8,128)S(1)} async-done(((f32[8,88,256]{2,1,0:T(8,128)}), f32[8,88,256]{2,1,0:T(8,128)S(1)}, u32[]{:S(2)}, u32[]{:S(2)}) %all-to-all-start.4) | async-done | bytes 720928 | tf_op jit(solution)/shard_map/all_to_all | solution.py:514
  126.2 0.0 copy-done.3
  126.2 0.0 copy-done.4
  126.2 1.5 %shard_map.126 = (f32[2,216,256]{2,1,0:T(8,128)}, f32[2,216,256]{2,1,0:T(8,128)}, f32[2,216,256]{2,1,0:T(8,128)}, f32[4,256]{1,0:T(4,128)}, bf16[8,24,256]{2,1,0:T(8,128)(2,1)}) custom-call(f32[8,88,256]{2,1,0:T(8,128)S(1)} %all-to-all-done.4.every, f32[2,216,256]{2,1,0:T(8,128)S(1)} %copy-done.3, f32[2,216,256]{2,1,0:T(8,128)S(1)} %copy-done.4), custom_call_target="tpu_custom_call" | custom-call | bytes 3035136 | tf_op jit(solution)/shard_map/pallas_call | solution.py:391
  (1 shorter events, 0.0 us)
Async XLA Ops:
  2.5 20.4 %all-to-all-start = ((bf16[8,8,24,256]{3,2,1,0:T(8,128)(2,1)}), bf16[8,8,24,256]{3,2,1,0:T(8,128)(2,1)S(1)}, u32[]{:S(2)}, u32[]{:S(2)}) async-start(bf16[8,8,24,256]{3,2,1,0:T(8,128)(2,1)} %broadcast_in_dim.15), calls=%async_computation | async-start | bytes 1572864 | tf_op jit(solution)/shard_map/all_to_all | solution.py:485
  8.5 14.4 %copy-start.9 = (bf16[1,8,3,8,256]{4,3,2,1,0:T(8,128)(2,1)S(1)}, bf16[1,8,3,8,256]{4,3,2,1,0:T(8,128)(2,1)}, u32[]{:S(2)}) copy-start(bf16[1,8,3,8,256]{4,3,2,1,0:T(8,128)(2,1)} %param.8) | copy-start | bytes 294916
  22.9 7.2 %copy-start.8 = (bf16[8,8,24,256]{3,2,1,0:T(8,128)(2,1)}, bf16[8,8,24,256]{3,2,1,0:T(8,128)(2,1)S(1)}, u32[]{:S(2)}) copy-start(bf16[8,8,24,256]{3,2,1,0:T(8,128)(2,1)S(1)} %all-to-all-done.raw.raw_lat) | copy-start | bytes 2359300
  23.9 20.0 %all-to-all-start.1 = ((bf16[8,8,24,256]{3,2,1,0:T(8,128)(2,1)}), bf16[8,8,24,256]{3,2,1,0:T(8,128)(2,1)S(1)}, u32[]{:S(2)}, u32[]{:S(2)}) async-start(bf16[8,8,24,256]{3,2,1,0:T(8,128)(2,1)} %broadcast_in_dim.17), calls=%async_computation.1 | async-start | bytes 1572864 | tf_op jit(solution)/shard_map/all_to_all | solution.py:485
  44.0 14.5 %copy-start = (bf16[8,8,24,256]{3,2,1,0:T(8,128)(2,1)}, bf16[8,8,24,256]{3,2,1,0:T(8,128)(2,1)S(1)}, u32[]{:S(2)}) copy-start(bf16[8,8,24,256]{3,2,1,0:T(8,128)(2,1)S(1)} %all-to-all-done.1.g.raw.raw_cot) | copy-start | bytes 2359300
  44.0 1.4 %copy-start.2 = (bf16[1536,256]{1,0:T(8,128)(2,1)S(1)}, bf16[1536,256]{1,0:T(8,128)(2,1)}, u32[]{:S(2)}) copy-start(bf16[1536,256]{1,0:T(8,128)(2,1)} %get-tuple-element.24.a_two.v) | copy-start | bytes 2359300
  48.4 33.0 %all-to-all-start.2 = ((bf16[32,32,256]{2,1,0:T(8,128)(2,1)}), bf16[32,32,256]{2,1,0:T(8,128)(2,1)S(1)}, u32[]{:S(2)}, u32[]{:S(2)}) async-start(bf16[32,32,256]{2,1,0:T(8,128)(2,1)} %shard_map.121), calls=%async_computation.2 | async-start | bytes 1048576 | tf_op jit(solution)/shard_map/all_to_all | solution.py:504
  70.7 6.8 %copy-start.1 = (bf16[1536,256]{1,0:T(8,128)(2,1)S(1)}, bf16[1536,256]{1,0:T(8,128)(2,1)}, u32[]{:S(2)}) copy-start(bf16[1536,256]{1,0:T(8,128)(2,1)} %get-tuple-element.31.d_h1.grads) | copy-start | bytes 2359300
  70.7 6.8 %copy-start.7 = (bf16[1536,256]{1,0:T(8,128)(2,1)S(1)}, bf16[1536,256]{1,0:T(8,128)(2,1)}, u32[]{:S(2)}) copy-start(bf16[1536,256]{1,0:T(8,128)(2,1)} %get-tuple-element.27.values) | copy-start | bytes 2359300
  77.6 0.8 copy-start.6
  78.4 47.9 %copy-start.3 = (f32[2,216,256]{2,1,0:T(8,128)S(1)}, f32[2,216,256]{2,1,0:T(8,128)}, u32[]{:S(2)}) copy-start(f32[2,216,256]{2,1,0:T(8,128)} %moment.1) | copy-start | bytes 1327108
  78.4 47.9 %copy-start.4 = (f32[2,216,256]{2,1,0:T(8,128)S(1)}, f32[2,216,256]{2,1,0:T(8,128)}, u32[]{:S(2)}) copy-start(f32[2,216,256]{2,1,0:T(8,128)} %second.1) | copy-start | bytes 1327108
  81.4 26.0 %all-to-all-start.3 = ((bf16[32,32,256]{2,1,0:T(8,128)(2,1)}), bf16[32,32,256]{2,1,0:T(8,128)(2,1)S(1)}, u32[]{:S(2)}, u32[]{:S(2)}) async-start(bf16[32,32,256]{2,1,0:T(8,128)(2,1)} %shard_map.124), calls=%async_computation.3 | async-start | bytes 1048576 | tf_op jit(solution)/shard_map/all_to_all | solution.py:509
  107.4 0.9 copy-start.5
  109.3 16.9 %all-to-all-start.4 = ((f32[8,88,256]{2,1,0:T(8,128)}), f32[8,88,256]{2,1,0:T(8,128)S(1)}, u32[]{:S(2)}, u32[]{:S(2)}) async-start(f32[8,88,256]{2,1,0:T(8,128)} %shard_map.125), calls=%async_computation.4 | async-start | bytes 1441792 | tf_op jit(solution)/shard_map/all_to_all | solution.py:514

commit v3 on v2

--- a/solution.py
+++ b/solution.py
@@ -89,9 +89,7 @@
     flat[pl.ds(pl.multiple_of(frame * size, 16), size), :] = value.reshape(size, -1).astype(flat.dtype)
 
 
-def ahead_kernel(raw, weights, gains, shifts, a_one, h_one, a_two, nine, weight, sem):
-    copy = pltpu.make_async_copy(weights.at[0], weight, sem)
-    copy.start()
+def ahead_part(raw, gains, shifts, a_one, h_one, a_two, nine, weight, copy):
     frames, chans = raw.shape[1], raw.shape[3]
     size = raw.shape[0] * raw.shape[2]
     depth = 9 * chans
@@ -109,7 +107,7 @@
     nine[size : 2 * size, :] = nine[2 * size : 3 * size, :]
     copy.wait()
 
-    @pl.loop(0, frames // STEP)
+    @pl.loop(0, frames // STEP, unroll=frames // STEP)
     def _(b):
         total = None
         for t in range(3):
@@ -126,9 +124,7 @@
         put_frame(a_two, t, u * jax.nn.sigmoid(u))
 
 
-def back_kernel(raw, weights, h_one, gains, shifts, d_h1, vectors, nine, d_act, weight, sem):
-    copy = pltpu.make_async_copy(weights.at[1], weight, sem)
-    copy.start()
+def back_part(raw, h_one, gains, shifts, d_h1, vectors, nine, d_act, weight, copy):
     frames, chans = raw.shape[1], raw.shape[3]
     size = raw.shape[0] * raw.shape[2]
     depth = 9 * chans
@@ -140,7 +136,7 @@
     nine[frames * size :, :] = jnp.zeros((2 * size, depth), jnp.bfloat16)
     copy.wait()
 
-    @pl.loop(0, frames // STEP)
+    @pl.loop(0, frames // STEP, unroll=frames // STEP)
     def _(b):
         total = None
         for t in range(3):
@@ -173,7 +169,7 @@
         put_frame(d_h1, t, factor * (d_out * gains[1:2, :] - one - normed * two))
 
 
-def grad_kernel(place, values, grads, extra, out, long, block, total):
+def grad_part(place, values, grads, extra, out, long, block, total):
     frames_size, chans = values.shape
     owners, tall, _ = out.shape
     size, outs = (long.shape[0] - frames_size) // 2, total.shape[0] // 27
@@ -257,9 +253,7 @@
     return kept
 
 
-def own_kernel(place, d_h1, weights, raw_lat, raw_cot, gains, shifts, sums_two, grad, extra, nine, d_act, weight, sem):
-    copy = pltpu.make_async_copy(weights.at[0], weight, sem)
-    copy.start()
+def own_part(place, d_h1, raw_lat, raw_cot, gains, shifts, sums_two, grad, extra, nine, d_act, weight, copy):
     blocks, frames, flat, chans = raw_lat.shape
     size = blocks * flat
     depth = 9 * chans
@@ -303,6 +297,25 @@
     turn = me % 4
     mine = jnp.where(turn < 2, jnp.where(turn == 0, gain_high, gain_low), jnp.where(turn == 2, shift_high, shift_low))
     extra[...] = jnp.concatenate(pieces, 0) + to_spare(0.5 * mine, owned + 32, 8)
+
+
+def first_kernel(place, raw, weights, gains, shifts, a_one, h_one, a_two, out, nine, weight, sem, long, block, total):
+    raw_lat, raw_cot = raw.at[:, 0], raw.at[:, 1]
+    copy = pltpu.make_async_copy(weights.at[0], weight, sem)
+    copy.start()
+    ahead_part(raw_lat, gains, shifts, a_one, h_one, a_two, nine, weight, copy)
+    grad_part(place, a_two, raw_cot, None, out, long, block, total)
+
+
+def second_kernel(place, raw, turned, h_one, a_one, gains, shifts, grad, out, nine, weight, sem, long, block, total, other, other_sem, d_act, own_act, d_h1, sums_two, extra):
+    raw_lat, raw_cot = raw.at[:, 0], raw.at[:, 1]
+    copy = pltpu.make_async_copy(turned.at[1], weight, sem)
+    copy.start()
+    other_copy = pltpu.make_async_copy(turned.at[0], other, other_sem)
+    other_copy.start()
+    back_part(raw_cot, h_one, gains, shifts, d_h1, sums_two, nine, d_act, weight, copy)
+    own_part(place, d_h1, raw_lat, raw_cot, gains, shifts, sums_two, grad, extra, nine, own_act, other, other_copy)
+    grad_part(place, a_one, d_h1, extra, out, long, block, total)
 
 
 def sum_kernel(later, earlier, grad, out, *, clips):
@@ -383,15 +396,14 @@
         decoded[t] = value.astype(jnp.bfloat16)
 
 
-def called(kernel, outs, scratch, args, scalars=0, flops=0, apart=None, limit=16):
+def called(kernel, outs, scratch, args, specs=None, flops=0, limit=16):
     whole = pl.BlockSpec(memory_space=pltpu.VMEM)
-    small = pl.BlockSpec(memory_space=pltpu.SMEM)
-    away = pl.BlockSpec(memory_space=pl.ANY)
+    specs = specs or [whole] * len(args)
     moved = sum(math.prod(a.shape) * a.dtype.itemsize for a in (*args, *outs))
     return pl.pallas_call(
         kernel,
         out_shape=outs,
-        in_specs=[small if n < scalars else away if n == apart else whole for n in range(len(args))],
+        in_specs=[whole if spec is None else spec for spec in specs],
         out_specs=[whole] * len(outs),
         scratch_shapes=scratch,
         compiler_params=pltpu.CompilerParams(vmem_limit_bytes=limit * 2**20),
@@ -403,51 +415,56 @@
     return [pltpu.VMEM(weights.shape[1:], weights.dtype), pltpu.SemaphoreType.DMA]
 
 
-def ahead(raw, weights, gains, shifts):
-    blocks, frames, flat, chans = raw.shape
-    places = blocks * frames * flat
-    shape = jax.ShapeDtypeStruct((places, chans), jnp.bfloat16)
-    scratch = [pltpu.VMEM((places + 2 * blocks * flat, 9 * chans), jnp.bfloat16)] + held(weights)
-    return called(ahead_kernel, [shape] * 3, scratch, (raw, weights, gains, shifts), 0, places * weights.size, 1, 58)
-
-
-def back(raw, weights, h_one, gains, shifts):
-    blocks, frames, flat, chans = raw.shape
-    places = blocks * frames * flat
-    outs = [jax.ShapeDtypeStruct((places, chans), jnp.bfloat16), jax.ShapeDtypeStruct((2, 8, chans), jnp.float32)]
-    scratch = [
-        pltpu.VMEM((places + 2 * blocks * flat, 9 * chans), jnp.bfloat16),
-        pltpu.VMEM((places, chans), jnp.float32),
-    ] + held(weights)
-    return called(back_kernel, outs, scratch, (raw, weights, h_one, gains, shifts), 0, places * weights.size, 1, 58)
-
-
-def kernel_grad(place, values, grads, extra, width, size, clips):
-    places, chans = values.shape
-    outs = [jax.ShapeDtypeStruct((clips, width, chans), jnp.bfloat16)]
-    if extra is None:
-        body = lambda p, v, g, *rest: grad_kernel(p, v, g, None, *rest)
-        args = (place, values, grads)
-    else:
-        body, args = grad_kernel, (place, values, grads, extra)
-    scratch = [
+def small():
+    return pl.BlockSpec(memory_space=pltpu.SMEM)
+
+
+def away():
+    return pl.BlockSpec(memory_space=pl.ANY)
+
+
+def scratches(raw, weights, width):
+    blocks, _, frames, flat, chans = raw.shape
+    size = blocks * flat
+    places = frames * size
+    return [
+        pltpu.VMEM((places + 2 * size, 9 * chans), jnp.bfloat16),
+        *held(weights),
         pltpu.VMEM((places + 2 * size, chans), jnp.bfloat16),
         pltpu.VMEM((places, -(-9 * width // 128) * 128), jnp.bfloat16),
         pltpu.VMEM((27 * width, chans), jnp.float32),
     ]
-    return called(body, outs, scratch, args, 1, 2 * places * 27 * width * chans)[0]
-
-
-def own(place, d_h1, weights, raw_lat, raw_cot, gains, shifts, sums_two):
-    blocks, frames, flat, chans = raw_lat.shape
+
+
+def first_part(place, raw, weights, gains, shifts, width, clips):
+    blocks, _, frames, flat, chans = raw.shape
+    places = blocks * frames * flat
+    shape = jax.ShapeDtypeStruct((places, chans), jnp.bfloat16)
+    outs = [shape, shape, shape, jax.ShapeDtypeStruct((clips, width, chans), jnp.bfloat16)]
+    args = (place, raw, weights, gains, shifts)
+    specs = [small(), None, away(), None, None]
+    return called(first_kernel, outs, scratches(raw, weights, width), args, specs, places * weights.size, 58)
+
+
+def second_part(place, raw, turned, h_one, a_one, gains, shifts, width, clips):
+    blocks, _, frames, flat, chans = raw.shape
     size = blocks * flat
+    places = frames * size
     outs = [
         jax.ShapeDtypeStruct((blocks, flat, chans), jnp.float32),
-        jax.ShapeDtypeStruct((32, chans), jnp.float32),
+        jax.ShapeDtypeStruct((clips, width, chans), jnp.bfloat16),
     ]
-    scratch = [pltpu.VMEM((3 * size, 9 * chans), jnp.bfloat16), pltpu.VMEM((size, chans), jnp.float32)] + held(weights)
-    args = (place, d_h1, weights, raw_lat, raw_cot, gains, shifts, sums_two)
-    return called(own_kernel, outs, scratch, args, 1, size * weights.size, 2, 58)
+    scratch = scratches(raw, turned, width) + [
+        *held(turned),
+        pltpu.VMEM((places, chans), jnp.float32),
+        pltpu.VMEM((size, chans), jnp.float32),
+        pltpu.VMEM((places, chans), jnp.bfloat16),
+        pltpu.VMEM((2, 8, chans), jnp.float32),
+        pltpu.VMEM((32, chans), jnp.float32),
+    ]
+    args = (place, raw, turned, h_one, a_one, gains, shifts)
+    specs = [small(), None, away(), None, None, None, None]
+    return called(second_kernel, outs, scratch, args, specs, places * turned.size, 58)
 
 
 def gathered(later, earlier, grads, clips):
@@ -478,7 +495,8 @@
         pltpu.VMEM((size // 8 + 2, 8, chans), jnp.float32),
         pltpu.VMEM(((frames + 2) * pitch, 9 * chans), jnp.bfloat16),
     ] + held(weights)
-    return called(decode_kernel, outs, scratch, (place, a_two, weights, latent), 1, frames * pitch * weights.size, 2, 58)[0]
+    args = (place, a_two, weights, latent)
+    return called(decode_kernel, outs, scratch, args, [small(), None, away(), None], frames * pitch * weights.size, 58)[0]
 
 
 def spread(value, axis):
@@ -490,22 +508,15 @@
     clips, parts = lax.axis_size("dp"), lax.axis_size("space")
     me = lax.axis_index("space")
     place = me.astype(jnp.int32).reshape(1)
-    width, size = chans // parts, parts * rows * cols
+    width = chans // parts
     f32, bf16 = jnp.float32, jnp.bfloat16
     latent = latents[0].reshape(frames, rows * cols, chans)
-    raw_lat = spread(latent, "space")
-    turned = turn(conv_weights)
-    upstream, raw_lat, turned = lax.optimization_barrier((cotangent[0], raw_lat, turned))
-    raw_cot = spread(upstream.reshape(frames, rows * cols, chans), "space")
-
-    a_one, h_one, a_two = ahead(raw_lat, conv_weights, gains, shifts)
-    later = kernel_grad(place, a_two, raw_cot, None, width, size, clips)
-    later, raw_cot = lax.optimization_barrier((later, raw_cot))
+    both = jnp.stack([latent, cotangent[0].reshape(latent.shape)])
+    raw, turned = lax.optimization_barrier((spread(both, "space"), turn(conv_weights)))
+
+    a_one, h_one, a_two, later = first_part(place, raw, conv_weights, gains, shifts, width, clips)
     later = lax.all_to_all(later, "dp", 0, 0)
-
-    d_h1, sums_two = back(raw_cot, turned, h_one, gains, shifts)
-    grads, extra = own(place, d_h1, turned, raw_lat, raw_cot, gains, shifts, sums_two)
-    earlier = kernel_grad(place, a_one, d_h1, extra, width, size, clips)
+    grads, earlier = second_part(place, raw, turned, h_one, a_one, gains, shifts, width, clips)
     earlier = lax.all_to_all(earlier, "dp", 0, 0)
     decoded = decode(place, a_two, conv_weights, latent)
 

time: 129 us -> 121 us (0.938)
  starting transfers between devices: 34.1 us -> 28.1 us
  waiting for transfers between devices: 30.2 us -> 35.6 us
  Pallas kernels: 56.6 us -> 51.2 us
  local copies, waits for them, and re-layouts: 6 us -> 3.6 us
    all_to_all x2 -> x1, starting transfers between devices: 12.2 us -> 6.03 us  [spread(): lax.all_to_all(jnp.broadcast_to(value[None], (lax.axis_size(axis),) + val...]
    all_to_all x2 -> x1, waiting for transfers between devices: 4.19 us -> 9.56 us  [spread(): lax.all_to_all(jnp.broadcast_to(value[None], (lax.axis_size(axis),) + val...]
    pallas_call x8 -> x5, Pallas kernels: 43.2 us -> 37.9 us  [called(): pl.pallas_call(kernel, out_shape=outs, in_specs=[whole if spec is None el...]
    broadcast_in_dim x2 -> x1, local copies, waits for them, and re-layouts: 2.87 us -> 1.41 us  [spread(): jnp.broadcast_to(value[None], (lax.axis_size(axis),) + value.shape)]
    unnamed x20 -> x8, local copies, waits for them, and re-layouts: 3.12 us -> 2.19 us
  transfers between devices with their start and end apart: 5 -> 4, of which waited for: 4 -> 3; matrix products, arithmetic and copies ran while one was open for 0% -> 0% of each run, Pallas kernels for 40% -> 30%
where the time goes in v3:
time: 121 us; the launch traced here: 120 us
  Pallas kernels  51.2 us (42%)
  waiting for transfers between devices  35.6 us (29%)
  starting transfers between devices  28.1 us (23%)
  local copies, waits for them, and re-layouts  3.6 us (3%)
    pallas_call x5, Pallas kernels, called(): pl.pallas_call(kernel, out_shape=outs, in_specs=[whole if spec is None el...  37.9 us
    all_to_all x1, waiting for transfers between devices, per_device(): earlier = lax.all_to_all(earlier, 'dp', 0, 0)  17.6 us
    pallas_call x1, Pallas kernels, turn(): pl.pallas_call(turn_kernel, grid=(layers, 9), out_shape=jax.ShapeDtypeStr...  13.3 us
    all_to_all x1, starting transfers between devices, per_device(): later = lax.all_to_all(later, 'dp', 0, 0)  10.1 us
    all_to_all x1, waiting for transfers between devices, spread(): lax.all_to_all(jnp.broadcast_to(value[None], (lax.axis_size(axis),) + val...  9.56 us
    all_to_all x1, waiting for transfers between devices, per_device(): every = lax.all_to_all(every, 'space', 0, 0)  8.45 us
    all_to_all x1, starting transfers between devices, per_device(): earlier = lax.all_to_all(earlier, 'dp', 0, 0)  8.41 us
    all_to_all x1, starting transfers between devices, spread(): lax.all_to_all(jnp.broadcast_to(value[None], (lax.axis_size(axis),) + val...  6.03 us
  transfers between devices with their start and end apart: 4, of which 3 were waited for; matrix products, arithmetic and copies ran while one was open for 0% of the time, Pallas kernels for 30%

profile of v3, /device:TPU:2, one launch (start us, length us, event | category | flops | bytes accessed | tf_op | source)
XLA Modules:
  0.0 120.2 jit_solution(747430246428385208)
XLA Ops:
  0.6 1.0 pad_maximum_fusion
  1.6 1.4 %broadcast_in_dim.2 = bf16[8,2,8,24,256]{4,3,2,1,0:T(8,128)(2,1)} broadcast(bf16[2,8,24,256]{3,2,1,0:T(8,128)(2,1)S(1)} %pad_maximum_fusion), dimensions={1,2,3,4} | broadcast | bytes 1769472 | tf_op jit(solution)/shard_map/broadcast_in_dim | solution.py:503
  3.0 6.0 %all-to-all-start = ((bf16[8,2,8,24,256]{4,3,2,1,0:T(8,128)(2,1)}), bf16[8,2,8,24,256]{4,3,2,1,0:T(8,128)(2,1)S(1)}, u32[]{:S(2)}, u32[]{:S(2)}) async-start(bf16[8,2,8,24,256]{4,3,2,1,0:T(8,128)(2,1)} %broadcast_in_dim.2), calls=%async_computation | async-start | bytes 3145728 | tf_op jit(solution)/shard_map/all_to_all | solution.py:503
  9.0 13.3 %shard_map.118.turned = bf16[2,6912,256]{2,1,0:T(8,128)(2,1)} custom-call(bf16[2,6912,256]{2,1,0:T(8,128)(2,1)} %weights.5), custom_call_target="tpu_custom_call" | custom-call | bytes 14155776 | tf_op jit(solution)/shard_map/pallas_call | solution.py:479
  22.3 9.6 %all-to-all-done.raw = bf16[8,2,8,24,256]{4,3,2,1,0:T(8,128)(2,1)S(1)} async-done(((bf16[8,2,8,24,256]{4,3,2,1,0:T(8,128)(2,1)}), bf16[8,2,8,24,256]{4,3,2,1,0:T(8,128)(2,1)S(1)}, u32[]{:S(2)}, u32[]{:S(2)}) %all-to-all-start) | async-done | bytes 1572896 | tf_op jit(solution)/shard_map/all_to_all | solution.py:503
  31.9 0.0 copy-start.3
  31.9 1.2 %copy-done.3 = bf16[8,2,8,24,256]{4,3,2,1,0:T(8,128)(2,1)} copy-done((bf16[8,2,8,24,256]{4,3,2,1,0:T(8,128)(2,1)}, bf16[8,2,8,24,256]{4,3,2,1,0:T(8,128)(2,1)S(1)}, u32[]{:S(2)}) %copy-start.3) | copy-done | bytes 1572888
  33.1 12.7 %shard_map.119 = (bf16[1536,256]{1,0:T(8,128)(2,1)}, bf16[1536,256]{1,0:T(8,128)(2,1)}, bf16[1536,256]{1,0:T(8,128)(2,1)}, bf16[32,32,256]{2,1,0:T(8,128)(2,1)}) custom-call(s32[1]{0:T(128)} %bitcast.place, bf16[8,2,8,24,256]{4,3,2,1,0:T(8,128)(2,1)} %copy-done.3, bf16[2,6912,256]{2,1,0:T(8,128)(2,1)} %weights.5, f32[2,256]{1,0:T(2,128)} %gains.3, ...), custom_call_target="tpu_custom_call" | custom-call | flops 5435817984 | bytes 11538436 | tf_op jit(solution)/shard_map/pallas_call | solution.py:403
  45.9 10.1 %all-to-all-start.1 = ((bf16[32,32,256]{2,1,0:T(8,128)(2,1)}), bf16[32,32,256]{2,1,0:T(8,128)(2,1)S(1)}, u32[]{:S(2)}, u32[]{:S(2)}) async-start(bf16[32,32,256]{2,1,0:T(8,128)(2,1)} %get-tuple-element.21), calls=%async_computation.1 | async-start | bytes 1048576 | tf_op jit(solution)/shard_map/all_to_all | solution.py:518
  56.0 17.8 %shard_map.121 = (f32[8,24,256]{2,1,0:T(8,128)}, bf16[32,32,256]{2,1,0:T(8,128)(2,1)}) custom-call(s32[1]{0:T(128)} %bitcast.place, bf16[8,2,8,24,256]{4,3,2,1,0:T(8,128)(2,1)} %copy-done.3, bf16[2,6912,256]{2,1,0:T(8,128)(2,1)} %shard_map.118.turned, bf16[1536,256]{1,0:T(8,128)(2,1)} %get-tuple-element.23.h_one, bf16[1536,256]{1,0:T(8,128)(2,1)} %get-tuple-element.24.a_one, ...), custom_call_target="tpu_custom_call" | custom-call | flops 5435817984 | bytes 10948612 | tf_op jit(solution)/shard_map/pallas_call | solution.py:403
  73.7 0.0 copy-start
  73.8 0.0 copy-start.1
  73.8 0.0 all-to-all-done.1
  73.8 8.4 %all-to-all-start.2 = ((bf16[32,32,256]{2,1,0:T(8,128)(2,1)}), bf16[32,32,256]{2,1,0:T(8,128)(2,1)S(1)}, u32[]{:S(2)}, u32[]{:S(2)}) async-start(bf16[32,32,256]{2,1,0:T(8,128)(2,1)} %get-tuple-element.25), calls=%async_computation.2 | async-start | bytes 1048576 | tf_op jit(solution)/shard_map/all_to_all | solution.py:520
  82.2 0.1 convert_reduce_fusion
  82.3 17.6 %all-to-all-done.2.earlier = bf16[32,32,256]{2,1,0:T(8,128)(2,1)S(1)} async-done(((bf16[32,32,256]{2,1,0:T(8,128)(2,1)}), bf16[32,32,256]{2,1,0:T(8,128)(2,1)S(1)}, u32[]{:S(2)}, u32[]{:S(2)}) %all-to-all-start.2) | async-done | bytes 524320 | tf_op jit(solution)/shard_map/all_to_all | solution.py:520
  99.9 0.0 copy-start.2
  99.9 0.9 copy-done.2
  100.8 1.0 shard_map.122
  101.8 3.5 %all-to-all-start.3 = ((f32[8,88,256]{2,1,0:T(8,128)}), f32[8,88,256]{2,1,0:T(8,128)S(1)}, u32[]{:S(2)}, u32[]{:S(2)}) async-start(f32[8,88,256]{2,1,0:T(8,128)} %shard_map.122), calls=%async_computation.3 | async-start | bytes 1441792 | tf_op jit(solution)/shard_map/all_to_all | solution.py:525
  105.3 4.9 %shard_map.120 = bf16[8,24,256]{2,1,0:T(8,128)(2,1)} custom-call(s32[1]{0:T(128)} %bitcast.place, bf16[1536,256]{1,0:T(8,128)(2,1)} %get-tuple-element.20.a_two, bf16[2,6912,256]{2,1,0:T(8,128)(2,1)} %weights.5, bf16[8,24,256]{2,1,0:T(8,128)(2,1)} %bitcast.7), custom_call_target="tpu_custom_call" | custom-call | flops 905969664 | bytes 8060932 | tf_op jit(solution)/shard_map/pallas_call | solution.py:403
  110.2 8.4 %all-to-all-done.3.every = f32[8,88,256]{2,1,0:T(8,128)S(1)} async-done(((f32[8,88,256]{2,1,0:T(8,128)}), f32[8,88,256]{2,1,0:T(8,128)S(1)}, u32[]{:S(2)}, u32[]{:S(2)}) %all-to-all-start.3) | async-done | bytes 720928 | tf_op jit(solution)/shard_map/all_to_all | solution.py:525
  118.7 0.0 copy-done
  118.7 0.0 copy-done.1
  118.7 1.5 %shard_map.123 = (f32[2,216,256]{2,1,0:T(8,128)}, f32[2,216,256]{2,1,0:T(8,128)}, f32[2,216,256]{2,1,0:T(8,128)}, f32[4,256]{1,0:T(4,128)}, bf16[8,24,256]{2,1,0:T(8,128)(2,1)}) custom-call(f32[8,88,256]{2,1,0:T(8,128)S(1)} %all-to-all-done.3.every, f32[2,216,256]{2,1,0:T(8,128)S(1)} %copy-done, f32[2,216,256]{2,1,0:T(8,128)S(1)} %copy-done.1), custom_call_target="tpu_custom_call" | custom-call | bytes 3035136 | tf_op jit(solution)/shard_map/pallas_call | solution.py:403
  (1 shorter events, 0.0 us)
Async XLA Ops:
  3.0 28.9 %all-to-all-start = ((bf16[8,2,8,24,256]{4,3,2,1,0:T(8,128)(2,1)}), bf16[8,2,8,24,256]{4,3,2,1,0:T(8,128)(2,1)S(1)}, u32[]{:S(2)}, u32[]{:S(2)}) async-start(bf16[8,2,8,24,256]{4,3,2,1,0:T(8,128)(2,1)} %broadcast_in_dim.2), calls=%async_computation | async-start | bytes 3145728 | tf_op jit(solution)/shard_map/all_to_all | solution.py:503
  31.9 1.2 %copy-start.3 = (bf16[8,2,8,24,256]{4,3,2,1,0:T(8,128)(2,1)}, bf16[8,2,8,24,256]{4,3,2,1,0:T(8,128)(2,1)S(1)}, u32[]{:S(2)}) copy-start(bf16[8,2,8,24,256]{4,3,2,1,0:T(8,128)(2,1)S(1)} %all-to-all-done.raw) | copy-start | bytes 4718596
  45.9 27.9 %all-to-all-start.1 = ((bf16[32,32,256]{2,1,0:T(8,128)(2,1)}), bf16[32,32,256]{2,1,0:T(8,128)(2,1)S(1)}, u32[]{:S(2)}, u32[]{:S(2)}) async-start(bf16[32,32,256]{2,1,0:T(8,128)(2,1)} %get-tuple-element.21), calls=%async_computation.1 | async-start | bytes 1048576 | tf_op jit(solution)/shard_map/all_to_all | solution.py:518
  73.7 45.0 %copy-start = (f32[2,216,256]{2,1,0:T(8,128)S(1)}, f32[2,216,256]{2,1,0:T(8,128)}, u32[]{:S(2)}) copy-start(f32[2,216,256]{2,1,0:T(8,128)} %moment.1) | copy-start | bytes 1327108
  73.8 44.9 %copy-start.1 = (f32[2,216,256]{2,1,0:T(8,128)S(1)}, f32[2,216,256]{2,1,0:T(8,128)}, u32[]{:S(2)}) copy-start(f32[2,216,256]{2,1,0:T(8,128)} %second.1) | copy-start | bytes 1327108
  73.8 26.1 %all-to-all-start.2 = ((bf16[32,32,256]{2,1,0:T(8,128)(2,1)}), bf16[32,32,256]{2,1,0:T(8,128)(2,1)S(1)}, u32[]{:S(2)}, u32[]{:S(2)}) async-start(bf16[32,32,256]{2,1,0:T(8,128)(2,1)} %get-tuple-element.25), calls=%async_computation.2 | async-start | bytes 1048576 | tf_op jit(solution)/shard_map/all_to_all | solution.py:520
  99.9 0.9 copy-start.2
  101.8 16.9 %all-to-all-start.3 = ((f32[8,88,256]{2,1,0:T(8,128)}), f32[8,88,256]{2,1,0:T(8,128)S(1)}, u32[]{:S(2)}, u32[]{:S(2)}) async-start(f32[8,88,256]{2,1,0:T(8,128)} %shard_map.122), calls=%async_computation.3 | async-start | bytes 1441792 | tf_op jit(solution)/shard_map/all_to_all | solution.py:525

commit v4 on v3

--- a/solution.py
+++ b/solution.py
@@ -6,6 +6,7 @@
 from jax import lax
 from jax.experimental import pallas as pl
 from jax.experimental.pallas import tpu as pltpu
+from jax.sharding import Mesh
 from jax.sharding import PartitionSpec as P
 
 GROUPS = 32
@@ -169,9 +170,10 @@
         put_frame(d_h1, t, factor * (d_out * gains[1:2, :] - one - normed * two))
 
 
-def grad_part(place, values, grads, extra, out, long, block, total):
+def grad_part(place, values, grads, extra, out, part_number, long, block, total):
     frames_size, chans = values.shape
-    owners, tall, _ = out.shape
+    cores, pairs, _, _ = out.shape
+    owners = cores * pairs
     size, outs = (long.shape[0] - frames_size) // 2, total.shape[0] // 27
     frames = frames_size // size
     long[0:size, :] = values[0:size, :]
@@ -216,7 +218,7 @@
         one = rolled(one, -start, 1)[:, :chans]
         if extra is not None:
             one = jnp.where(lane < owned, one, extra[...])
-        out[d] = one.astype(jnp.bfloat16)
+        out[d % cores, d // cores, part_number * outs : (part_number + 1) * outs, :] = one.astype(jnp.bfloat16)
 
 
 def halves(value):
@@ -299,35 +301,31 @@
     extra[...] = jnp.concatenate(pieces, 0) + to_spare(0.5 * mine, owned + 32, 8)
 
 
-def first_kernel(place, raw, weights, gains, shifts, a_one, h_one, a_two, out, nine, weight, sem, long, block, total):
+def whole_kernel(place, raw, weights, turned, gains, shifts, a_two, grad, out, nine, straight, back_one, back_two, sems, a_one, h_one, d_h1, d_act, own_act, sums_two, extra, long, block, total):
     raw_lat, raw_cot = raw.at[:, 0], raw.at[:, 1]
-    copy = pltpu.make_async_copy(weights.at[0], weight, sem)
-    copy.start()
-    ahead_part(raw_lat, gains, shifts, a_one, h_one, a_two, nine, weight, copy)
-    grad_part(place, a_two, raw_cot, None, out, long, block, total)
-
-
-def second_kernel(place, raw, turned, h_one, a_one, gains, shifts, grad, out, nine, weight, sem, long, block, total, other, other_sem, d_act, own_act, d_h1, sums_two, extra):
-    raw_lat, raw_cot = raw.at[:, 0], raw.at[:, 1]
-    copy = pltpu.make_async_copy(turned.at[1], weight, sem)
-    copy.start()
-    other_copy = pltpu.make_async_copy(turned.at[0], other, other_sem)
-    other_copy.start()
-    back_part(raw_cot, h_one, gains, shifts, d_h1, sums_two, nine, d_act, weight, copy)
-    own_part(place, d_h1, raw_lat, raw_cot, gains, shifts, sums_two, grad, extra, nine, own_act, other, other_copy)
-    grad_part(place, a_one, d_h1, extra, out, long, block, total)
-
-
-def sum_kernel(later, earlier, grad, out, *, clips):
-    total = earlier[0].astype(jnp.float32)
-    for d in range(1, clips):
-        total = total + earlier[d].astype(jnp.float32)
+    copies = [
+        pltpu.make_async_copy(weights.at[0], straight, sems.at[0]),
+        pltpu.make_async_copy(turned.at[1], back_two, sems.at[1]),
+        pltpu.make_async_copy(turned.at[0], back_one, sems.at[2]),
+    ]
+    for copy in copies:
+        copy.start()
+    ahead_part(raw_lat, gains, shifts, a_one, h_one, a_two, nine, straight, copies[0])
+    grad_part(place, a_two, raw_cot, None, out, 0, long, block, total)
+    back_part(raw_cot, h_one, gains, shifts, d_h1, sums_two, nine, d_act, back_two, copies[1])
+    own_part(place, d_h1, raw_lat, raw_cot, gains, shifts, sums_two, grad, extra, nine, own_act, back_one, copies[2])
+    grad_part(place, a_one, d_h1, extra, out, 1, long, block, total)
+
+
+def sum_kernel(pieces, grad, out, *, clips):
+    total = pieces[0].astype(jnp.float32)
+    for d in range(1, pieces.shape[0]):
+        total = total + pieces[d].astype(jnp.float32)
     total = total / clips
     rows = total.shape[0]
     for p in range(out.shape[0]):
-        out[p, 0:rows, :] = later[...]
-        out[p, rows : 2 * rows, :] = total
-        out[p, 2 * rows :, :] = grad[p]
+        out[p, 0:rows, :] = total
+        out[p, rows:, :] = grad[p]
 
 
 def adam_kernel(every, moment, second, new_moment, new_second, direction, vector, grad_input):
@@ -423,54 +421,43 @@
     return pl.BlockSpec(memory_space=pl.ANY)
 
 
-def scratches(raw, weights, width):
+def whole(place, raw, weights, turned, gains, shifts, width, clips, cores):
     blocks, _, frames, flat, chans = raw.shape
     size = blocks * flat
     places = frames * size
-    return [
-        pltpu.VMEM((places + 2 * size, 9 * chans), jnp.bfloat16),
-        *held(weights),
-        pltpu.VMEM((places + 2 * size, chans), jnp.bfloat16),
-        pltpu.VMEM((places, -(-9 * width // 128) * 128), jnp.bfloat16),
-        pltpu.VMEM((27 * width, chans), jnp.float32),
+    f32, bf16 = jnp.float32, jnp.bfloat16
+    outs = [
+        jax.ShapeDtypeStruct((places, chans), bf16),
+        jax.ShapeDtypeStruct((blocks, flat, chans), f32),
+        jax.ShapeDtypeStruct((cores, clips // cores, 2 * width, chans), bf16),
     ]
-
-
-def first_part(place, raw, weights, gains, shifts, width, clips):
-    blocks, _, frames, flat, chans = raw.shape
-    places = blocks * frames * flat
-    shape = jax.ShapeDtypeStruct((places, chans), jnp.bfloat16)
-    outs = [shape, shape, shape, jax.ShapeDtypeStruct((clips, width, chans), jnp.bfloat16)]
-    args = (place, raw, weights, gains, shifts)
-    specs = [small(), None, away(), None, None]
-    return called(first_kernel, outs, scratches(raw, weights, width), args, specs, places * weights.size, 58)
-
-
-def second_part(place, raw, turned, h_one, a_one, gains, shifts, width, clips):
-    blocks, _, frames, flat, chans = raw.shape
-    size = blocks * flat
-    places = frames * size
-    outs = [
-        jax.ShapeDtypeStruct((blocks, flat, chans), jnp.float32),
-        jax.ShapeDtypeStruct((clips, width, chans), jnp.bfloat16),
+    layer = pltpu.VMEM(weights.shape[1:], bf16)
+    scratch = [
+        pltpu.VMEM((places + 2 * size, 9 * chans), bf16),
+        layer,
+        layer,
+        layer,
+        pltpu.SemaphoreType.DMA((3,)),
+        pltpu.VMEM((places, chans), bf16),
+        pltpu.VMEM((places, chans), bf16),
+        pltpu.VMEM((places, chans), bf16),
+        pltpu.VMEM((places, chans), f32),
+        pltpu.VMEM((size, chans), f32),
+        pltpu.VMEM((2, 8, chans), f32),
+        pltpu.VMEM((32, chans), f32),
+        pltpu.VMEM((places + 2 * size, chans), bf16),
+        pltpu.VMEM((places, -(-9 * width // 128) * 128), bf16),
+        pltpu.VMEM((27 * width, chans), f32),
     ]
-    scratch = scratches(raw, turned, width) + [
-        *held(turned),
-        pltpu.VMEM((places, chans), jnp.float32),
-        pltpu.VMEM((size, chans), jnp.float32),
-        pltpu.VMEM((places, chans), jnp.bfloat16),
-        pltpu.VMEM((2, 8, chans), jnp.float32),
-        pltpu.VMEM((32, chans), jnp.float32),
-    ]
-    args = (place, raw, turned, h_one, a_one, gains, shifts)
-    specs = [small(), None, away(), None, None, None, None]
-    return called(second_kernel, outs, scratch, args, specs, places * turned.size, 58)
-
-
-def gathered(later, earlier, grads, clips):
+    args = (place, raw, weights, turned, gains, shifts)
+    specs = [small(), None, away(), away(), None, None]
+    return called(whole_kernel, outs, scratch, args, specs, 2 * places * weights.size, 58)
+
+
+def gathered(pieces, grads, clips):
     parts, flat, chans = grads.shape
-    outs = [jax.ShapeDtypeStruct((parts, 2 * later.shape[0] + flat, chans), jnp.float32)]
-    return called(functools.partial(sum_kernel, clips=clips), outs, [], (later, earlier, grads))[0]
+    outs = [jax.ShapeDtypeStruct((parts, pieces.shape[1] + flat, chans), jnp.float32)]
+    return called(functools.partial(sum_kernel, clips=clips), outs, [], (pieces, grads))[0]
 
 
 def turn(weights):
@@ -505,7 +492,8 @@
 
 def per_device(latents, cotangent, conv_weights, gains, shifts, moment, second):
     frames, rows, cols, chans = latents.shape[1:]
-    clips, parts = lax.axis_size("dp"), lax.axis_size("space")
+    cores, parts = lax.axis_size("core"), lax.axis_size("space")
+    clips = lax.axis_size("pair") * cores
     me = lax.axis_index("space")
     place = me.astype(jnp.int32).reshape(1)
     width = chans // parts
@@ -514,14 +502,13 @@
     both = jnp.stack([latent, cotangent[0].reshape(latent.shape)])
     raw, turned = lax.optimization_barrier((spread(both, "space"), turn(conv_weights)))
 
-    a_one, h_one, a_two, later = first_part(place, raw, conv_weights, gains, shifts, width, clips)
-    later = lax.all_to_all(later, "dp", 0, 0)
-    grads, earlier = second_part(place, raw, turned, h_one, a_one, gains, shifts, width, clips)
-    earlier = lax.all_to_all(earlier, "dp", 0, 0)
+    a_two, grads, pieces = whole(place, raw, conv_weights, turned, gains, shifts, width, clips, cores)
+    pieces = lax.all_to_all(pieces, "core", 0, 0)
+    pieces = jnp.sum(pieces.astype(f32), 0).astype(bf16)
+    pieces = lax.all_to_all(pieces, "pair", 0, 0)
     decoded = decode(place, a_two, conv_weights, latent)
 
-    later = jnp.sum(later.astype(f32), 0) / clips
-    every = gathered(later, earlier, grads, clips)
+    every = gathered(pieces, grads, clips)
     every = lax.all_to_all(every, "space", 0, 0)
     shape = jax.ShapeDtypeStruct(moment.shape, f32)
     outs = [shape, shape, shape, jax.ShapeDtypeStruct((4, chans), f32)]
@@ -533,25 +520,28 @@
 
 
 def solution(mesh):
+    clips, parts = mesh.devices.shape
+    mesh = Mesh(mesh.devices.reshape(clips // 2, 2, parts), ("pair", "core", "space"))
+    dp = ("pair", "core")
     placed = (
-        P("dp", None, "space", None, None),
-        P("dp", None, "space", None, None),
+        P(dp, None, "space", None, None),
+        P(dp, None, "space", None, None),
         P(),
         P(),
         P(),
-        P(None, "dp", None),
-        P(None, "dp", None),
+        P(None, dp, None),
+        P(None, dp, None),
     )
     return jax.shard_map(
         per_device,
         mesh=mesh,
         in_specs=placed,
         out_specs=(
-            P("dp", None, "space", None, None),
-            P("dp", None, "space", None, None),
-            P(None, "dp", None),
-            P(None, "dp", None),
-            P(None, "dp", None),
+            P(dp, None, "space", None, None),
+            P(dp, None, "space", None, None),
+            P(None, dp, None),
+            P(None, dp, None),
+            P(None, dp, None),
             P(),
         ),
         check_vma=False,

time: 121 us -> 111 us (0.917)
  blocking collectives: 0 us -> 32.1 us
  waiting for transfers between devices: 35.6 us -> 16.1 us
  starting transfers between devices: 28.1 us -> 9.57 us
  Pallas kernels: 51.2 us -> 46.8 us
    all_to_all x0 -> x2, blocking collectives: none -> 32.1 us  [the longest x1 26.4 us: per_device(): pieces = lax.all_to_all(pieces, 'pair', 0, 0)]
    all_to_all x2 -> x0, starting transfers between devices: 18.5 us -> none  [the longest x1 10.1 us: per_device(): later = lax.all_to_all(later, 'dp', 0, 0)]
    all_to_all x2 -> x0, waiting for transfers between devices: 17.6 us -> none  [the longest x1 17.6 us: per_device(): earlier = lax.all_to_all(earlier, 'dp', 0, 0)]
    pallas_call x5 -> x4, Pallas kernels: 37.9 us -> 33.5 us  [called(): pl.pallas_call(kernel, out_shape=outs, in_specs=[whole if spec is None el...]
    all_to_all x1, waiting for transfers between devices: 8.45 us -> 6.59 us  [per_device(): every = lax.all_to_all(every, 'space', 0, 0)]
  transfers between devices with their start and end apart: 4 -> 2, of which waited for: 3 -> 2; matrix products, arithmetic and copies ran while one was open for 0% -> 0% of each run, Pallas kernels for 30% -> 17%
where the time goes in v4:
time: 111 us; the launch traced here: 110 us
  Pallas kernels  46.8 us (42%)
  blocking collectives  32.1 us (29%)
  waiting for transfers between devices  16.1 us (15%)
  starting transfers between devices  9.57 us (9%)
  local copies, waits for them, and re-layouts  3.53 us (3%)
  other arithmetic  1.26 us (1%)
    pallas_call x4, Pallas kernels, called(): pl.pallas_call(kernel, out_shape=outs, in_specs=[whole if spec is None el...  33.5 us
    all_to_all x1, blocking collectives, per_device(): pieces = lax.all_to_all(pieces, 'pair', 0, 0)  26.4 us
    pallas_call x1, Pallas kernels, turn(): pl.pallas_call(turn_kernel, grid=(layers, 9), out_shape=jax.ShapeDtypeStr...  13.3 us
    all_to_all x1, waiting for transfers between devices, spread(): lax.all_to_all(jnp.broadcast_to(value[None], (lax.axis_size(axis),) + val...  9.55 us
    all_to_all x1, waiting for transfers between devices, per_device(): every = lax.all_to_all(every, 'space', 0, 0)  6.59 us
    all_to_all x1, starting transfers between devices, spread(): lax.all_to_all(jnp.broadcast_to(value[None], (lax.axis_size(axis),) + val...  6.03 us
    all_to_all x1, blocking collectives, per_device(): pieces = lax.all_to_all(pieces, 'core', 0, 0)  5.69 us
    all_to_all x1, starting transfers between devices, per_device(): every = lax.all_to_all(every, 'space', 0, 0)  3.54 us
  transfers between devices with their start and end apart: 2, of which 2 were waited for; matrix products, arithmetic and copies ran while one was open for 0% of the time, Pallas kernels for 17%

profile of v4, /device:TPU:2, one launch (start us, length us, event | category | flops | bytes accessed | tf_op | source)
XLA Modules:
  0.0 110.1 jit_solution(7909578392276785390)
XLA Ops:
  0.6 1.0 pad_maximum_fusion
  1.6 1.4 %broadcast_in_dim.2 = bf16[8,2,8,24,256]{4,3,2,1,0:T(8,128)(2,1)} broadcast(bf16[2,8,24,256]{3,2,1,0:T(8,128)(2,1)S(1)} %pad_maximum_fusion), dimensions={1,2,3,4} | broadcast | bytes 1769472 | tf_op jit(solution)/shard_map/broadcast_in_dim | solution.py:490
  3.0 6.0 %all-to-all-start = ((bf16[8,2,8,24,256]{4,3,2,1,0:T(8,128)(2,1)}), bf16[8,2,8,24,256]{4,3,2,1,0:T(8,128)(2,1)S(1)}, u32[]{:S(2)}, u32[]{:S(2)}) async-start(bf16[8,2,8,24,256]{4,3,2,1,0:T(8,128)(2,1)} %broadcast_in_dim.2), calls=%async_computation | async-start | bytes 3145728 | tf_op jit(solution)/shard_map/all_to_all | solution.py:490
  9.0 13.3 %shard_map.118.turned = bf16[2,6912,256]{2,1,0:T(8,128)(2,1)} custom-call(bf16[2,6912,256]{2,1,0:T(8,128)(2,1)} %weights.5), custom_call_target="tpu_custom_call" | custom-call | bytes 14155776 | tf_op jit(solution)/shard_map/pallas_call | solution.py:466
  22.3 9.5 %all-to-all-done.raw = bf16[8,2,8,24,256]{4,3,2,1,0:T(8,128)(2,1)S(1)} async-done(((bf16[8,2,8,24,256]{4,3,2,1,0:T(8,128)(2,1)}), bf16[8,2,8,24,256]{4,3,2,1,0:T(8,128)(2,1)S(1)}, u32[]{:S(2)}, u32[]{:S(2)}) %all-to-all-start) | async-done | bytes 1572896 | tf_op jit(solution)/shard_map/all_to_all | solution.py:490
  31.9 0.0 copy-start.3
  31.9 1.2 %copy-done.3 = bf16[8,2,8,24,256]{4,3,2,1,0:T(8,128)(2,1)} copy-done((bf16[8,2,8,24,256]{4,3,2,1,0:T(8,128)(2,1)}, bf16[8,2,8,24,256]{4,3,2,1,0:T(8,128)(2,1)S(1)}, u32[]{:S(2)}) %copy-start.3) | copy-done | bytes 1572888
  33.1 26.1 %shard_map.119 = (bf16[1536,256]{1,0:T(8,128)(2,1)}, f32[8,24,256]{2,1,0:T(8,128)}, bf16[2,16,64,256]{3,2,1,0:T(8,128)(2,1)}) custom-call(s32[1]{0:T(128)} %bitcast.place, bf16[8,2,8,24,256]{4,3,2,1,0:T(8,128)(2,1)} %copy-done.3, bf16[2,6912,256]{2,1,0:T(8,128)(2,1)} %weights.5, bf16[2,6912,256]{2,1,0:T(8,128)(2,1)} %shard_map.118.turned, f32[2,256]{1,0:T(2,128)} %gains.1, ...), custom_call_target="tpu_custom_call" | custom-call | flops 10871635968 | bytes 17764356 | tf_op jit(solution)/shard_map/pallas_call | solution.py:401
  59.2 5.7 %all_to_all.20 = bf16[2,16,64,256]{3,2,1,0:T(8,128)(2,1)S(1)} all-to-all(bf16[2,16,64,256]{3,2,1,0:T(8,128)(2,1)} %get-tuple-element.19), channel_id=1, replica_groups=mesh['pair'=16,'core'=2,'space'=8] {'core'}, dimensions={0} | all-to-all | bytes 2097152 | tf_op jit(solution)/shard_map/all_to_all | solution.py:506
  64.9 0.0 copy-start
  64.9 0.0 copy-start.1
  64.9 0.3 reduce_sum.12
  65.2 26.4 %all_to_all.21.pieces = bf16[16,64,256]{2,1,0:T(8,128)(2,1)S(1)} all-to-all(bf16[16,64,256]{2,1,0:T(8,128)(2,1)S(1)} %reduce_sum.12), channel_id=1, replica_groups=mesh['pair'=16,'core'=2,'space'=8] {'pair'}, dimensions={0} | all-to-all | bytes 1048576 | tf_op jit(solution)/shard_map/all_to_all | solution.py:508
  91.7 0.0 copy-start.2
  91.7 0.9 copy-done.2
  92.6 1.0 shard_map.121
  93.5 3.5 %all-to-all-start.3 = ((f32[8,88,256]{2,1,0:T(8,128)}), f32[8,88,256]{2,1,0:T(8,128)S(1)}, u32[]{:S(2)}, u32[]{:S(2)}) async-start(f32[8,88,256]{2,1,0:T(8,128)} %shard_map.121), calls=%async_computation.3 | async-start | bytes 1441792 | tf_op jit(solution)/shard_map/all_to_all | solution.py:512
  97.1 4.9 %shard_map.120 = bf16[8,24,256]{2,1,0:T(8,128)(2,1)} custom-call(s32[1]{0:T(128)} %bitcast.place, bf16[1536,256]{1,0:T(8,128)(2,1)} %get-tuple-element.18.a_two, bf16[2,6912,256]{2,1,0:T(8,128)(2,1)} %weights.5, bf16[8,24,256]{2,1,0:T(8,128)(2,1)} %bitcast.7), custom_call_target="tpu_custom_call" | custom-call | flops 905969664 | bytes 8060932 | tf_op jit(solution)/shard_map/pallas_call | solution.py:401
  102.0 6.6 %all-to-all-done.3.every = f32[8,88,256]{2,1,0:T(8,128)S(1)} async-done(((f32[8,88,256]{2,1,0:T(8,128)}), f32[8,88,256]{2,1,0:T(8,128)S(1)}, u32[]{:S(2)}, u32[]{:S(2)}) %all-to-all-start.3) | async-done | bytes 720928 | tf_op jit(solution)/shard_map/all_to_all | solution.py:512
  108.6 0.0 copy-done
  108.6 0.0 copy-done.1
  108.6 1.5 %shard_map.122 = (f32[2,216,256]{2,1,0:T(8,128)}, f32[2,216,256]{2,1,0:T(8,128)}, f32[2,216,256]{2,1,0:T(8,128)}, f32[4,256]{1,0:T(4,128)}, bf16[8,24,256]{2,1,0:T(8,128)(2,1)}) custom-call(f32[8,88,256]{2,1,0:T(8,128)S(1)} %all-to-all-done.3.every, f32[2,216,256]{2,1,0:T(8,128)S(1)} %copy-done, f32[2,216,256]{2,1,0:T(8,128)S(1)} %copy-done.1), custom_call_target="tpu_custom_call" | custom-call | bytes 3035136 | tf_op jit(solution)/shard_map/pallas_call | solution.py:401
Async XLA Ops:
  3.0 28.9 %all-to-all-start = ((bf16[8,2,8,24,256]{4,3,2,1,0:T(8,128)(2,1)}), bf16[8,2,8,24,256]{4,3,2,1,0:T(8,128)(2,1)S(1)}, u32[]{:S(2)}, u32[]{:S(2)}) async-start(bf16[8,2,8,24,256]{4,3,2,1,0:T(8,128)(2,1)} %broadcast_in_dim.2), calls=%async_computation | async-start | bytes 3145728 | tf_op jit(solution)/shard_map/all_to_all | solution.py:490
  31.9 1.2 %copy-start.3 = (bf16[8,2,8,24,256]{4,3,2,1,0:T(8,128)(2,1)}, bf16[8,2,8,24,256]{4,3,2,1,0:T(8,128)(2,1)S(1)}, u32[]{:S(2)}) copy-start(bf16[8,2,8,24,256]{4,3,2,1,0:T(8,128)(2,1)S(1)} %all-to-all-done.raw) | copy-start | bytes 4718596
  64.9 43.7 %copy-start = (f32[2,216,256]{2,1,0:T(8,128)S(1)}, f32[2,216,256]{2,1,0:T(8,128)}, u32[]{:S(2)}) copy-start(f32[2,216,256]{2,1,0:T(8,128)} %moment.1) | copy-start | bytes 1327108
  64.9 43.7 %copy-start.1 = (f32[2,216,256]{2,1,0:T(8,128)S(1)}, f32[2,216,256]{2,1,0:T(8,128)}, u32[]{:S(2)}) copy-start(f32[2,216,256]{2,1,0:T(8,128)} %second.1) | copy-start | bytes 1327108
  91.7 0.9 copy-start.2
  93.5 15.0 %all-to-all-start.3 = ((f32[8,88,256]{2,1,0:T(8,128)}), f32[8,88,256]{2,1,0:T(8,128)S(1)}, u32[]{:S(2)}, u32[]{:S(2)}) async-start(f32[8,88,256]{2,1,0:T(8,128)} %shard_map.121), calls=%async_computation.3 | async-start | bytes 1441792 | tf_op jit(solution)/shard_map/all_to_all | solution.py:512

commit v5 on v4

--- a/solution.py
+++ b/solution.py
@@ -394,6 +394,12 @@
         decoded[t] = value.astype(jnp.bfloat16)
 
 
+def spread_kernel(latent, upstream, out):
+    for p in range(out.shape[0]):
+        out[p, 0] = latent[...]
+        out[p, 1] = upstream[...]
+
+
 def called(kernel, outs, scratch, args, specs=None, flops=0, limit=16):
     whole = pl.BlockSpec(memory_space=pltpu.VMEM)
     specs = specs or [whole] * len(args)
@@ -451,7 +457,7 @@
     ]
     args = (place, raw, weights, turned, gains, shifts)
     specs = [small(), None, away(), away(), None, None]
-    return called(whole_kernel, outs, scratch, args, specs, 2 * places * weights.size, 58)
+    return called(whole_kernel, outs, scratch, args, specs, 2 * places * weights.size, 44)
 
 
 def gathered(pieces, grads, clips):
@@ -483,11 +489,7 @@
         pltpu.VMEM(((frames + 2) * pitch, 9 * chans), jnp.bfloat16),
     ] + held(weights)
     args = (place, a_two, weights, latent)
-    return called(decode_kernel, outs, scratch, args, [small(), None, away(), None], frames * pitch * weights.size, 58)[0]
-
-
-def spread(value, axis):
-    return lax.all_to_all(jnp.broadcast_to(value[None], (lax.axis_size(axis),) + value.shape), axis, 0, 0)
+    return called(decode_kernel, outs, scratch, args, [small(), None, away(), None], frames * pitch * weights.size, 44)[0]
 
 
 def per_device(latents, cotangent, conv_weights, gains, shifts, moment, second):
@@ -499,8 +501,11 @@
     width = chans // parts
     f32, bf16 = jnp.float32, jnp.bfloat16
     latent = latents[0].reshape(frames, rows * cols, chans)
-    both = jnp.stack([latent, cotangent[0].reshape(latent.shape)])
-    raw, turned = lax.optimization_barrier((spread(both, "space"), turn(conv_weights)))
+    upstream = cotangent[0].reshape(latent.shape)
+    outs = [jax.ShapeDtypeStruct((parts, 2) + latent.shape, bf16)]
+    raw = called(spread_kernel, outs, [], (latent, upstream), limit=58)[0]
+    raw = lax.all_to_all(raw, "space", 0, 0)
+    raw, turned = lax.optimization_barrier((raw, turn(conv_weights)))
 
     a_two, grads, pieces = whole(place, raw, conv_weights, turned, gains, shifts, width, clips, cores)
     pieces = lax.all_to_all(pieces, "core", 0, 0)

time: 111 us -> 107 us (0.964)
  Pallas kernels: 46.8 us -> 43.8 us
    pallas_call x4 -> x5, Pallas kernels: 33.5 us -> 30.5 us  [called(): pl.pallas_call(kernel, out_shape=outs, in_specs=[whole if spec is None el...]
    broadcast_in_dim x1 -> x0, local copies, waits for them, and re-layouts: 1.38 us -> none  [spread(): jnp.broadcast_to(value[None], (lax.axis_size(axis),) + value.shape)]
    reduce_sum x1, other arithmetic: 0.3 us -> 1.54 us  [per_device(): pieces = jnp.sum(pieces.astype(f32), 0).astype(bf16)]
    unnamed x8 -> x12, local copies, waits for them, and re-layouts: 2.15 us -> 3.03 us
  transfers between devices with their start and end apart: 2 -> 2, of which waited for: 2 -> 2; matrix products, arithmetic and copies ran while one was open for 0% -> 0% of each run, Pallas kernels for 17% -> 15%
where the time goes in v5:
time: 107 us; the launch traced here: 106 us
  Pallas kernels  43.8 us (41%)
  blocking collectives  31.9 us (30%)
  waiting for transfers between devices  15.7 us (15%)
  starting transfers between devices  9.57 us (9%)
  local copies, waits for them, and re-layouts  3.03 us (3%)
  other arithmetic  1.54 us (1%)
    pallas_call x5, Pallas kernels, called(): pl.pallas_call(kernel, out_shape=outs, in_specs=[whole if spec is None el...  30.5 us
    all_to_all x1, blocking collectives, per_device(): pieces = lax.all_to_all(pieces, 'pair', 0, 0)  26.4 us
    pallas_call x1, Pallas kernels, turn(): pl.pallas_call(turn_kernel, grid=(layers, 9), out_shape=jax.ShapeDtypeStr...  13.3 us
    all_to_all x1, waiting for transfers between devices, per_device(): raw = lax.all_to_all(raw, 'space', 0, 0)  9.52 us
    all_to_all x1, waiting for transfers between devices, per_device(): every = lax.all_to_all(every, 'space', 0, 0)  6.16 us
    all_to_all x1, starting transfers between devices, per_device(): raw = lax.all_to_all(raw, 'space', 0, 0)  6.03 us
    all_to_all x1, blocking collectives, per_device(): pieces = lax.all_to_all(pieces, 'core', 0, 0)  5.5 us
    all_to_all x1, starting transfers between devices, per_device(): every = lax.all_to_all(every, 'space', 0, 0)  3.54 us
  transfers between devices with their start and end apart: 2, of which 2 were waited for; matrix products, arithmetic and copies ran while one was open for 0% of the time, Pallas kernels for 15%

profile of v5, /device:TPU:2, one launch (start us, length us, event | category | flops | bytes accessed | tf_op | source)
XLA Modules:
  0.0 106.3 jit_solution(12204959685589944020)
XLA Ops:
  0.6 2.3 %shard_map.118 = bf16[8,2,8,24,256]{4,3,2,1,0:T(8,128)(2,1)} custom-call(bf16[8,24,256]{2,1,0:T(8,128)(2,1)} %bitcast.5, bf16[8,24,256]{2,1,0:T(8,128)(2,1)} %bitcast.8), custom_call_target="tpu_custom_call" | custom-call | bytes 1769472 | tf_op jit(solution)/shard_map/pallas_call | solution.py:407
  2.9 6.0 %all-to-all-start = ((bf16[8,2,8,24,256]{4,3,2,1,0:T(8,128)(2,1)}), bf16[8,2,8,24,256]{4,3,2,1,0:T(8,128)(2,1)S(1)}, u32[]{:S(2)}, u32[]{:S(2)}) async-start(bf16[8,2,8,24,256]{4,3,2,1,0:T(8,128)(2,1)} %shard_map.118), calls=%async_computation | async-start | bytes 3145728 | tf_op jit(solution)/shard_map/all_to_all | solution.py:507
  8.9 0.0 copy-start.4
  8.9 0.0 copy-start.5
  9.0 13.3 %shard_map.119.turned = bf16[2,6912,256]{2,1,0:T(8,128)(2,1)} custom-call(bf16[2,6912,256]{2,1,0:T(8,128)(2,1)} %weights.5), custom_call_target="tpu_custom_call" | custom-call | bytes 14155776 | tf_op jit(solution)/shard_map/pallas_call | solution.py:472
  22.3 9.5 %all-to-all-done.raw = bf16[8,2,8,24,256]{4,3,2,1,0:T(8,128)(2,1)S(1)} async-done(((bf16[8,2,8,24,256]{4,3,2,1,0:T(8,128)(2,1)}), bf16[8,2,8,24,256]{4,3,2,1,0:T(8,128)(2,1)S(1)}, u32[]{:S(2)}, u32[]{:S(2)}) %all-to-all-start) | async-done | bytes 1572896 | tf_op jit(solution)/shard_map/all_to_all | solution.py:507
  31.8 0.0 copy-done.4
  31.8 0.0 copy-done.5
  31.8 23.5 %shard_map.120 = (bf16[1536,256]{1,0:T(8,128)(2,1)S(1)}, f32[8,24,256]{2,1,0:T(8,128)S(1)}, bf16[2,16,64,256]{3,2,1,0:T(8,128)(2,1)S(1)}) custom-call(s32[1]{0:T(128)} %bitcast.place, bf16[8,2,8,24,256]{4,3,2,1,0:T(8,128)(2,1)S(1)} %all-to-all-done.raw, bf16[2,6912,256]{2,1,0:T(8,128)(2,1)} %weights.5, bf16[2,6912,256]{2,1,0:T(8,128)(2,1)} %shard_map.119.turned, ...), custom_call_target="tpu_custom_call" | custom-call | flops 10871635968 | bytes 17764356 | tf_op jit(solution)/shard_map/pallas_call | solution.py:407
  55.3 0.0 copy-start.3
  55.3 5.5 %all_to_all.20 = bf16[2,16,64,256]{3,2,1,0:T(8,128)(2,1)} all-to-all(bf16[2,16,64,256]{3,2,1,0:T(8,128)(2,1)S(1)} %get-tuple-element.19), channel_id=1, replica_groups=mesh['pair'=16,'core'=2,'space'=8] {'core'}, dimensions={0} | all-to-all | bytes 2097152 | tf_op jit(solution)/shard_map/all_to_all | solution.py:511
  60.8 0.0 copy-start.1
  60.8 0.0 copy-start.2
  60.8 1.5 %reduce_sum.12 = bf16[16,64,256]{2,1,0:T(8,128)(2,1)S(1)} reduce(bf16[2,16,64,256]{3,2,1,0:T(8,128)(2,1)} %all_to_all.20, bf16[]{:T(256)} %constant.6.clone.1), dimensions={0}, to_apply=%region_0.0 | reduce | flops 262144 | bytes 1572866 | tf_op jit(solution)/shard_map/reduce_sum | solution.py:512
  62.3 26.4 %all_to_all.21.pieces = bf16[16,64,256]{2,1,0:T(8,128)(2,1)S(1)} all-to-all(bf16[16,64,256]{2,1,0:T(8,128)(2,1)S(1)} %reduce_sum.12), channel_id=1, replica_groups=mesh['pair'=16,'core'=2,'space'=8] {'pair'}, dimensions={0} | all-to-all | bytes 1048576 | tf_op jit(solution)/shard_map/all_to_all | solution.py:513
  88.8 1.0 shard_map.122
  89.7 3.5 %all-to-all-start.3 = ((f32[8,88,256]{2,1,0:T(8,128)}), f32[8,88,256]{2,1,0:T(8,128)S(1)}, u32[]{:S(2)}, u32[]{:S(2)}) async-start(f32[8,88,256]{2,1,0:T(8,128)} %shard_map.122), calls=%async_computation.3 | async-start | bytes 1441792 | tf_op jit(solution)/shard_map/all_to_all | solution.py:517
  93.3 0.0 copy-done.3
  93.3 0.0 copy-start
  93.3 3.0 %copy-done = bf16[2,6912,256]{2,1,0:T(8,128)(2,1)S(1)} copy-done((bf16[2,6912,256]{2,1,0:T(8,128)(2,1)S(1)}, bf16[2,6912,256]{2,1,0:T(8,128)(2,1)}, u32[]{:S(2)}) %copy-start) | copy-done | bytes 7077912
  96.3 2.3 %shard_map.121 = bf16[8,24,256]{2,1,0:T(8,128)(2,1)} custom-call(s32[1]{0:T(128)} %bitcast.place, bf16[1536,256]{1,0:T(8,128)(2,1)S(1)} %get-tuple-element.18.a_two, bf16[2,6912,256]{2,1,0:T(8,128)(2,1)S(1)} %copy-done, bf16[8,24,256]{2,1,0:T(8,128)(2,1)S(1)} %bitcast.6), custom_call_target="tpu_custom_call" | custom-call | flops 905969664 | bytes 8060932 | tf_op jit(solution)/shard_map/pallas_call | solution.py:407
  98.6 6.2 %all-to-all-done.3.every = f32[8,88,256]{2,1,0:T(8,128)S(1)} async-done(((f32[8,88,256]{2,1,0:T(8,128)}), f32[8,88,256]{2,1,0:T(8,128)S(1)}, u32[]{:S(2)}, u32[]{:S(2)}) %all-to-all-start.3) | async-done | bytes 720928 | tf_op jit(solution)/shard_map/all_to_all | solution.py:517
  104.8 0.0 copy-done.1
  104.8 0.0 copy-done.2
  104.8 1.5 %shard_map.123 = (f32[2,216,256]{2,1,0:T(8,128)}, f32[2,216,256]{2,1,0:T(8,128)}, f32[2,216,256]{2,1,0:T(8,128)}, f32[4,256]{1,0:T(4,128)}, bf16[8,24,256]{2,1,0:T(8,128)(2,1)}) custom-call(f32[8,88,256]{2,1,0:T(8,128)S(1)} %all-to-all-done.3.every, f32[2,216,256]{2,1,0:T(8,128)S(1)} %copy-done.1, f32[2,216,256]{2,1,0:T(8,128)S(1)} %copy-done.2), custom_call_target="tpu_custom_call" | custom-call | bytes 3035136 | tf_op jit(solution)/shard_map/pallas_call | solution.py:407
Async XLA Ops:
  2.9 28.9 %all-to-all-start = ((bf16[8,2,8,24,256]{4,3,2,1,0:T(8,128)(2,1)}), bf16[8,2,8,24,256]{4,3,2,1,0:T(8,128)(2,1)S(1)}, u32[]{:S(2)}, u32[]{:S(2)}) async-start(bf16[8,2,8,24,256]{4,3,2,1,0:T(8,128)(2,1)} %shard_map.118), calls=%async_computation | async-start | bytes 3145728 | tf_op jit(solution)/shard_map/all_to_all | solution.py:507
  8.9 22.9 %copy-start.4 = (f32[2,256]{1,0:T(2,128)S(1)}, f32[2,256]{1,0:T(2,128)}, u32[]{:S(2)}) copy-start(f32[2,256]{1,0:T(2,128)} %gains.1) | copy-start | bytes 6148
  8.9 22.9 %copy-start.5 = (f32[2,256]{1,0:T(2,128)S(1)}, f32[2,256]{1,0:T(2,128)}, u32[]{:S(2)}) copy-start(f32[2,256]{1,0:T(2,128)} %shifts.1) | copy-start | bytes 6148
  55.3 38.0 %copy-start.3 = (bf16[1,8,3,8,256]{4,3,2,1,0:T(8,128)(2,1)S(1)}, bf16[1,8,3,8,256]{4,3,2,1,0:T(8,128)(2,1)}, u32[]{:S(2)}) copy-start(bf16[1,8,3,8,256]{4,3,2,1,0:T(8,128)(2,1)} %param.7) | copy-start | bytes 294916
  60.8 44.0 %copy-start.1 = (f32[2,216,256]{2,1,0:T(8,128)S(1)}, f32[2,216,256]{2,1,0:T(8,128)}, u32[]{:S(2)}) copy-start(f32[2,216,256]{2,1,0:T(8,128)} %moment.1) | copy-start | bytes 1327108
  60.8 44.0 %copy-start.2 = (f32[2,216,256]{2,1,0:T(8,128)S(1)}, f32[2,216,256]{2,1,0:T(8,128)}, u32[]{:S(2)}) copy-start(f32[2,216,256]{2,1,0:T(8,128)} %second.1) | copy-start | bytes 1327108
  89.7 15.0 %all-to-all-start.3 = ((f32[8,88,256]{2,1,0:T(8,128)}), f32[8,88,256]{2,1,0:T(8,128)S(1)}, u32[]{:S(2)}, u32[]{:S(2)}) async-start(f32[8,88,256]{2,1,0:T(8,128)} %shard_map.122), calls=%async_computation.3 | async-start | bytes 1441792 | tf_op jit(solution)/shard_map/all_to_all | solution.py:517
  93.3 3.0 %copy-start = (bf16[2,6912,256]{2,1,0:T(8,128)(2,1)S(1)}, bf16[2,6912,256]{2,1,0:T(8,128)(2,1)}, u32[]{:S(2)}) copy-start(bf16[2,6912,256]{2,1,0:T(8,128)(2,1)} %weights.5) | copy-start | bytes 21233668

commit v6 on v5

--- a/solution.py
+++ b/solution.py
@@ -394,13 +394,23 @@
         decoded[t] = value.astype(jnp.bfloat16)
 
 
-def spread_kernel(latent, upstream, out):
+def spread_kernel(latent, upstream, out, sems):
+    copies = []
     for p in range(out.shape[0]):
-        out[p, 0] = latent[...]
-        out[p, 1] = upstream[...]
-
-
-def called(kernel, outs, scratch, args, specs=None, flops=0, limit=16):
+        copies.append(pltpu.make_async_copy(latent, out.at[p, 0], sems.at[p, 0]))
+        copies.append(pltpu.make_async_copy(upstream, out.at[p, 1], sems.at[p, 1]))
+    for copy in copies:
+        copy.start()
+    for copy in copies:
+        copy.wait()
+
+
+def pair_kernel(pieces, out):
+    for n in range(out.shape[0]):
+        out[n] = (pieces[0, n].astype(jnp.float32) + pieces[1, n].astype(jnp.float32)).astype(jnp.bfloat16)
+
+
+def called(kernel, outs, scratch, args, specs=None, flops=0, limit=16, out_specs=None):
     whole = pl.BlockSpec(memory_space=pltpu.VMEM)
     specs = specs or [whole] * len(args)
     moved = sum(math.prod(a.shape) * a.dtype.itemsize for a in (*args, *outs))
@@ -408,7 +418,7 @@
         kernel,
         out_shape=outs,
         in_specs=[whole if spec is None else spec for spec in specs],
-        out_specs=[whole] * len(outs),
+        out_specs=out_specs or [whole] * len(outs),
         scratch_shapes=scratch,
         compiler_params=pltpu.CompilerParams(vmem_limit_bytes=limit * 2**20),
         cost_estimate=pl.CostEstimate(flops=flops, bytes_accessed=moved, transcendentals=0),
@@ -503,13 +513,13 @@
     latent = latents[0].reshape(frames, rows * cols, chans)
     upstream = cotangent[0].reshape(latent.shape)
     outs = [jax.ShapeDtypeStruct((parts, 2) + latent.shape, bf16)]
-    raw = called(spread_kernel, outs, [], (latent, upstream), limit=58)[0]
+    raw = called(spread_kernel, outs, [pltpu.SemaphoreType.DMA((parts, 2))], (latent, upstream), limit=58, out_specs=[away()])[0]
     raw = lax.all_to_all(raw, "space", 0, 0)
     raw, turned = lax.optimization_barrier((raw, turn(conv_weights)))
 
     a_two, grads, pieces = whole(place, raw, conv_weights, turned, gains, shifts, width, clips, cores)
     pieces = lax.all_to_all(pieces, "core", 0, 0)
-    pieces = jnp.sum(pieces.astype(f32), 0).astype(bf16)
+    pieces = called(pair_kernel, [jax.ShapeDtypeStruct(pieces.shape[1:], bf16)], [], (pieces,))[0]
     pieces = lax.all_to_all(pieces, "pair", 0, 0)
     decoded = decode(place, a_two, conv_weights, latent)
 

time: 107 us -> 105 us (0.981)
  other arithmetic: 1.54 us -> 0 us
    reduce_sum x1 -> x0, other arithmetic: 1.54 us -> none  [per_device(): pieces = jnp.sum(pieces.astype(f32), 0).astype(bf16)]
    pallas_call x5 -> x6, Pallas kernels: 30.5 us -> 30.7 us  [called(): pl.pallas_call(kernel, out_shape=outs, in_specs=[whole if spec is None el...]
where the time goes in v6:
time: 105 us; the launch traced here: 104 us
  Pallas kernels  44 us (42%)
  blocking collectives  31.3 us (30%)
  waiting for transfers between devices  15.7 us (15%)
  starting transfers between devices  9.59 us (9%)
  local copies, waits for them, and re-layouts  3.03 us (3%)
    pallas_call x6, Pallas kernels, called(): pl.pallas_call(kernel, out_shape=outs, in_specs=[whole if spec is None el...  30.7 us
    all_to_all x1, blocking collectives, per_device(): pieces = lax.all_to_all(pieces, 'pair', 0, 0)  26.6 us
    pallas_call x1, Pallas kernels, turn(): pl.pallas_call(turn_kernel, grid=(layers, 9), out_shape=jax.ShapeDtypeStr...  13.3 us
    all_to_all x1, waiting for transfers between devices, per_device(): raw = lax.all_to_all(raw, 'space', 0, 0)  9.53 us
    all_to_all x1, waiting for transfers between devices, per_device(): every = lax.all_to_all(every, 'space', 0, 0)  6.16 us
    all_to_all x1, starting transfers between devices, per_device(): raw = lax.all_to_all(raw, 'space', 0, 0)  6.04 us
    all_to_all x1, blocking collectives, per_device(): pieces = lax.all_to_all(pieces, 'core', 0, 0)  4.71 us
    all_to_all x1, starting transfers between devices, per_device(): every = lax.all_to_all(every, 'space', 0, 0)  3.54 us
  transfers between devices with their start and end apart: 2, of which 2 were waited for; matrix products, arithmetic and copies ran while one was open for 0% of the time, Pallas kernels for 15%

profile of v6, /device:TPU:2, one launch (start us, length us, event | category | flops | bytes accessed | tf_op | source)
XLA Modules:
  0.0 104.3 jit_solution(12406430804724230286)
XLA Ops:
  0.6 2.3 %shard_map.118 = bf16[8,2,8,24,256]{4,3,2,1,0:T(8,128)(2,1)} custom-call(bf16[8,24,256]{2,1,0:T(8,128)(2,1)} %bitcast.5, bf16[8,24,256]{2,1,0:T(8,128)(2,1)} %bitcast.8), custom_call_target="tpu_custom_call" | custom-call | bytes 1769472 | tf_op jit(solution)/shard_map/pallas_call | solution.py:417
  3.0 6.0 %all-to-all-start = ((bf16[8,2,8,24,256]{4,3,2,1,0:T(8,128)(2,1)}), bf16[8,2,8,24,256]{4,3,2,1,0:T(8,128)(2,1)S(1)}, u32[]{:S(2)}, u32[]{:S(2)}) async-start(bf16[8,2,8,24,256]{4,3,2,1,0:T(8,128)(2,1)} %shard_map.118), calls=%async_computation | async-start | bytes 3145728 | tf_op jit(solution)/shard_map/all_to_all | solution.py:517
  9.0 0.0 copy-start.4
  9.0 0.0 copy-start.5
  9.0 13.3 %shard_map.119.turned = bf16[2,6912,256]{2,1,0:T(8,128)(2,1)} custom-call(bf16[2,6912,256]{2,1,0:T(8,128)(2,1)} %weights.5), custom_call_target="tpu_custom_call" | custom-call | bytes 14155776 | tf_op jit(solution)/shard_map/pallas_call | solution.py:482
  22.3 9.5 %all-to-all-done.raw = bf16[8,2,8,24,256]{4,3,2,1,0:T(8,128)(2,1)S(1)} async-done(((bf16[8,2,8,24,256]{4,3,2,1,0:T(8,128)(2,1)}), bf16[8,2,8,24,256]{4,3,2,1,0:T(8,128)(2,1)S(1)}, u32[]{:S(2)}, u32[]{:S(2)}) %all-to-all-start) | async-done | bytes 1572896 | tf_op jit(solution)/shard_map/all_to_all | solution.py:517
  31.9 0.0 copy-done.4
  31.9 0.0 copy-done.5
  31.9 23.5 %shard_map.120 = (bf16[1536,256]{1,0:T(8,128)(2,1)S(1)}, f32[8,24,256]{2,1,0:T(8,128)S(1)}, bf16[2,16,64,256]{3,2,1,0:T(8,128)(2,1)S(1)}) custom-call(s32[1]{0:T(128)} %bitcast.place, bf16[8,2,8,24,256]{4,3,2,1,0:T(8,128)(2,1)S(1)} %all-to-all-done.raw, bf16[2,6912,256]{2,1,0:T(8,128)(2,1)} %weights.5, bf16[2,6912,256]{2,1,0:T(8,128)(2,1)} %shard_map.119.turned, ...), custom_call_target="tpu_custom_call" | custom-call | flops 10871635968 | bytes 17764356 | tf_op jit(solution)/shard_map/pallas_call | solution.py:417
  55.3 0.0 copy-start.3
  55.4 4.7 %all_to_all.20.pieces = bf16[2,16,64,256]{3,2,1,0:T(8,128)(2,1)S(1)} all-to-all(bf16[2,16,64,256]{3,2,1,0:T(8,128)(2,1)S(1)} %get-tuple-element.19), channel_id=1, replica_groups=mesh['pair'=16,'core'=2,'space'=8] {'core'}, dimensions={0} | all-to-all | bytes 2097152 | tf_op jit(solution)/shard_map/all_to_all | solution.py:521
  60.1 0.0 copy-start.1
  60.1 0.0 copy-start.2
  60.1 0.1 shard_map.122
  60.2 26.6 %all_to_all.21.pieces = bf16[16,64,256]{2,1,0:T(8,128)(2,1)S(1)} all-to-all(bf16[16,64,256]{2,1,0:T(8,128)(2,1)S(1)} %shard_map.122), channel_id=1, replica_groups=mesh['pair'=16,'core'=2,'space'=8] {'pair'}, dimensions={0} | all-to-all | bytes 1048576 | tf_op jit(solution)/shard_map/all_to_all | solution.py:523
  86.7 1.0 shard_map.123
  87.7 3.5 %all-to-all-start.3 = ((f32[8,88,256]{2,1,0:T(8,128)}), f32[8,88,256]{2,1,0:T(8,128)S(1)}, u32[]{:S(2)}, u32[]{:S(2)}) async-start(f32[8,88,256]{2,1,0:T(8,128)} %shard_map.123), calls=%async_computation.3 | async-start | bytes 1441792 | tf_op jit(solution)/shard_map/all_to_all | solution.py:527
  91.2 0.0 copy-done.3
  91.3 0.0 copy-start
  91.3 3.0 %copy-done = bf16[2,6912,256]{2,1,0:T(8,128)(2,1)S(1)} copy-done((bf16[2,6912,256]{2,1,0:T(8,128)(2,1)S(1)}, bf16[2,6912,256]{2,1,0:T(8,128)(2,1)}, u32[]{:S(2)}) %copy-start) | copy-done | bytes 7077912
  94.3 2.3 %shard_map.121 = bf16[8,24,256]{2,1,0:T(8,128)(2,1)} custom-call(s32[1]{0:T(128)} %bitcast.place, bf16[1536,256]{1,0:T(8,128)(2,1)S(1)} %get-tuple-element.18.a_two, bf16[2,6912,256]{2,1,0:T(8,128)(2,1)S(1)} %copy-done, bf16[8,24,256]{2,1,0:T(8,128)(2,1)S(1)} %bitcast.6), custom_call_target="tpu_custom_call" | custom-call | flops 905969664 | bytes 8060932 | tf_op jit(solution)/shard_map/pallas_call | solution.py:417
  96.6 6.2 %all-to-all-done.3.every = f32[8,88,256]{2,1,0:T(8,128)S(1)} async-done(((f32[8,88,256]{2,1,0:T(8,128)}), f32[8,88,256]{2,1,0:T(8,128)S(1)}, u32[]{:S(2)}, u32[]{:S(2)}) %all-to-all-start.3) | async-done | bytes 720928 | tf_op jit(solution)/shard_map/all_to_all | solution.py:527
  102.7 0.0 copy-done.1
  102.7 0.0 copy-done.2
  102.7 1.5 %shard_map.124 = (f32[2,216,256]{2,1,0:T(8,128)}, f32[2,216,256]{2,1,0:T(8,128)}, f32[2,216,256]{2,1,0:T(8,128)}, f32[4,256]{1,0:T(4,128)}, bf16[8,24,256]{2,1,0:T(8,128)(2,1)}) custom-call(f32[8,88,256]{2,1,0:T(8,128)S(1)} %all-to-all-done.3.every, f32[2,216,256]{2,1,0:T(8,128)S(1)} %copy-done.1, f32[2,216,256]{2,1,0:T(8,128)S(1)} %copy-done.2), custom_call_target="tpu_custom_call" | custom-call | bytes 3035136 | tf_op jit(solution)/shard_map/pallas_call | solution.py:417
Async XLA Ops:
  3.0 28.9 %all-to-all-start = ((bf16[8,2,8,24,256]{4,3,2,1,0:T(8,128)(2,1)}), bf16[8,2,8,24,256]{4,3,2,1,0:T(8,128)(2,1)S(1)}, u32[]{:S(2)}, u32[]{:S(2)}) async-start(bf16[8,2,8,24,256]{4,3,2,1,0:T(8,128)(2,1)} %shard_map.118), calls=%async_computation | async-start | bytes 3145728 | tf_op jit(solution)/shard_map/all_to_all | solution.py:517
  9.0 22.9 %copy-start.4 = (f32[2,256]{1,0:T(2,128)S(1)}, f32[2,256]{1,0:T(2,128)}, u32[]{:S(2)}) copy-start(f32[2,256]{1,0:T(2,128)} %gains.1) | copy-start | bytes 6148
  9.0 22.9 %copy-start.5 = (f32[2,256]{1,0:T(2,128)S(1)}, f32[2,256]{1,0:T(2,128)}, u32[]{:S(2)}) copy-start(f32[2,256]{1,0:T(2,128)} %shifts.1) | copy-start | bytes 6148
  55.3 35.9 %copy-start.3 = (bf16[1,8,3,8,256]{4,3,2,1,0:T(8,128)(2,1)S(1)}, bf16[1,8,3,8,256]{4,3,2,1,0:T(8,128)(2,1)}, u32[]{:S(2)}) copy-start(bf16[1,8,3,8,256]{4,3,2,1,0:T(8,128)(2,1)} %param.7) | copy-start | bytes 294916
  60.1 42.7 %copy-start.1 = (f32[2,216,256]{2,1,0:T(8,128)S(1)}, f32[2,216,256]{2,1,0:T(8,128)}, u32[]{:S(2)}) copy-start(f32[2,216,256]{2,1,0:T(8,128)} %moment.1) | copy-start | bytes 1327108
  60.1 42.7 %copy-start.2 = (f32[2,216,256]{2,1,0:T(8,128)S(1)}, f32[2,216,256]{2,1,0:T(8,128)}, u32[]{:S(2)}) copy-start(f32[2,216,256]{2,1,0:T(8,128)} %second.1) | copy-start | bytes 1327108
  87.7 15.0 %all-to-all-start.3 = ((f32[8,88,256]{2,1,0:T(8,128)}), f32[8,88,256]{2,1,0:T(8,128)S(1)}, u32[]{:S(2)}, u32[]{:S(2)}) async-start(f32[8,88,256]{2,1,0:T(8,128)} %shard_map.123), calls=%async_computation.3 | async-start | bytes 1441792 | tf_op jit(solution)/shard_map/all_to_all | solution.py:527
  91.3 3.0 %copy-start = (bf16[2,6912,256]{2,1,0:T(8,128)(2,1)S(1)}, bf16[2,6912,256]{2,1,0:T(8,128)(2,1)}, u32[]{:S(2)}) copy-start(bf16[2,6912,256]{2,1,0:T(8,128)(2,1)} %weights.5) | copy-start | bytes 21233668

commit v7 on v6

--- a/solution.py
+++ b/solution.py
@@ -275,7 +275,8 @@
 
     @pl.when(me == 0)
     def _():
-        d_act[...] = d_act[...] + (term(0, 1) + (term(0, 0) + term(1, 0)))
+        pair = jnp.dot(nine[0 : 2 * size, :], weight[0:depth, :], preferred_element_type=jnp.float32)
+        d_act[...] = d_act[...] + (term(0, 1) + (pair[:size] + pair[size:]))
 
     count = size * (chans // GROUPS)
     value = load_frame(raw_lat, me)
@@ -513,7 +514,7 @@
     latent = latents[0].reshape(frames, rows * cols, chans)
     upstream = cotangent[0].reshape(latent.shape)
     outs = [jax.ShapeDtypeStruct((parts, 2) + latent.shape, bf16)]
-    raw = called(spread_kernel, outs, [pltpu.SemaphoreType.DMA((parts, 2))], (latent, upstream), limit=58, out_specs=[away()])[0]
+    raw = called(spread_kernel, outs, [pltpu.SemaphoreType.DMA((parts, 2))], (latent, upstream), [away(), away()], limit=58, out_specs=[away()])[0]
     raw = lax.all_to_all(raw, "space", 0, 0)
     raw, turned = lax.optimization_barrier((raw, turn(conv_weights)))
 

time: 105 us -> 152 us (1.45)
  Pallas kernels: 44 us -> 90.5 us
    pallas_call x6, Pallas kernels: 30.7 us -> 77.2 us  [called(): pl.pallas_call(kernel, out_shape=outs, in_specs=[whole if spec is None el...]
  transfers between devices with their start and end apart: 2 -> 2, of which waited for: 2 -> 2; matrix products, arithmetic and copies ran while one was open for 0% -> 0% of each run, Pallas kernels for 15% -> 10%
where the time goes in v7:
time: 152 us; the launch traced here: 151 us
  Pallas kernels  90.5 us (60%)
  blocking collectives  31.3 us (21%)
  waiting for transfers between devices  15.7 us (10%)
  starting transfers between devices  9.59 us (6%)
  local copies, waits for them, and re-layouts  3.03 us (2%)
    pallas_call x6, Pallas kernels, called(): pl.pallas_call(kernel, out_shape=outs, in_specs=[whole if spec is None el...  77.2 us
    all_to_all x1, blocking collectives, per_device(): pieces = lax.all_to_all(pieces, 'pair', 0, 0)  26.6 us
    pallas_call x1, Pallas kernels, turn(): pl.pallas_call(turn_kernel, grid=(layers, 9), out_shape=jax.ShapeDtypeStr...  13.3 us
    all_to_all x1, waiting for transfers between devices, per_device(): raw = lax.all_to_all(raw, 'space', 0, 0)  9.53 us
    all_to_all x1, waiting for transfers between devices, per_device(): every = lax.all_to_all(every, 'space', 0, 0)  6.16 us
    all_to_all x1, starting transfers between devices, per_device(): raw = lax.all_to_all(raw, 'space', 0, 0)  6.04 us
    all_to_all x1, blocking collectives, per_device(): pieces = lax.all_to_all(pieces, 'core', 0, 0)  4.71 us
    all_to_all x1, starting transfers between devices, per_device(): every = lax.all_to_all(every, 'space', 0, 0)  3.54 us
  transfers between devices with their start and end apart: 2, of which 2 were waited for; matrix products, arithmetic and copies ran while one was open for 0% of the time, Pallas kernels for 10%

profile of v7, /device:TPU:2, one launch (start us, length us, event | category | flops | bytes accessed | tf_op | source)
XLA Modules:
  0.0 150.8 jit_solution(2892126053097611299)
XLA Ops:
  0.6 48.9 %shard_map.118 = bf16[8,2,8,24,256]{4,3,2,1,0:T(8,128)(2,1)} custom-call(bf16[8,24,256]{2,1,0:T(8,128)(2,1)} %bitcast.5, bf16[8,24,256]{2,1,0:T(8,128)(2,1)} %bitcast.8), custom_call_target="tpu_custom_call" | custom-call | bytes 1769472 | tf_op jit(solution)/shard_map/pallas_call | solution.py:418
  49.5 6.0 %all-to-all-start = ((bf16[8,2,8,24,256]{4,3,2,1,0:T(8,128)(2,1)}), bf16[8,2,8,24,256]{4,3,2,1,0:T(8,128)(2,1)S(1)}, u32[]{:S(2)}, u32[]{:S(2)}) async-start(bf16[8,2,8,24,256]{4,3,2,1,0:T(8,128)(2,1)} %shard_map.118), calls=%async_computation | async-start | bytes 3145728 | tf_op jit(solution)/shard_map/all_to_all | solution.py:518
  55.6 0.0 copy-start.4
  55.6 0.0 copy-start.5
  55.6 13.3 %shard_map.119.turned = bf16[2,6912,256]{2,1,0:T(8,128)(2,1)} custom-call(bf16[2,6912,256]{2,1,0:T(8,128)(2,1)} %weights.5), custom_call_target="tpu_custom_call" | custom-call | bytes 14155776 | tf_op jit(solution)/shard_map/pallas_call | solution.py:483
  68.9 9.5 %all-to-all-done.raw = bf16[8,2,8,24,256]{4,3,2,1,0:T(8,128)(2,1)S(1)} async-done(((bf16[8,2,8,24,256]{4,3,2,1,0:T(8,128)(2,1)}), bf16[8,2,8,24,256]{4,3,2,1,0:T(8,128)(2,1)S(1)}, u32[]{:S(2)}, u32[]{:S(2)}) %all-to-all-start) | async-done | bytes 1572896 | tf_op jit(solution)/shard_map/all_to_all | solution.py:518
  78.4 0.0 copy-done.4
  78.4 0.0 copy-done.5
  78.4 23.4 %shard_map.120 = (bf16[1536,256]{1,0:T(8,128)(2,1)S(1)}, f32[8,24,256]{2,1,0:T(8,128)S(1)}, bf16[2,16,64,256]{3,2,1,0:T(8,128)(2,1)S(1)}) custom-call(s32[1]{0:T(128)} %bitcast.place, bf16[8,2,8,24,256]{4,3,2,1,0:T(8,128)(2,1)S(1)} %all-to-all-done.raw, bf16[2,6912,256]{2,1,0:T(8,128)(2,1)} %weights.5, bf16[2,6912,256]{2,1,0:T(8,128)(2,1)} %shard_map.119.turned, ...), custom_call_target="tpu_custom_call" | custom-call | flops 10871635968 | bytes 17764356 | tf_op jit(solution)/shard_map/pallas_call | solution.py:418
  101.9 0.0 copy-start.3
  101.9 4.7 %all_to_all.20.pieces = bf16[2,16,64,256]{3,2,1,0:T(8,128)(2,1)S(1)} all-to-all(bf16[2,16,64,256]{3,2,1,0:T(8,128)(2,1)S(1)} %get-tuple-element.19), channel_id=1, replica_groups=mesh['pair'=16,'core'=2,'space'=8] {'core'}, dimensions={0} | all-to-all | bytes 2097152 | tf_op jit(solution)/shard_map/all_to_all | solution.py:522
  106.6 0.0 copy-start.1
  106.6 0.0 copy-start.2
  106.6 0.1 shard_map.122
  106.7 26.6 %all_to_all.21.pieces = bf16[16,64,256]{2,1,0:T(8,128)(2,1)S(1)} all-to-all(bf16[16,64,256]{2,1,0:T(8,128)(2,1)S(1)} %shard_map.122), channel_id=1, replica_groups=mesh['pair'=16,'core'=2,'space'=8] {'pair'}, dimensions={0} | all-to-all | bytes 1048576 | tf_op jit(solution)/shard_map/all_to_all | solution.py:524
  133.3 1.0 shard_map.123
  134.2 3.5 %all-to-all-start.3 = ((f32[8,88,256]{2,1,0:T(8,128)}), f32[8,88,256]{2,1,0:T(8,128)S(1)}, u32[]{:S(2)}, u32[]{:S(2)}) async-start(f32[8,88,256]{2,1,0:T(8,128)} %shard_map.123), calls=%async_computation.3 | async-start | bytes 1441792 | tf_op jit(solution)/shard_map/all_to_all | solution.py:528
  137.8 0.0 copy-done.3
  137.8 0.0 copy-start
  137.8 3.0 %copy-done = bf16[2,6912,256]{2,1,0:T(8,128)(2,1)S(1)} copy-done((bf16[2,6912,256]{2,1,0:T(8,128)(2,1)S(1)}, bf16[2,6912,256]{2,1,0:T(8,128)(2,1)}, u32[]{:S(2)}) %copy-start) | copy-done | bytes 7077912
  140.8 2.3 %shard_map.121 = bf16[8,24,256]{2,1,0:T(8,128)(2,1)} custom-call(s32[1]{0:T(128)} %bitcast.place, bf16[1536,256]{1,0:T(8,128)(2,1)S(1)} %get-tuple-element.18.a_two, bf16[2,6912,256]{2,1,0:T(8,128)(2,1)S(1)} %copy-done, bf16[8,24,256]{2,1,0:T(8,128)(2,1)S(1)} %bitcast.6), custom_call_target="tpu_custom_call" | custom-call | flops 905969664 | bytes 8060932 | tf_op jit(solution)/shard_map/pallas_call | solution.py:418
  143.1 6.2 %all-to-all-done.3.every = f32[8,88,256]{2,1,0:T(8,128)S(1)} async-done(((f32[8,88,256]{2,1,0:T(8,128)}), f32[8,88,256]{2,1,0:T(8,128)S(1)}, u32[]{:S(2)}, u32[]{:S(2)}) %all-to-all-start.3) | async-done | bytes 720928 | tf_op jit(solution)/shard_map/all_to_all | solution.py:528
  149.3 0.0 copy-done.1
  149.3 0.0 copy-done.2
  149.3 1.5 %shard_map.124 = (f32[2,216,256]{2,1,0:T(8,128)}, f32[2,216,256]{2,1,0:T(8,128)}, f32[2,216,256]{2,1,0:T(8,128)}, f32[4,256]{1,0:T(4,128)}, bf16[8,24,256]{2,1,0:T(8,128)(2,1)}) custom-call(f32[8,88,256]{2,1,0:T(8,128)S(1)} %all-to-all-done.3.every, f32[2,216,256]{2,1,0:T(8,128)S(1)} %copy-done.1, f32[2,216,256]{2,1,0:T(8,128)S(1)} %copy-done.2), custom_call_target="tpu_custom_call" | custom-call | bytes 3035136 | tf_op jit(solution)/shard_map/pallas_call | solution.py:418
Async XLA Ops:
  49.5 28.9 %all-to-all-start = ((bf16[8,2,8,24,256]{4,3,2,1,0:T(8,128)(2,1)}), bf16[8,2,8,24,256]{4,3,2,1,0:T(8,128)(2,1)S(1)}, u32[]{:S(2)}, u32[]{:S(2)}) async-start(bf16[8,2,8,24,256]{4,3,2,1,0:T(8,128)(2,1)} %shard_map.118), calls=%async_computation | async-start | bytes 3145728 | tf_op jit(solution)/shard_map/all_to_all | solution.py:518
  55.6 22.9 %copy-start.4 = (f32[2,256]{1,0:T(2,128)S(1)}, f32[2,256]{1,0:T(2,128)}, u32[]{:S(2)}) copy-start(f32[2,256]{1,0:T(2,128)} %gains.1) | copy-start | bytes 6148
  55.6 22.9 %copy-start.5 = (f32[2,256]{1,0:T(2,128)S(1)}, f32[2,256]{1,0:T(2,128)}, u32[]{:S(2)}) copy-start(f32[2,256]{1,0:T(2,128)} %shifts.1) | copy-start | bytes 6148
  101.9 35.9 %copy-start.3 = (bf16[1,8,3,8,256]{4,3,2,1,0:T(8,128)(2,1)S(1)}, bf16[1,8,3,8,256]{4,3,2,1,0:T(8,128)(2,1)}, u32[]{:S(2)}) copy-start(bf16[1,8,3,8,256]{4,3,2,1,0:T(8,128)(2,1)} %param.7) | copy-start | bytes 294916
  106.6 42.7 %copy-start.1 = (f32[2,216,256]{2,1,0:T(8,128)S(1)}, f32[2,216,256]{2,1,0:T(8,128)}, u32[]{:S(2)}) copy-start(f32[2,216,256]{2,1,0:T(8,128)} %moment.1) | copy-start | bytes 1327108
  106.6 42.7 %copy-start.2 = (f32[2,216,256]{2,1,0:T(8,128)S(1)}, f32[2,216,256]{2,1,0:T(8,128)}, u32[]{:S(2)}) copy-start(f32[2,216,256]{2,1,0:T(8,128)} %second.1) | copy-start | bytes 1327108
  134.2 15.0 %all-to-all-start.3 = ((f32[8,88,256]{2,1,0:T(8,128)}), f32[8,88,256]{2,1,0:T(8,128)S(1)}, u32[]{:S(2)}, u32[]{:S(2)}) async-start(f32[8,88,256]{2,1,0:T(8,128)} %shard_map.123), calls=%async_computation.3 | async-start | bytes 1441792 | tf_op jit(solution)/shard_map/all_to_all | solution.py:528
  137.8 3.0 %copy-start = (bf16[2,6912,256]{2,1,0:T(8,128)(2,1)S(1)}, bf16[2,6912,256]{2,1,0:T(8,128)(2,1)}, u32[]{:S(2)}) copy-start(bf16[2,6912,256]{2,1,0:T(8,128)(2,1)} %weights.5) | copy-start | bytes 21233668
